TPU v7x, 256 devices: a whole 4x4x8 slice. The times are simulated.
256 devices in a mesh: gx: 8 (over z), gy: 8 (over x, core), gz: 4 (over y).
Axes of the slice: x: 4, y: 4, z: 8, core: 2. Of those that a mesh axis runs over, the one named last changes fastest.
Arguments:
- conserved: float32 [5, 256, 64, 512], P(None, 'gx', 'gy', 'gz'), may hold values from -0.6 to 11, as said below
- gamma_field: float32 [256, 64, 512], P('gx', 'gy', 'gz'), may hold values from 1.2 to 1.67
- species: int32 [256, 64, 512], P('gx', 'gy', 'gz'), may hold values from 0 to 3
- lut_color: float32 [4, 3, 256], replicated, may hold values from 0 to 1
- lut_extinction: float32 [4, 256], replicated, may hold values from 0.0005 to 0.01
Outputs:
- new_state: float32 [5, 256, 64, 512], P(None, 'gx', 'gy', 'gz')
- image_rgba: float32 [4, 1024, 1920], P(None, ('gx', 'gy', 'gz'))
Inputs may be any that keep to these rules, and one draw needn't show every extreme that they name: `conserved`: component 0 (density) lies in [0.5, 2]; each velocity component, momentum over density, lies in [-0.3, 0.3]; the pressure computed with gamma_field lies in [0.5, 2].
All inputs are finite; a program needn't handle non-finite values.
Results may differ from a plain program's by a relative error of at most 0.0003.
Values sent between devices are 32-bit elements; how exact they have to be, the bound alone decides.
No kernel may reach another device: no remote copies, remote signals or barrier semaphores. Data moves between devices by JAX's collectives and lax.ppermute only.
A program may use at most 64 MiB of HBM per device.

v0:
```python
import jax
import jax.numpy as jnp
from jax import lax
from jax.sharding import PartitionSpec as P

SW = 1920
ZOOM = 4


dissipation = 3.0
courant = 0.11
density_low = 0.6
density_high = 1.6


def swapped(x, axis, stride):
    return lax.ppermute(x, axis, [(i, i ^ 1 << stride) for i in range(lax.axis_size(axis))])


def with_halo(x, sides, width):
    for axis, dim in sides:
        size, length = (lax.axis_size(axis), x.shape[dim])
        up = [(i, (i + 1) % size) for i in range(size)]
        down = [(j, i) for i, j in up]
        last = lax.slice_in_dim(x, length - width, length, axis=dim)
        first = lax.slice_in_dim(x, 0, width, axis=dim)
        before = lax.ppermute(last, axis, up)
        after = lax.ppermute(first, axis, down)
        x = jnp.concatenate([before, x, after], axis=dim)
    return x


def from_behind(value, axis, steps):
    count = lax.axis_size(axis)
    first, last = (max(0, -steps), min(count, count - steps))
    return lax.ppermute(value, axis, [(source, source + steps) for source in range(first, last)])


def divergence(padded, gamma_pad):
    inverse = 1.0 / padded[0]
    momenta = padded[1:4]
    energy = padded[4]
    kinetic = (
        0.5
        * (momenta[0] * momenta[0] + momenta[1] * momenta[1] + momenta[2] * momenta[2])
        * inverse
    )
    pressure = (gamma_pad - 1.0) * (energy - kinetic)
    summed = None
    for direction in range(3):
        velocity = momenta[direction] * inverse
        pieces_list = [momenta[direction]]
        for member in range(3):
            component = momenta[member] * velocity
            if member == direction:
                component = component + pressure
            pieces_list.append(component)
        pieces_list.append((energy + pressure) * velocity)
        fluxes = jnp.stack(pieces_list)
        axis_now = direction + 1
        length = padded.shape[axis_now]
        lower_cells = lax.slice_in_dim(padded, 0, length - 1, axis=axis_now)
        upper_cells = lax.slice_in_dim(padded, 1, length, axis=axis_now)
        face_flux = 0.5 * (
            lax.slice_in_dim(fluxes, 0, length - 1, axis=axis_now)
            + lax.slice_in_dim(fluxes, 1, length, axis=axis_now)
        ) - 0.5 * dissipation * (upper_cells - lower_cells)
        change = lax.slice_in_dim(face_flux, 1, length - 1, axis=axis_now) - lax.slice_in_dim(
            face_flux, 0, length - 2, axis=axis_now
        )
        for other_axis in range(1, 4):
            if other_axis != axis_now:
                change = lax.slice_in_dim(change, 1, change.shape[other_axis] - 1, axis=other_axis)
        summed = change if summed is None else summed + change
    return summed


def classify(density, species, lut_table):
    class_count = lut_table.shape[0]
    knots_count = lut_table.shape[2]
    table_rows = lut_table.reshape(class_count * 4, knots_count)
    table_pos = (density - density_low) * ((knots_count - 1) / (density_high - density_low))
    flat_pos = table_pos.reshape(-1)
    knot_values = jnp.arange(knots_count).astype(jnp.float32)
    hat_weights = jnp.maximum(0.0, 1.0 - jnp.abs(knot_values[:, None] - flat_pos[None, :]))
    every_class = jnp.dot(
        table_rows, hat_weights, precision=lax.Precision.HIGHEST, preferred_element_type=jnp.float32
    )
    every_class = every_class.reshape(class_count, 4, flat_pos.shape[0])
    selector = (jnp.arange(class_count)[:, None] == species.reshape(-1)[None, :]).astype(
        jnp.float32
    )
    chosen = jnp.sum(every_class * selector[:, None, :], axis=0)
    return chosen.reshape((4,) + density.shape)


def brick_planes(density, species, lut_table):
    block_rows = 8
    extent_x, extent_y, depth_cells = density.shape
    block_count = extent_x // block_rows
    lower_tri = (jnp.arange(depth_cells)[:, None] < jnp.arange(depth_cells)[None, :]).astype(
        jnp.float32
    )

    def one_block(pair_args):
        block_density, block_species = pair_args
        properties = classify(block_density, block_species, lut_table)
        extinction = properties[3]
        before = jnp.einsum("xyz,zw->xyw", extinction, lower_tri, precision=lax.Precision.HIGHEST)
        transmit = jnp.exp(-before)
        opacity = 1.0 - jnp.exp(-extinction)
        emitted = jnp.sum(properties[:3] * (opacity * transmit)[None], axis=-1)
        through = jnp.exp(-(before[..., -1] + extinction[..., -1]))
        return jnp.concatenate([emitted, through[None]], axis=0)

    blocks = lax.map(
        one_block,
        (
            density.reshape(block_count, block_rows, extent_y, depth_cells),
            species.reshape(block_count, block_rows, extent_y, depth_cells),
        ),
    )
    return blocks.transpose(1, 0, 2, 3).reshape(4, extent_x, extent_y)


def composite_over(front_planes, back_planes):
    return jnp.concatenate(
        [front_planes[:3] + front_planes[3:] * back_planes[:3], front_planes[3:] * back_planes[3:]],
        axis=0,
    )


def spread_rows(grouped):
    return lax.all_to_all(grouped, "gy", split_axis=1, concat_axis=4, tiled=True)


def composite(grouped):
    position = lax.axis_index("gz")
    for level_bit in range(lax.axis_size("gz").bit_length() - 1):
        extent = grouped.shape
        paired = grouped.reshape(extent[0], extent[1], extent[2] // 2, 2, extent[3], extent[4])
        my_bit = position // (1 << level_bit) % 2
        kept_half = lax.dynamic_index_in_dim(paired, my_bit, 3, keepdims=False)
        given_half = lax.dynamic_index_in_dim(paired, 1 - my_bit, 3, keepdims=False)
        received = swapped(given_half, "gz", level_bit)
        grouped = jnp.where(
            my_bit == 0, composite_over(kept_half, received), composite_over(received, kept_half)
        )
    return grouped


def warp(planes, screen_width):
    source_rows = planes.shape[1] - 1
    out_rows = jnp.arange(ZOOM * source_rows).astype(jnp.float32) / ZOOM
    vertical = jnp.maximum(
        0.0,
        1.0 - jnp.abs(out_rows[:, None] - jnp.arange(source_rows + 1).astype(jnp.float32)[None, :]),
    )
    columns = planes.shape[2]
    column_pos = jnp.arange(screen_width).astype(jnp.float32) * (columns / screen_width)
    horizontal = jnp.maximum(
        0.0, 1.0 - jnp.abs(jnp.arange(columns).astype(jnp.float32)[:, None] - column_pos[None, :])
    )
    stretched = jnp.einsum("ri,civ->crv", vertical, planes, precision=lax.Precision.HIGHEST)
    return jnp.einsum("crv,vs->crs", stretched, horizontal, precision=lax.Precision.HIGHEST)


def local(conserved, gamma_field, species, lut_color, lut_extinction):
    lut_table = jnp.concatenate([lut_color, lut_extinction[:, None, :]], axis=1)
    joined = jnp.concatenate([conserved, gamma_field[None]], axis=0)
    padded = with_halo(joined, (("gx", 1), ("gy", 2), ("gz", 3)), 1)
    halfway = conserved - courant * divergence(padded[:5], padded[5])
    halfway_pad = with_halo(halfway, (("gx", 1), ("gy", 2), ("gz", 3)), 1)
    new_state = 0.5 * (conserved + halfway - courant * divergence(halfway_pad, padded[5]))
    planes = brick_planes(new_state[0], species, lut_table)
    across_y = lax.axis_size("gy")
    across_z = lax.axis_size("gz")
    per_device = planes.shape[1] // (across_y * across_z)
    grouped = planes.reshape(4, across_y, across_z, per_device, planes.shape[2])
    merged = spread_rows(composite(grouped))
    row_planes = merged.reshape(4, per_device, merged.shape[4])
    visible = jnp.concatenate([row_planes[:3], 1.0 - row_planes[3:]], axis=0)
    next_rows = from_behind(visible, ("gx", "gy", "gz"), -1)
    stacked = jnp.concatenate([visible, next_rows], axis=1)
    return (new_state, warp(stacked, SW))


def solution(mesh):
    return jax.shard_map(
        local,
        mesh=mesh,
        in_specs=(P(None, "gx", "gy", "gz"), P("gx", "gy", "gz"), P("gx", "gy", "gz"), P(), P()),
        out_specs=(P(None, "gx", "gy", "gz"), P(None, ("gx", "gy", "gz"), None)),
        check_vma=False,
    )
```

profile of v0, /device:TPU:127, one launch (start us, length us, event | category | flops | bytes accessed | tf_op | source)
XLA Modules:
  0.0 132.9 jit_solution(2379489386986604909)
XLA Ops:
  2.8 2.9 %collective-permute-start = (f32[6,1,8,128]{3,1,2,0:T(1,128)S(1)}, f32[6,1,8,128]{3,1,2,0:T(1,128)S(1)}, u32[]{:S(2)}, u32[]{:S(2)}) collective-permute-start(f32[6,1,8,128]{3,1,2,0:T(1,128)S(1)} %get-tuple-element.165), channel_id=1, source_target_pairs={{0,32},{32,64},{64,96},{96,128},{128,160},{160,192},{192,224},{224... | collective-permute-start | bytes 73736 | tf_op jit(solution)/shard_map/ppermute | solution.py:27
  6.7 2.9 %collective-permute-done.1 = f32[6,1,8,128]{3,1,2,0:T(1,128)S(1)} collective-permute-done((f32[6,1,8,128]{3,1,2,0:T(1,128)S(1)}, f32[6,1,8,128]{3,1,2,0:T(1,128)S(1)}, u32[]{:S(2)}, u32[]{:S(2)}) %collective-permute-start.1) | collective-permute-done | bytes 24608 | tf_op jit(solution)/shard_map/ppermute | solution.py:28
  9.7 2.2 %collective-permute-start.2 = (f32[6,34,1,128]{3,1,2,0:T(8,128)S(1)}, f32[6,34,1,128]{3,1,2,0:T(8,128)S(1)}, u32[]{:S(2)}, u32[]{:S(2)}) collective-permute-start(f32[6,34,1,128]{3,1,2,0:T(8,128)S(1)} %get-tuple-element.163), channel_id=1, source_target_pairs={{0,4},{4,8},{8,12},{12,16},{16,20},{20,24},{24,28},{28,0},{1,5},{5... | collective-permute-start | bytes 313352 | tf_op jit(solution)/shard_map/ppermute | solution.py:27
  13.7 3.6 %collective-permute-done.3 = f32[6,34,1,128]{3,1,2,0:T(8,128)S(1)} collective-permute-done((f32[6,34,1,128]{3,1,2,0:T(8,128)S(1)}, f32[6,34,1,128]{3,1,2,0:T(8,128)S(1)}, u32[]{:S(2)}, u32[]{:S(2)}) %collective-permute-start.3) | collective-permute-done | bytes 104480 | tf_op jit(solution)/shard_map/ppermute | solution.py:28
  25.6 2.9 %pad_maximum_fusion = f32[6,34,10,130]{3,1,2,0:T(8,128)S(1)} fusion(f32[6,34,10,1]{3,1,2,0:T(8,128)} %copy.23, f32[6,34,1,128]{3,1,2,0:T(8,128)S(1)} %collective-permute-done.3, f32[6,1,8,128]{3,1,2,0:T(1,128)S(1)} %collective-permute-done.1, f32[1,32,8,128]{3,1,2,0:T(8,128)S(1)} %bitcast.98, f32[5,32,8,128]{3,1,2,0:T(8,128)S(1)} %copy.27, ...), kind=kLoop, calls=%fused_computation.35 | loop fusion | flops 1856400 | bytes 2121600 | tf_op jit(solution)/shard_map/concatenate | solution.py:29
  32.5 2.8 %fusion.30 = f32[5,34,10,129]{3,1,2,0:T(8,128)S(1)} fusion(f32[6,34,10,1]{3,1,2,0:T(8,128)S(1)} %copy-done, f32[6,34,1,128]{3,1,2,0:T(8,128)S(1)} %collective-permute-done.3, f32[6,34,1,128]{3,1,2,0:T(8,128)S(1)} %collective-permute-done.2, f32[6,1,8,128]{3,1,2,0:T(1,128)S(1)} %collective-permute-done.1, f32[6,1,8,128]{3,1,2,0:T(1,128)S(1)} %collective-permute-done, ...), kind=kLoop, calls=%fused_computation.47 | loop fusion | flops 3728100 | bytes 3692400 | tf_op jit(solution)/shard_map/sub | solution.py:64
  41.7 2.5 %collective-permute-start.8 = (f32[5,34,1,128]{3,1,2,0:T(8,128)S(1)}, f32[5,34,1,128]{3,1,2,0:T(8,128)S(1)}, u32[]{:S(2)}, u32[]{:S(2)}) collective-permute-start(f32[5,34,1,128]{3,1,2,0:T(8,128)S(1)} %get-tuple-element.167), channel_id=1, source_target_pairs={{0,4},{4,8},{8,12},{12,16},{16,20},{20,24},{24,28},{28,0},{1,5},{5... | collective-permute-start | bytes 261128 | tf_op jit(solution)/shard_map/ppermute | solution.py:27
  45.9 3.6 %collective-permute-done.9 = f32[5,34,1,128]{3,1,2,0:T(8,128)S(1)} collective-permute-done((f32[5,34,1,128]{3,1,2,0:T(8,128)S(1)}, f32[5,34,1,128]{3,1,2,0:T(8,128)S(1)}, u32[]{:S(2)}, u32[]{:S(2)}) %collective-permute-start.9) | collective-permute-done | bytes 87072 | tf_op jit(solution)/shard_map/ppermute | solution.py:28
  54.1 2.5 %copy.29 = f32[5,34,10,1]{1,2,3,0:T(8,128)} copy(f32[5,34,10,1]{3,1,2,0:T(8,128)} %get-tuple-element.162) | data formatting | bytes 13600 | tf_op jit(solution)/shard_map/slice | solution.py:26
  58.7 2.2 %collective-permute-done.11 = f32[5,34,10,1]{1,2,3,0:T(8,128)} collective-permute-done((f32[5,34,10,1]{1,2,3,0:T(8,128)}, f32[5,34,10,1]{1,2,3,0:T(8,128)}, u32[]{:S(2)}, u32[]{:S(2)}) %collective-permute-start.11) | collective-permute-done | bytes 6832 | tf_op jit(solution)/shard_map/ppermute | solution.py:28
  60.9 2.2 %copy.31 = f32[5,34,10,1]{3,1,2,0:T(8,128)} copy(f32[5,34,10,1]{1,2,3,0:T(8,128)} %collective-permute-done.11) | data formatting | bytes 13600 | tf_op jit(solution)/shard_map/ppermute | solution.py:28
  63.1 2.6 %pad_maximum_fusion.13 = f32[5,34,10,130]{3,1,2,0:T(8,128)S(1)} fusion(f32[5,34,10,1]{3,1,2,0:T(8,128)} %copy.31, f32[5,34,1,128]{3,1,2,0:T(8,128)S(1)} %collective-permute-done.9, f32[5,1,8,128]{3,1,2,0:T(1,128)S(1)} %collective-permute-done.7, f32[5,32,8,128]{3,1,2,0:T(8,128)S(1)} %fusion.49, f32[5,1,8,128]{3,1,2,0:T(1,128)S(1)} %collective-permute-done.6, ...), kind=kLoop, calls=%fused_computation.66 | loop fusion | flops 1326000 | bytes 1768000 | tf_op jit(solution)/shard_map/concatenate | solution.py:29
  69.7 2.4 %fusion.24 = f32[5,34,10,129]{3,1,2,0:T(8,128)S(1)} fusion(f32[5,34,10,130]{3,1,2,0:T(8,128)S(1)} %get-tuple-element.131, f32[5,34,10,1]{3,1,2,0:T(8,128)S(1)} %copy-done.3, f32[5,34,1,128]{3,1,2,0:T(8,128)S(1)} %collective-permute-done.9, f32[5,1,8,128]{3,1,2,0:T(1,128)S(1)} %collective-permute-done.7, f32[5,32,8,128]{3,1,2,0:T(8,128)S(1)} %fusion.49, ...), kind=kLoop, calls=%fused_computation.38 | loop fusion | flops 3289500 | bytes 3515600 | tf_op jit(solution)/shard_map/sub | solution.py:64
  74.3 28.8 %while.14 = (s32[]{:T(128)}, f32[4,4,8,8]{3,2,0,1:T(8,128)S(1)}, f32[4,8,8,128]{3,1,0,2:T(8,128)S(1)}, f32[4,4,256]{2,1,0:T(4,128)}, s32[4,8,8,128]{3,2,1,0:T(8,128)}, /*index=5*/f32[16,256]{1,0:T(8,128)S(1)}, s32[]{:T(128)}) while((s32[]{:T(128)}, f32[4,4,8,8]{3,2,0,1:T(8,128)S(1)}, f32[4,8,8,128]{3,1,0,2:T(8,128)S(1)}, ...), condition=%wide.wide.region_3.4_spmd.clone, body=%wide.wide.region_0.3_spmd.clone.sunk | while | flops 424051136 | bytes 3296857 | solution.py:116
  74.3 5.5 %convolution_bitcast_fusion.4 = f32[16,8192]{1,0:T(8,128)S(1)} fusion(f32[16,256]{1,0:T(8,128)S(1)} %get-tuple-element.260, f32[8192]{0:T(1024)S(1)} %fusion.111, f32[256]{0:T(256)S(1)} %iota_convert_fusion.5), kind=kOutput, calls=%fused_computation.1.clone.clone.1 | convolution fusion | flops 411041792 | bytes 574464 | tf_op jit(solution)/shard_map/while/body/eval_jaxpr/dot_general | solution.py:86
  81.6 5.5 %convolution_bitcast_fusion.4 = f32[16,8192]{1,0:T(8,128)S(1)} fusion(f32[16,256]{1,0:T(8,128)S(1)} %get-tuple-element.260, f32[8192]{0:T(1024)S(1)} %fusion.111, f32[256]{0:T(256)S(1)} %iota_convert_fusion.5), kind=kOutput, calls=%fused_computation.1.clone.clone.1 | convolution fusion | flops 411041792 | bytes 574464 | tf_op jit(solution)/shard_map/while/body/eval_jaxpr/dot_general | solution.py:86
  88.8 5.5 %convolution_bitcast_fusion.4 = f32[16,8192]{1,0:T(8,128)S(1)} fusion(f32[16,256]{1,0:T(8,128)S(1)} %get-tuple-element.260, f32[8192]{0:T(1024)S(1)} %fusion.111, f32[256]{0:T(256)S(1)} %iota_convert_fusion.5), kind=kOutput, calls=%fused_computation.1.clone.clone.1 | convolution fusion | flops 411041792 | bytes 574464 | tf_op jit(solution)/shard_map/while/body/eval_jaxpr/dot_general | solution.py:86
  96.0 5.5 %convolution_bitcast_fusion.4 = f32[16,8192]{1,0:T(8,128)S(1)} fusion(f32[16,256]{1,0:T(8,128)S(1)} %get-tuple-element.260, f32[8192]{0:T(1024)S(1)} %fusion.111, f32[256]{0:T(256)S(1)} %iota_convert_fusion.5), kind=kOutput, calls=%fused_computation.1.clone.clone.1 | convolution fusion | flops 411041792 | bytes 574464 | tf_op jit(solution)/shard_map/while/body/eval_jaxpr/dot_general | solution.py:86
  103.3 2.7 %collective-permute-done.12 = f32[4,8,2,1,8]{4,2,1,0,3:T(2,128)S(1)} collective-permute-done((f32[4,8,2,1,8]{4,2,1,0,3:T(2,128)S(1)}, f32[4,8,2,1,8]{4,2,1,0,3:T(2,128)S(1)}, u32[]{:S(2)}, u32[]{:S(2)}) %collective-permute-start.12) | collective-permute-done | bytes 2080 | tf_op jit(solution)/shard_map/ppermute | solution.py:17
  106.3 4.0 %collective-permute-done.13 = f32[4,8,1,1,8]{4,2,1,0,3:T(1,128)S(1)} collective-permute-done((f32[4,8,1,1,8]{4,2,1,0,3:T(1,128)S(1)}, f32[4,8,1,1,8]{4,2,1,0,3:T(1,128)S(1)}, u32[]{:S(2)}, u32[]{:S(2)}) %collective-permute-start.13) | collective-permute-done | bytes 1056 | tf_op jit(solution)/shard_map/ppermute | solution.py:17
  111.0 7.0 %all-to-all-start = ((f32[4,8,1,1,8]{4,2,0,3,1:T(1,128)}), f32[4,8,1,1,8]{4,2,0,3,1:T(1,128)S(1)}, u32[]{:S(2)}, u32[]{:S(2)}) async-start(f32[4,8,1,1,8]{4,2,0,3,1:T(1,128)} %copy.43), calls=%async_computation | async-start | bytes 32768 | tf_op jit(solution)/shard_map/all_to_all | solution.py:134
  118.0 2.9 %all-to-all-done = f32[4,8,1,1,8]{4,2,0,3,1:T(1,128)S(1)} async-done(((f32[4,8,1,1,8]{4,2,0,3,1:T(1,128)}), f32[4,8,1,1,8]{4,2,0,3,1:T(1,128)S(1)}, u32[]{:S(2)}, u32[]{:S(2)}) %all-to-all-start) | async-done | bytes 1056 | tf_op jit(solution)/shard_map/all_to_all | solution.py:134
  121.2 1.9 %collective-permute-start.14 = (f32[4,1,64]{2,1,0:T(1,128)S(1)}, f32[4,1,64]{2,1,0:T(1,128)S(1)}, u32[]{:S(2)}, u32[]{:S(2)}) collective-permute-start(f32[4,1,64]{2,1,0:T(1,128)S(1)} %constant_dynamic-update-slice_fusion), channel_id=1, source_target_pairs={{1,0},{2,1},{3,2},{4,3},{5,4},{6,5},{7,6},{8,7},{9,8},{10,9},{11,1... | collective-permute-start | bytes 3080 | tf_op jit(solution)/shard_map/ppermute | solution.py:36
  124.3 7.2 %collective-permute-done.14 = f32[4,1,64]{2,1,0:T(1,128)S(1)} collective-permute-done((f32[4,1,64]{2,1,0:T(1,128)S(1)}, f32[4,1,64]{2,1,0:T(1,128)S(1)}, u32[]{:S(2)}, u32[]{:S(2)}) %collective-permute-start.14) | collective-permute-done | bytes 1056 | tf_op jit(solution)/shard_map/ppermute | solution.py:36
  (166 shorter events, 48.2 us)
Async XLA Ops:
  2.8 3.9 %collective-permute-start = (f32[6,1,8,128]{3,1,2,0:T(1,128)S(1)}, f32[6,1,8,128]{3,1,2,0:T(1,128)S(1)}, u32[]{:S(2)}, u32[]{:S(2)}) collective-permute-start(f32[6,1,8,128]{3,1,2,0:T(1,128)S(1)} %get-tuple-element.165), channel_id=1, source_target_pairs={{0,32},{32,64},{64,96},{96,128},{128,160},{160,192},{192,224},{224... | collective-permute-start | bytes 73736 | tf_op jit(solution)/shard_map/ppermute | solution.py:27
  5.7 3.9 %collective-permute-start.1 = (f32[6,1,8,128]{3,1,2,0:T(1,128)S(1)}, f32[6,1,8,128]{3,1,2,0:T(1,128)S(1)}, u32[]{:S(2)}, u32[]{:S(2)}) collective-permute-start(f32[6,1,8,128]{3,1,2,0:T(1,128)S(1)} %get-tuple-element.166), channel_id=1, source_target_pairs={{32,0},{64,32},{96,64},{128,96},{160,128},{192,160},{224,192},{0,2... | collective-permute-start | bytes 73736 | tf_op jit(solution)/shard_map/ppermute | solution.py:28
  9.7 4.1 %collective-permute-start.2 = (f32[6,34,1,128]{3,1,2,0:T(8,128)S(1)}, f32[6,34,1,128]{3,1,2,0:T(8,128)S(1)}, u32[]{:S(2)}, u32[]{:S(2)}) collective-permute-start(f32[6,34,1,128]{3,1,2,0:T(8,128)S(1)} %get-tuple-element.163), channel_id=1, source_target_pairs={{0,4},{4,8},{8,12},{12,16},{16,20},{20,24},{24,28},{28,0},{1,5},{5... | collective-permute-start | bytes 313352 | tf_op jit(solution)/shard_map/ppermute | solution.py:27
  11.9 5.5 %collective-permute-start.3 = (f32[6,34,1,128]{3,1,2,0:T(8,128)S(1)}, f32[6,34,1,128]{3,1,2,0:T(8,128)S(1)}, u32[]{:S(2)}, u32[]{:S(2)}) collective-permute-start(f32[6,34,1,128]{3,1,2,0:T(8,128)S(1)} %get-tuple-element.164), channel_id=1, source_target_pairs={{4,0},{8,4},{12,8},{16,12},{20,16},{24,20},{28,24},{0,28},{5,1},{9... | collective-permute-start | bytes 313352 | tf_op jit(solution)/shard_map/ppermute | solution.py:28
  19.2 3.1 %collective-permute-start.4 = (f32[6,34,10,1]{1,0,3,2:T(8,128)}, f32[6,34,10,1]{1,0,3,2:T(8,128)S(1)}, u32[]{:S(2)}, u32[]{:S(2)}) collective-permute-start(f32[6,34,10,1]{1,0,3,2:T(8,128)} %copy.20), channel_id=1, source_target_pairs={{0,1},{1,2},{2,3},{3,0},{4,5},{5,6},{6,7},{7,4},{8,9},{9,10},{10,1... | collective-permute-start | bytes 24488 | tf_op jit(solution)/shard_map/ppermute | solution.py:27
  19.8 4.1 %collective-permute-start.5 = (f32[6,34,10,1]{1,0,3,2:T(8,128)S(1)}, f32[6,34,10,1]{1,0,3,2:T(8,128)S(1)}, u32[]{:S(2)}, u32[]{:S(2)}) collective-permute-start(f32[6,34,10,1]{1,0,3,2:T(8,128)S(1)} %copy.21), channel_id=1, source_target_pairs={{1,0},{2,1},{3,2},{0,3},{5,4},{6,5},{7,6},{4,7},{9,8},{10,9},{11,1... | collective-permute-start | bytes 24488 | tf_op jit(solution)/shard_map/ppermute | solution.py:28
  30.9 1.3 copy-start
  30.9 1.6 %copy-start.1 = (f32[6,34,10,1]{3,1,2,0:T(8,128)S(1)}, f32[6,34,10,1]{3,1,2,0:T(8,128)}, u32[]{:S(2)}) copy-start(f32[6,34,10,1]{3,1,2,0:T(8,128)} %copy.23) | copy-start | bytes 24484
  35.4 1.1 copy-start.4
  36.5 2.7 %copy-start.7 = (f32[4,3,256]{2,0,1:T(4,128)S(1)}, f32[4,3,256]{2,0,1:T(4,128)}, u32[]{:S(2)}) copy-start(f32[4,3,256]{2,0,1:T(4,128)} %param.10) | copy-start | bytes 36868
  36.5 2.7 %copy-start.8 = (f32[4,256]{1,0:T(4,128)S(1)}, f32[4,256]{1,0:T(4,128)}, u32[]{:S(2)}) copy-start(f32[4,256]{1,0:T(4,128)} %param.11) | copy-start | bytes 12292
  37.5 2.9 %collective-permute-start.6 = (f32[5,1,8,128]{3,1,2,0:T(1,128)S(1)}, f32[5,1,8,128]{3,1,2,0:T(1,128)S(1)}, u32[]{:S(2)}, u32[]{:S(2)}) collective-permute-start(f32[5,1,8,128]{3,1,2,0:T(1,128)S(1)} %get-tuple-element.169), channel_id=1, source_target_pairs={{0,32},{32,64},{64,96},{96,128},{128,160},{160,192},{192,224},{224... | collective-permute-start | bytes 61448 | tf_op jit(solution)/shard_map/ppermute | solution.py:27
  37.7 3.9 %collective-permute-start.7 = (f32[5,1,8,128]{3,1,2,0:T(1,128)S(1)}, f32[5,1,8,128]{3,1,2,0:T(1,128)S(1)}, u32[]{:S(2)}, u32[]{:S(2)}) collective-permute-start(f32[5,1,8,128]{3,1,2,0:T(1,128)S(1)} %get-tuple-element.170), channel_id=1, source_target_pairs={{32,0},{64,32},{96,64},{128,96},{160,128},{192,160},{224,192},{0,2... | collective-permute-start | bytes 61448 | tf_op jit(solution)/shard_map/ppermute | solution.py:28
  41.7 4.2 %collective-permute-start.8 = (f32[5,34,1,128]{3,1,2,0:T(8,128)S(1)}, f32[5,34,1,128]{3,1,2,0:T(8,128)S(1)}, u32[]{:S(2)}, u32[]{:S(2)}) collective-permute-start(f32[5,34,1,128]{3,1,2,0:T(8,128)S(1)} %get-tuple-element.167), channel_id=1, source_target_pairs={{0,4},{4,8},{8,12},{12,16},{16,20},{20,24},{24,28},{28,0},{1,5},{5... | collective-permute-start | bytes 261128 | tf_op jit(solution)/shard_map/ppermute | solution.py:27
  44.3 5.3 %collective-permute-start.9 = (f32[5,34,1,128]{3,1,2,0:T(8,128)S(1)}, f32[5,34,1,128]{3,1,2,0:T(8,128)S(1)}, u32[]{:S(2)}, u32[]{:S(2)}) collective-permute-start(f32[5,34,1,128]{3,1,2,0:T(8,128)S(1)} %get-tuple-element.168), channel_id=1, source_target_pairs={{4,0},{8,4},{12,8},{16,12},{20,16},{24,20},{28,24},{0,28},{5,1},{9... | collective-permute-start | bytes 261128 | tf_op jit(solution)/shard_map/ppermute | solution.py:28
  44.3 12.9 %copy-start.6 = (f32[4,4,256]{2,1,0:T(4,128)}, f32[4,4,256]{2,1,0:T(4,128)S(1)}, u32[]{:S(2)}) copy-start(f32[4,4,256]{2,1,0:T(4,128)S(1)} %pad_maximum_fusion.27) | copy-start | bytes 49156
  53.2 4.1 %collective-permute-start.10 = (f32[5,34,10,1]{1,2,3,0:T(8,128)S(1)}, f32[5,34,10,1]{1,2,3,0:T(8,128)S(1)}, u32[]{:S(2)}, u32[]{:S(2)}) collective-permute-start(f32[5,34,10,1]{1,2,3,0:T(8,128)S(1)} %copy.28), channel_id=1, source_target_pairs={{0,1},{1,2},{2,3},{3,0},{4,5},{5,6},{6,7},{7,4},{8,9},{9,10},{10,1... | collective-permute-start | bytes 20408 | tf_op jit(solution)/shard_map/ppermute | solution.py:27
  56.5 4.4 %collective-permute-start.11 = (f32[5,34,10,1]{1,2,3,0:T(8,128)}, f32[5,34,10,1]{1,2,3,0:T(8,128)}, u32[]{:S(2)}, u32[]{:S(2)}) collective-permute-start(f32[5,34,10,1]{1,2,3,0:T(8,128)} %copy.29), channel_id=1, source_target_pairs={{1,0},{2,1},{3,2},{0,3},{5,4},{6,5},{7,6},{4,7},{9,8},{10,9},{11,1... | collective-permute-start | bytes 20408 | tf_op jit(solution)/shard_map/ppermute | solution.py:28
  68.2 1.2 copy-start.2
  68.2 1.5 %copy-start.3 = (f32[5,34,10,1]{3,1,2,0:T(8,128)S(1)}, f32[5,34,10,1]{3,1,2,0:T(8,128)}, u32[]{:S(2)}) copy-start(f32[5,34,10,1]{3,1,2,0:T(8,128)} %copy.31) | copy-start | bytes 20404
  103.2 2.9 %collective-permute-start.12 = (f32[4,8,2,1,8]{4,2,1,0,3:T(2,128)S(1)}, f32[4,8,2,1,8]{4,2,1,0,3:T(2,128)S(1)}, u32[]{:S(2)}, u32[]{:S(2)}) collective-permute-start(f32[4,8,2,1,8]{4,2,1,0,3:T(2,128)S(1)} %bitcast.108), channel_id=1, source_target_pairs={{0,1},{1,0},{2,3},{3,2},{4,5},{5,4},{6,7},{7,6},{8,9},{9,8},{10,11... | collective-permute-start | bytes 6152 | tf_op jit(solution)/shard_map/ppermute | solution.py:17
  106.1 4.2 %collective-permute-start.13 = (f32[4,8,1,1,8]{4,2,1,0,3:T(1,128)S(1)}, f32[4,8,1,1,8]{4,2,1,0,3:T(1,128)S(1)}, u32[]{:S(2)}, u32[]{:S(2)}) collective-permute-start(f32[4,8,1,1,8]{4,2,1,0,3:T(1,128)S(1)} %constant_dynamic-slice_fusion.2), channel_id=1, source_target_pairs={{0,2},{1,3},{2,0},{3,1},{4,6},{5,7},{6,4},{7,5},{8,10},{9,11},{10,... | collective-permute-start | bytes 3080 | tf_op jit(solution)/shard_map/ppermute | solution.py:17
  111.0 10.0 %all-to-all-start = ((f32[4,8,1,1,8]{4,2,0,3,1:T(1,128)}), f32[4,8,1,1,8]{4,2,0,3,1:T(1,128)S(1)}, u32[]{:S(2)}, u32[]{:S(2)}) async-start(f32[4,8,1,1,8]{4,2,0,3,1:T(1,128)} %copy.43), calls=%async_computation | async-start | bytes 32768 | tf_op jit(solution)/shard_map/all_to_all | solution.py:134
  121.2 10.3 %collective-permute-start.14 = (f32[4,1,64]{2,1,0:T(1,128)S(1)}, f32[4,1,64]{2,1,0:T(1,128)S(1)}, u32[]{:S(2)}, u32[]{:S(2)}) collective-permute-start(f32[4,1,64]{2,1,0:T(1,128)S(1)} %constant_dynamic-update-slice_fusion), channel_id=1, source_target_pairs={{1,0},{2,1},{3,2},{4,3},{5,4},{6,5},{7,6},{8,7},{9,8},{10,9},{11,1... | collective-permute-start | bytes 3080 | tf_op jit(solution)/shard_map/ppermute | solution.py:36
  (1 other events, 1.1 us)
where the time goes:
time: 134 us; the launch traced here: 133 us
  waiting for transfers between devices  37.2 us (28%)
  local copies, waits for them, and re-layouts  29.4 us (22%)
  matrix products  24.1 us (18%)
  starting transfers between devices  21.7 us (16%)
  other arithmetic  19 us (14%)
    dot_general x4, matrix products, classify(): jnp.dot(table_rows, hat_weights, precision=lax.Precision.HIGHEST, preferr...  21.9 us
    ppermute x6, waiting for transfers between devices, with_halo(): after = lax.ppermute(first, axis, down)  13.9 us
    ppermute x6, starting transfers between devices, with_halo(): before = lax.ppermute(last, axis, up)  8.85 us
    unnamed x25, local copies, waits for them, and re-layouts  7.57 us
    sub x6, other arithmetic, divergence(): 0.5 * (lax.slice_in_dim(fluxes, 0, length - 1, axis=axis_now) + lax.slice...  7.31 us
    ppermute x1, waiting for transfers between devices, from_behind(): lax.ppermute(value, axis, [(source, source + steps) for source in range(f...  7.18 us
    all_to_all x1, starting transfers between devices, spread_rows(): lax.all_to_all(grouped, 'gy', split_axis=1, concat_axis=4, tiled=True)  7.04 us
    ppermute x2, waiting for transfers between devices, swapped(): lax.ppermute(x, axis, [(i, i ^ 1 << stride) for i in range(lax.axis_size(...  6.73 us
  transfers between devices with their start and end apart: 16, of which 15 were waited for; matrix products, arithmetic and copies ran while one was open for 6% of the time, Pallas kernels for 0%

commit v1 on v0

v1 whole, which is shorter than its diff:
```python
import functools

import jax
import jax.numpy as jnp
from jax import lax
from jax.experimental import pallas as pl
from jax.experimental.pallas import tpu as pltpu
from jax.sharding import PartitionSpec as P

SW = 1920
ZOOM = 4
CLASSES = 4
LUT = 256

dissipation = 3.0
courant = 0.11
density_low = 0.6
density_high = 1.6

F32 = jnp.float32
LANES = 128
SUBS = 8
VMEM_LIMIT = 48 * 1024 * 1024


def iota(shape, dim):
    return lax.broadcasted_iota(jnp.int32, shape, dim)


def halves(direction, cell):
    density, m1, m2, m3, energy, gamma = cell
    momenta = (m1, m2, m3)
    inverse = 1.0 / density
    kinetic = 0.5 * (m1 * m1 + m2 * m2 + m3 * m3) * inverse
    pressure = (gamma - 1.0) * (energy - kinetic)
    half_p = 0.5 * pressure
    scaled = [(0.5 * dissipation) * q for q in (density, m1, m2, m3, energy)]
    result = []
    for d in direction:
        half_v = 0.5 * momenta[d] * inverse
        flux = [0.5 * momenta[d]]
        for member in range(3):
            component = momenta[member] * half_v
            flux.append(component + half_p if member == d else component)
        flux.append((energy + pressure) * half_v)
        result.append(
            ([a - b for a, b in zip(flux, scaled)], [a + b for a, b in zip(flux, scaled)])
        )
    return result


def prepare_halo(ym, yp, zm, zp, gym, gyp, gzm, gzp, y_below, y_above, z_edge):
    below = halves((1,), [ym[f] for f in range(5)] + [gym])[0][1]
    above = halves((1,), [yp[f] for f in range(5)] + [gyp])[0][0]
    for f in range(5):
        y_below[f] = below[f]
        y_above[f] = above[f]
    z_lower = [pltpu.roll(zm[f], 1, 1) for f in range(5)] + [pltpu.roll(gzm, 1, 1)]
    z_upper = [pltpu.roll(zp[f], LANES - 1, 1) for f in range(5)] + [
        pltpu.roll(gzp, LANES - 1, 1)
    ]
    odd = iota((SUBS, LANES), 1) % 2 == 1
    merged = [jnp.where(odd, a, b) for a, b in zip(z_lower, z_upper)]
    merged = [jnp.where(iota((SUBS, LANES), 1) < 64, q, 1.0) for q in merged]
    up, down = halves((2,), merged)[0]
    for f in range(5):
        z_edge[f] = jnp.where(odd, down[f], up[f])


def row_terms(cell, row, y_below, y_above, z_edge):
    lane = iota((SUBS, LANES), 1)
    sub = iota((SUBS, LANES), 0)
    (x_up, x_down), (y_up, y_down), (z_up, z_down) = halves((0, 1, 2), cell)
    core = []
    for f in range(5):
        edge = pltpu.roll(z_edge[f], LANES - 1 - 2 * row, 1)
        from_above = jnp.where(lane == LANES - 1, edge, pltpu.roll(z_up[f], LANES - 1, 1))
        from_below = jnp.where(lane == 0, edge, pltpu.roll(z_down[f], 1, 1))
        total = 6.0 * (0.5 * dissipation) * cell[f] + (from_above - from_below)
        from_above = jnp.where(
            sub == SUBS - 1, y_above[f, pl.ds(row, 1), :], pltpu.roll(y_up[f], SUBS - 1, 0)
        )
        from_below = jnp.where(
            sub == 0, y_below[f, pl.ds(row, 1), :], pltpu.roll(y_down[f], 1, 0)
        )
        core.append(total + (from_above - from_below))
    return x_up, x_down, core


def walk(rows, load, x_first, x_last, finish, y_below, y_above, z_edge):
    down_before = halves((0,), x_first)[0][1]
    up_after = halves((0,), x_last)[0][0]

    def step(row, carry, emit):
        pending, down = carry
        x_up, x_down, core = row_terms(load(row), row, y_below, y_above, z_edge)
        if emit:
            finish(row - 1, [a + b for a, b in zip(pending, x_up)])
        return [a - b for a, b in zip(core, down)], x_down

    carry = step(0, (None, down_before), False)
    carry = lax.fori_loop(1, rows, lambda row, c: step(row, c, True), carry)
    finish(rows - 1, [a + b for a, b in zip(carry[0], up_after)])


def put_faces(f, row, rows, value, y_low, y_high, z_pack):
    y_low[f, pl.ds(row, 1), :] = value[0:1, :]
    y_high[f, pl.ds(row, 1), :] = value[SUBS - 1 : SUBS, :]
    lane = iota((SUBS, LANES), 1)
    z_pack[f] = jnp.where(lane // 2 == row, pltpu.roll(value, 2 * row + 1, 1), z_pack[f])


def pack_kernel(u, g, x_low, x_high, y_low, y_high, z_pack):
    rows = u.shape[1]
    z_pack[...] = jnp.zeros(z_pack.shape, F32)
    for f in range(6):
        x_low[f] = u[f, 0] if f < 5 else g[0]
        x_high[f] = u[f, rows - 1] if f < 5 else g[rows - 1]

    def body(row, _):
        for f in range(6):
            put_faces(f, row, rows, u[f, row] if f < 5 else g[row], y_low, y_high, z_pack)
        return 0

    lax.fori_loop(0, rows, body, 0)


def half_kernel(
    u, g, xm, xp, ym, yp, zm, zp, h, x_low, x_high, y_low, y_high, z_pack, y_below, y_above, z_edge
):
    rows = u.shape[1]
    prepare_halo(ym, yp, zm, zp, ym[5], yp[5], zm[5], zp[5], y_below, y_above, z_edge)
    z_pack[...] = jnp.zeros(z_pack.shape, F32)

    def load(row):
        return [u[f, row] for f in range(5)] + [g[row]]

    def finish(row, change):
        for f in range(5):
            value = u[f, row] - courant * change[f]
            h[f, row] = value
            put_faces(f, row, rows, value, y_low, y_high, z_pack)

    walk(
        rows,
        load,
        [xm[f] for f in range(6)],
        [xp[f] for f in range(6)],
        finish,
        y_below,
        y_above,
        z_edge,
    )
    for f in range(5):
        x_low[f] = h[f, 0]
        x_high[f] = h[f, rows - 1]


def lookup(density, species, tables):
    position = (density - density_low) * ((LUT - 1) / (density_high - density_low))
    knot = jnp.clip(jnp.floor(position), 0.0, LUT - 1.0)
    offset = position - knot
    lower_weight = jnp.maximum(0.0, 1.0 - jnp.abs(offset))
    upper_weight = jnp.maximum(0.0, 1.0 - jnp.abs(offset - 1.0))
    index = knot.astype(jnp.int32)
    lane_index = index % LANES
    bits = (index >= LANES, species % 2 == 1, species >= 2)
    result = []
    for channel in range(4):
        total = None
        for side, weight in ((0, lower_weight), (1, upper_weight)):
            values = [
                jnp.take_along_axis(
                    tables[channel, side, k], lane_index, axis=1, mode="promise_in_bounds"
                )
                for k in range(8)
            ]
            for bit in bits:
                values = [
                    jnp.where(bit, values[k + 1], values[k]) for k in range(0, len(values), 2)
                ]
            term = weight * values[0]
            total = term if total is None else total + term
        result.append(total)
    return result


def spread_tables(lut_lower, lut_upper, tables):
    for channel in range(4):
        for k in range(8):
            for side, source in ((0, lut_lower), (1, lut_upper)):
                row = source[pl.ds(channel * 8 + k, 1), :]
                tables[channel, side, k] = jnp.broadcast_to(row, (SUBS, LANES))


def split_dot(value, weights):
    first = value.astype(jnp.bfloat16)
    rest = value - first.astype(F32)
    second = rest.astype(jnp.bfloat16)
    third = (rest - second.astype(F32)).astype(jnp.bfloat16)
    total = jnp.dot(first, weights, preferred_element_type=F32)
    total += jnp.dot(second, weights, preferred_element_type=F32)
    return total + jnp.dot(third, weights, preferred_element_type=F32)


def integrate(properties, planes, rows):
    extinction = properties[3]
    below = (iota((LANES, LANES), 0) < iota((LANES, LANES), 1)).astype(jnp.bfloat16)
    before = split_dot(extinction, below)
    factor = (1.0 - jnp.exp(-extinction)) * jnp.exp(-before)
    lane = iota((SUBS, LANES), 1)
    gathered = []
    for channel in range(4):
        if channel < 3:
            weighted = properties[channel] * factor
        else:
            weighted = extinction
        summed = jnp.sum(weighted, axis=1, keepdims=True)
        if channel == 3:
            summed = jnp.exp(-summed)
        plane = jnp.zeros((SUBS, LANES), F32)
        for row in range(rows):
            plane = jnp.where(lane == row, summed[row * SUBS : (row + 1) * SUBS], plane)
        gathered.append(plane)
    block = jnp.concatenate(gathered + [jnp.zeros((LANES - 32, LANES), F32)], axis=0)
    planes[...] = jnp.transpose(block)[:rows]


def step_kernel(
    u, g, sp, h, gxm, gxp, gym, gyp, gzm, gzp, xm, xp, ym, yp, zm, zp, lut_lower, lut_upper,
    new, planes, y_below, y_above, z_edge, tables, properties
):
    rows = u.shape[1]
    spread_tables(lut_lower, lut_upper, tables)
    prepare_halo(ym, yp, zm, zp, gym[...], gyp[...], gzm[...], gzp[...], y_below, y_above, z_edge)

    def load(row):
        return [h[f, row] for f in range(5)] + [g[row]]

    def finish(row, change):
        for f in range(5):
            value = 0.5 * (u[f, row] + h[f, row] - courant * change[f])
            new[f, row] = value
            if f == 0:
                density = value
        found = lookup(density, sp[row], tables)
        for channel in range(4):
            properties[channel, pl.ds(pl.multiple_of(row * SUBS, SUBS), SUBS), :] = found[channel]

    walk(
        rows,
        load,
        [xm[f] for f in range(5)] + [gxm[...]],
        [xp[f] for f in range(5)] + [gxp[...]],
        finish,
        y_below,
        y_above,
        z_edge,
    )
    integrate(properties, planes, rows)


def image_kernel(across_y, across_z, flags, parts, out):
    lane = iota((across_y, LANES), 1)
    channel = (lane // 8) % 4
    total = None
    for k in reversed(range(across_z)):
        part = parts[pl.ds(k, across_y, stride=across_z), :]
        through = part
        for c in range(3):
            moved = pltpu.roll(part, LANES - (24 - 8 * c), 1)
            through = jnp.where(channel == c, moved, through)
        if total is None:
            total = part
        else:
            total = jnp.where(channel == 3, 0.0, part) + through * total
    total = jnp.where(channel == 3, 1.0 - total, total)
    keep = jnp.where(lane >= 32, flags[0], 1.0)
    total = jnp.where(lane < 64, total * keep, 0.0)
    sub8 = iota((8, LANES), 0)
    lane8 = iota((8, LANES), 1)
    moved = jnp.zeros((8, LANES), F32)
    for k in range(across_y):
        wide = jnp.broadcast_to(total[k : k + 1, :], (8, LANES))
        shifted = wide
        for bit in range(3):
            amount = (LANES - (8 << bit)) % LANES
            shifted = jnp.where(
                (sub8 >> bit) & 1 == 1, pltpu.roll(shifted, amount, 1), shifted
            )
        if k:
            shifted = pltpu.roll(shifted, 8 * k, 1)
        moved = jnp.where(lane8 // 8 == k, shifted, moved)
    columns = 8 * across_y
    screen = jnp.concatenate(
        [
            (1.0 - q / ZOOM) * moved[c : c + 1, :columns]
            + (q / ZOOM) * moved[4 + c : 5 + c, :columns]
            for c in range(4)
            for q in range(ZOOM)
        ],
        axis=0,
    )
    position = iota((columns, SW), 1).astype(F32) * (columns / SW)
    horizontal = jnp.maximum(
        0.0, 1.0 - jnp.abs(iota((columns, SW), 0).astype(F32) - position)
    )
    image = jnp.dot(
        screen, horizontal, precision=lax.Precision.HIGHEST, preferred_element_type=F32
    )
    for c in range(4):
        out[c] = image[c * ZOOM : (c + 1) * ZOOM]


def shifted(value, axis, steps):
    size = lax.axis_size(axis)
    return lax.ppermute(value, axis, [(i, (i + steps) % size) for i in range(size)])


def exchange(x_low, x_high, y_low, y_high, z_pack):
    return (
        shifted(x_high, "gx", 1),
        shifted(x_low, "gx", -1),
        shifted(y_high, "gy", 1),
        shifted(y_low, "gy", -1),
        shifted(z_pack, "gz", 1),
        shifted(z_pack, "gz", -1),
    )


def struct(*shape):
    return jax.ShapeDtypeStruct(shape, F32)


def faces(fields, rows):
    return (
        struct(fields, SUBS, LANES),
        struct(fields, SUBS, LANES),
        struct(fields, rows, LANES),
        struct(fields, rows, LANES),
        struct(fields, SUBS, LANES),
    )


def local(conserved, gamma_field, species, lut_color, lut_extinction):
    rows = conserved.shape[1]
    params = pltpu.CompilerParams(vmem_limit_bytes=VMEM_LIMIT)
    halo_scratch = [
        pltpu.VMEM((5, rows, LANES), F32),
        pltpu.VMEM((5, rows, LANES), F32),
        pltpu.VMEM((5, SUBS, LANES), F32),
    ]
    across_y = lax.axis_size("gy")
    across_z = lax.axis_size("gz")

    lut_table = jnp.concatenate([lut_color, lut_extinction[:, None, :]], axis=1)
    lut_lower = lut_table.transpose(1, 0, 2).reshape(32, LANES)
    lut_upper = (
        jnp.pad(lut_table[:, :, 1:], ((0, 0), (0, 0), (0, 1))).transpose(1, 0, 2).reshape(32, LANES)
    )

    first = exchange(
        *pl.pallas_call(pack_kernel, out_shape=faces(6, rows), compiler_params=params, name="pack")(
            conserved, gamma_field
        )
    )
    halfway, *edges = pl.pallas_call(
        half_kernel,
        out_shape=(struct(*conserved.shape),) + faces(5, rows),
        scratch_shapes=halo_scratch,
        compiler_params=params,
        name="half",
    )(conserved, gamma_field, *first)
    second = exchange(*edges)
    new_state, planes = pl.pallas_call(
        step_kernel,
        out_shape=(struct(*conserved.shape), struct(rows, LANES)),
        scratch_shapes=halo_scratch
        + [
            pltpu.VMEM((4, 2, 8, SUBS, LANES), F32),
            pltpu.VMEM((4, rows * SUBS, LANES), F32),
        ],
        compiler_params=params,
        name="step",
    )(
        conserved,
        gamma_field,
        species,
        halfway,
        *[part[5] for part in first],
        *second,
        lut_lower,
        lut_upper,
    )
    next_first = shifted(planes[:1], "gx", -1)
    below = jnp.concatenate([planes[1:], next_first], axis=0)
    grouped = jnp.concatenate(
        [planes[:, :32], below[:, :32], jnp.zeros((rows, 64), F32)], axis=1
    )
    merged = lax.all_to_all(
        grouped.reshape(across_y * across_z, 1, LANES), ("gy", "gz"), 0, 0, tiled=True
    ).reshape(across_y * across_z, LANES)
    place = lax.axis_index(("gx", "gy", "gz"))
    last = lax.axis_size(("gx", "gy", "gz")) - 1
    flags = jnp.where(place == last, 0.0, 1.0).reshape(1)
    image = pl.pallas_call(
        functools.partial(image_kernel, across_y, across_z),
        out_shape=struct(4, ZOOM, SW),
        in_specs=[
            pl.BlockSpec(memory_space=pltpu.SMEM),
            pl.BlockSpec(memory_space=pltpu.VMEM),
        ],
        compiler_params=params,
        name="image",
    )(flags, merged)
    return new_state, image


def solution(mesh):
    return jax.shard_map(
        local,
        mesh=mesh,
        in_specs=(P(None, "gx", "gy", "gz"), P("gx", "gy", "gz"), P("gx", "gy", "gz"), P(), P()),
        out_specs=(P(None, "gx", "gy", "gz"), P(None, ("gx", "gy", "gz"), None)),
        check_vma=False,
    )
```

time: 134 us -> 59.2 us (0.44)
  the two profiles are of different devices: /device:TPU:127 before, /device:TPU:1 now
where the time goes in v1:
time: 59.2 us; the launch traced here: 59 us
  starting transfers between devices  31.8 us (54%)
  Pallas kernels  13.7 us (23%)
  waiting for transfers between devices  9.85 us (17%)
  local copies, waits for them, and re-layouts  2.13 us (4%)
  other arithmetic  0.76 us (1%)
  between operations  0.76 us (1%)
    ppermute x13, starting transfers between devices, shifted(): lax.ppermute(value, axis, [(i, (i + steps) % size) for i in range(size)])  23.7 us
    all_to_all x1, starting transfers between devices, local(): lax.all_to_all(grouped.reshape(across_y * across_z, 1, LANES), ('gy', 'gz...  8.08 us
    all_to_all x1, waiting for transfers between devices, local(): lax.all_to_all(grouped.reshape(across_y * across_z, 1, LANES), ('gy', 'gz...  6.92 us
    pallas_call x1, Pallas kernels, local(): pl.pallas_call(step_kernel, out_shape=(struct(*conserved.shape), struct(r...  6.7 us
    pallas_call x1, Pallas kernels, local(): pl.pallas_call(half_kernel, out_shape=(struct(*conserved.shape),) + faces...  3.03 us
    ppermute x13, waiting for transfers between devices, shifted(): lax.ppermute(value, axis, [(i, (i + steps) % size) for i in range(size)])  2.93 us
    pallas_call x1, Pallas kernels, local(): pl.pallas_call(pack_kernel, out_shape=faces(6, rows), compiler_params=par...  2.59 us
    unnamed x14, local copies, waits for them, and re-layouts  2.01 us
  transfers between devices with their start and end apart: 14, of which 4 were waited for; matrix products, arithmetic and copies ran while one was open for 0% of the time, Pallas kernels for 0%

profile of v1, /device:TPU:1, one launch (start us, length us, event | category | flops | bytes accessed | tf_op | source)
XLA Modules:
  0.0 59.0 jit_solution(1241543725375266389)
XLA Ops:
  0.6 1.1 %copy-done = f32[5,32,8,128]{3,2,1,0:T(8,128)S(1)} copy-done((f32[5,32,8,128]{3,2,1,0:T(8,128)S(1)}, f32[5,32,8,128]{3,2,1,0:T(8,128)}, u32[]{:S(2)}) %copy-start) | copy-done | bytes 655384
  1.7 0.9 %copy-done.2 = f32[32,8,128]{2,1,0:T(8,128)S(1)} copy-done((f32[32,8,128]{2,1,0:T(8,128)S(1)}, f32[32,8,128]{2,1,0:T(8,128)}, u32[]{:S(2)}) %copy-start.2) | copy-done | bytes 131096
  2.6 2.6 %pack.1 = (f32[6,8,128]{2,1,0:T(8,128)S(1)}, f32[6,8,128]{2,1,0:T(8,128)S(1)}, f32[6,32,128]{2,1,0:T(8,128)S(1)}, f32[6,32,128]{2,1,0:T(8,128)S(1)}, f32[6,8,128]{2,1,0:T(8,128)S(1)}) custom-call(f32[5,32,8,128]{3,2,1,0:T(8,128)S(1)} %copy-done, f32[32,8,128]{2,1,0:T(8,128)S(1)} %copy-done.2), custom_call_target="tpu_custom_call" | custom-call | tf_op jit(solution)/shard_map/pack/pallas_call | solution.py:363
  5.2 2.2 %collective-permute-start.4 = (f32[6,8,128]{2,1,0:T(8,128)S(1)}, f32[6,8,128]{2,1,0:T(8,128)S(1)}, u32[]{:S(2)}, u32[]{:S(2)}) collective-permute-start(f32[6,8,128]{2,1,0:T(8,128)S(1)} %get-tuple-element.19), channel_id=1, source_target_pairs={{0,1},{1,2},{2,3},{3,0},{4,5},{5,6},{6,7},{7,4},{8,9},{9,10},{10,1... | collective-permute-start | bytes 73736 | tf_op jit(solution)/shard_map/ppermute | solution.py:317
  7.4 1.5 %collective-permute-start.5 = (f32[6,8,128]{2,1,0:T(8,128)S(1)}, f32[6,8,128]{2,1,0:T(8,128)S(1)}, u32[]{:S(2)}, u32[]{:S(2)}) collective-permute-start(f32[6,8,128]{2,1,0:T(8,128)S(1)} %get-tuple-element.19), channel_id=1, source_target_pairs={{0,3},{1,0},{2,1},{3,2},{4,7},{5,4},{6,5},{7,6},{8,11},{9,8},{10,9... | collective-permute-start | bytes 73736 | tf_op jit(solution)/shard_map/ppermute | solution.py:317
  8.9 2.2 %collective-permute-start.2 = (f32[6,32,128]{2,1,0:T(8,128)S(1)}, f32[6,32,128]{2,1,0:T(8,128)S(1)}, u32[]{:S(2)}, u32[]{:S(2)}) collective-permute-start(f32[6,32,128]{2,1,0:T(8,128)S(1)} %get-tuple-element.17), channel_id=1, source_target_pairs={{0,4},{4,8},{8,12},{12,16},{16,20},{20,24},{24,28},{28,0},{1,5},{5... | collective-permute-start | bytes 294920 | tf_op jit(solution)/shard_map/ppermute | solution.py:317
  11.1 0.6 %collective-permute-start.3 = (f32[6,32,128]{2,1,0:T(8,128)S(1)}, f32[6,32,128]{2,1,0:T(8,128)S(1)}, u32[]{:S(2)}, u32[]{:S(2)}) collective-permute-start(f32[6,32,128]{2,1,0:T(8,128)S(1)} %get-tuple-element.18), channel_id=1, source_target_pairs={{0,28},{4,0},{8,4},{12,8},{16,12},{20,16},{24,20},{28,24},{1,29},{... | collective-permute-start | bytes 294920 | tf_op jit(solution)/shard_map/ppermute | solution.py:317
  11.8 1.0 %collective-permute-start = (f32[6,8,128]{2,1,0:T(8,128)S(1)}, f32[6,8,128]{2,1,0:T(8,128)S(1)}, u32[]{:S(2)}, u32[]{:S(2)}) collective-permute-start(f32[6,8,128]{2,1,0:T(8,128)S(1)} %get-tuple-element.15), channel_id=1, source_target_pairs={{0,32},{32,64},{64,96},{96,128},{128,160},{160,192},{192,224},{224... | collective-permute-start | bytes 73736 | tf_op jit(solution)/shard_map/ppermute | solution.py:317
  12.9 4.0 %collective-permute-start.1 = (f32[6,8,128]{2,1,0:T(8,128)S(1)}, f32[6,8,128]{2,1,0:T(8,128)S(1)}, u32[]{:S(2)}, u32[]{:S(2)}) collective-permute-start(f32[6,8,128]{2,1,0:T(8,128)S(1)} %get-tuple-element.16), channel_id=1, source_target_pairs={{0,224},{32,0},{64,32},{96,64},{128,96},{160,128},{192,160},{224,1... | collective-permute-start | bytes 73736 | tf_op jit(solution)/shard_map/ppermute | solution.py:317
  16.9 0.9 %collective-permute-done.1.xp = f32[6,8,128]{2,1,0:T(8,128)S(1)} collective-permute-done((f32[6,8,128]{2,1,0:T(8,128)S(1)}, f32[6,8,128]{2,1,0:T(8,128)S(1)}, u32[]{:S(2)}, u32[]{:S(2)}) %collective-permute-start.1) | collective-permute-done | bytes 24608 | tf_op jit(solution)/shard_map/ppermute | solution.py:317
  18.0 3.0 %half.1 = (f32[5,32,8,128]{3,2,1,0:T(8,128)S(1)}, f32[5,8,128]{2,1,0:T(8,128)S(1)}, f32[5,8,128]{2,1,0:T(8,128)S(1)}, f32[5,32,128]{2,1,0:T(8,128)S(1)}, f32[5,3...) custom-call(f32[5,32,8,128]{3,2,1,0:T(8,128)S(1)} %copy-done.1, f32[32,8,128]{2,1,0:T(8,128)S(1)} %copy-done.3, ...), custom_call_target="tpu_custom_call" | custom-call | tf_op jit(solution)/shard_map/half/pallas_call | solution.py:367
  21.0 0.2 collective-permute-start.10
  21.1 2.5 %collective-permute-start.11 = (f32[5,8,128]{2,1,0:T(8,128)S(1)}, f32[5,8,128]{2,1,0:T(8,128)S(1)}, u32[]{:S(2)}, u32[]{:S(2)}) collective-permute-start(f32[5,8,128]{2,1,0:T(8,128)S(1)} %get-tuple-element.25), channel_id=1, source_target_pairs={{0,3},{1,0},{2,1},{3,2},{4,7},{5,4},{6,5},{7,6},{8,11},{9,8},{10,9... | collective-permute-start | bytes 61448 | tf_op jit(solution)/shard_map/ppermute | solution.py:317
  23.7 3.3 %collective-permute-start.8 = (f32[5,32,128]{2,1,0:T(8,128)S(1)}, f32[5,32,128]{2,1,0:T(8,128)S(1)}, u32[]{:S(2)}, u32[]{:S(2)}) collective-permute-start(f32[5,32,128]{2,1,0:T(8,128)S(1)} %get-tuple-element.23), channel_id=1, source_target_pairs={{0,4},{4,8},{8,12},{12,16},{16,20},{20,24},{24,28},{28,0},{1,5},{5... | collective-permute-start | bytes 245768 | tf_op jit(solution)/shard_map/ppermute | solution.py:317
  27.0 3.3 %collective-permute-start.7 = (f32[5,8,128]{2,1,0:T(8,128)S(1)}, f32[5,8,128]{2,1,0:T(8,128)S(1)}, u32[]{:S(2)}, u32[]{:S(2)}) collective-permute-start(f32[5,8,128]{2,1,0:T(8,128)S(1)} %get-tuple-element.22), channel_id=1, source_target_pairs={{0,224},{32,0},{64,32},{96,64},{128,96},{160,128},{192,160},{224,1... | collective-permute-start | bytes 61448 | tf_op jit(solution)/shard_map/ppermute | solution.py:317
  30.4 1.3 %collective-permute-done.6.xm = f32[5,8,128]{2,1,0:T(8,128)S(1)} collective-permute-done((f32[5,8,128]{2,1,0:T(8,128)S(1)}, f32[5,8,128]{2,1,0:T(8,128)S(1)}, u32[]{:S(2)}, u32[]{:S(2)}) %collective-permute-start.6) | collective-permute-done | bytes 20512 | tf_op jit(solution)/shard_map/ppermute | solution.py:317
  31.7 6.7 %step.1 = (f32[5,32,8,128]{3,2,1,0:T(8,128)}, f32[32,128]{1,0:T(8,128)S(1)}) custom-call(f32[5,32,8,128]{3,2,1,0:T(8,128)S(1)} %copy-done.1, f32[32,8,128]{2,1,0:T(8,128)S(1)} %copy-done.3, s32[32,8,128]{2,1,0:T(8,128)S(1)} %copy-done.4, f32[5,32,8,128]{3,2,1,0:T(8,128)S(1)} %get-tuple-element.20.h, f32[8,128]{1,0:T(8,128)S(1)} %slice_bitcast_fusion.5.gxm, ...), custom_call_target="tpu_custom_call" | custom-call | tf_op jit(solution)/shard_map/step/pallas_call | solution.py:375
  38.4 2.8 %collective-permute-start.12 = (f32[1,128]{1,0:T(1,128)S(1)}, f32[1,128]{1,0:T(1,128)S(1)}, u32[]{:S(2)}, u32[]{:S(2)}) collective-permute-start(f32[1,128]{1,0:T(1,128)S(1)} %slice.42), channel_id=1, source_target_pairs={{0,224},{32,0},{64,32},{96,64},{128,96},{160,128},{192,160},{224,1... | collective-permute-start | bytes 1544 | tf_op jit(solution)/shard_map/ppermute | solution.py:317
  41.2 0.1 pad.7.clone
  41.3 0.6 %collective-permute-done.12 = f32[1,128]{1,0:T(1,128)S(1)} collective-permute-done((f32[1,128]{1,0:T(1,128)S(1)}, f32[1,128]{1,0:T(1,128)S(1)}, u32[]{:S(2)}, u32[]{:S(2)}) %collective-permute-start.12) | collective-permute-done | bytes 544 | tf_op jit(solution)/shard_map/ppermute | solution.py:317
  41.9 0.7 %fusion.3 = f32[32,128]{1,0:T(8,128)} fusion(f32[1,128]{1,0:T(1,128)S(1)} %collective-permute-done.12, f32[31,128]{1,0:T(8,128)S(1)} %slice.41, f32[32,32]{1,0:T(8,128)S(1)} %bitcast.22, f32[128]{0:T(128)S(1)} %pad.7.clone), kind=kLoop, calls=%fused_computation.9 | loop fusion | flops 32768 | bytes 37376 | tf_op jit(solution)/shard_map/concatenate | solution.py:397
  42.6 8.1 %all-to-all-start = ((f32[32,1,128]{2,1,0:T(1,128)}), f32[32,1,128]{2,1,0:T(1,128)S(1)}, u32[]{:S(2)}, u32[]{:S(2)}) async-start(f32[32,1,128]{2,1,0:T(1,128)} %bitcast.10), calls=%async_computation | async-start | bytes 32768 | tf_op jit(solution)/shard_map/all_to_all | solution.py:400
  50.7 6.9 %all-to-all-done = f32[32,1,128]{2,1,0:T(1,128)S(1)} async-done(((f32[32,1,128]{2,1,0:T(1,128)}), f32[32,1,128]{2,1,0:T(1,128)S(1)}, u32[]{:S(2)}, u32[]{:S(2)}) %all-to-all-start) | async-done | bytes 16416 | tf_op jit(solution)/shard_map/all_to_all | solution.py:400
  57.6 1.3 %image.1 = f32[4,4,1920]{2,1,0:T(4,128)} custom-call(f32[1]{0:T(128)} %bitcast.9.flags, f32[32,128]{1,0:T(8,128)S(1)} %bitcast.21), custom_call_target="tpu_custom_call" | custom-call | tf_op jit(solution)/shard_map/image/pallas_call | solution.py:406
  (38 shorter events, 0.2 us)
Async XLA Ops:
  0.6 1.1 %copy-start = (f32[5,32,8,128]{3,2,1,0:T(8,128)S(1)}, f32[5,32,8,128]{3,2,1,0:T(8,128)}, u32[]{:S(2)}) copy-start(f32[5,32,8,128]{3,2,1,0:T(8,128)} %u.5) | copy-start | bytes 1966084
  1.7 0.9 %copy-start.2 = (f32[32,8,128]{2,1,0:T(8,128)S(1)}, f32[32,8,128]{2,1,0:T(8,128)}, u32[]{:S(2)}) copy-start(f32[32,8,128]{2,1,0:T(8,128)} %g.5) | copy-start | bytes 393220
  2.6 10.1 %copy-start.5 = (f32[4,3,256]{2,0,1:T(4,128)S(1)}, f32[4,3,256]{2,0,1:T(4,128)}, u32[]{:S(2)}) copy-start(f32[4,3,256]{2,0,1:T(4,128)} %param.8) | copy-start | bytes 36868
  2.6 10.1 %copy-start.6 = (f32[4,256]{1,0:T(4,128)S(1)}, f32[4,256]{1,0:T(4,128)}, u32[]{:S(2)}) copy-start(f32[4,256]{1,0:T(4,128)} %param.9) | copy-start | bytes 12292
  2.6 15.3 %copy-start.1 = (f32[5,32,8,128]{3,2,1,0:T(8,128)S(1)}, f32[5,32,8,128]{3,2,1,0:T(8,128)}, u32[]{:S(2)}) copy-start(f32[5,32,8,128]{3,2,1,0:T(8,128)} %u.5) | copy-start | bytes 1966084
  5.2 12.7 %copy-start.3 = (f32[32,8,128]{2,1,0:T(8,128)S(1)}, f32[32,8,128]{2,1,0:T(8,128)}, u32[]{:S(2)}) copy-start(f32[32,8,128]{2,1,0:T(8,128)} %g.5) | copy-start | bytes 393220
  5.2 11.7 %collective-permute-start.4 = (f32[6,8,128]{2,1,0:T(8,128)S(1)}, f32[6,8,128]{2,1,0:T(8,128)S(1)}, u32[]{:S(2)}, u32[]{:S(2)}) collective-permute-start(f32[6,8,128]{2,1,0:T(8,128)S(1)} %get-tuple-element.19), channel_id=1, source_target_pairs={{0,1},{1,2},{2,3},{3,0},{4,5},{5,6},{6,7},{7,4},{8,9},{9,10},{10,1... | collective-permute-start | bytes 73736 | tf_op jit(solution)/shard_map/ppermute | solution.py:317
  7.4 5.5 %collective-permute-start.5 = (f32[6,8,128]{2,1,0:T(8,128)S(1)}, f32[6,8,128]{2,1,0:T(8,128)S(1)}, u32[]{:S(2)}, u32[]{:S(2)}) collective-permute-start(f32[6,8,128]{2,1,0:T(8,128)S(1)} %get-tuple-element.19), channel_id=1, source_target_pairs={{0,3},{1,0},{2,1},{3,2},{4,7},{5,4},{6,5},{7,6},{8,11},{9,8},{10,9... | collective-permute-start | bytes 73736 | tf_op jit(solution)/shard_map/ppermute | solution.py:317
  8.9 9.0 %collective-permute-start.2 = (f32[6,32,128]{2,1,0:T(8,128)S(1)}, f32[6,32,128]{2,1,0:T(8,128)S(1)}, u32[]{:S(2)}, u32[]{:S(2)}) collective-permute-start(f32[6,32,128]{2,1,0:T(8,128)S(1)} %get-tuple-element.17), channel_id=1, source_target_pairs={{0,4},{4,8},{8,12},{12,16},{16,20},{20,24},{24,28},{28,0},{1,5},{5... | collective-permute-start | bytes 294920 | tf_op jit(solution)/shard_map/ppermute | solution.py:317
  11.1 6.8 %collective-permute-start.3 = (f32[6,32,128]{2,1,0:T(8,128)S(1)}, f32[6,32,128]{2,1,0:T(8,128)S(1)}, u32[]{:S(2)}, u32[]{:S(2)}) collective-permute-start(f32[6,32,128]{2,1,0:T(8,128)S(1)} %get-tuple-element.18), channel_id=1, source_target_pairs={{0,28},{4,0},{8,4},{12,8},{16,12},{20,16},{24,20},{28,24},{1,29},{... | collective-permute-start | bytes 294920 | tf_op jit(solution)/shard_map/ppermute | solution.py:317
  11.8 6.1 %collective-permute-start = (f32[6,8,128]{2,1,0:T(8,128)S(1)}, f32[6,8,128]{2,1,0:T(8,128)S(1)}, u32[]{:S(2)}, u32[]{:S(2)}) collective-permute-start(f32[6,8,128]{2,1,0:T(8,128)S(1)} %get-tuple-element.15), channel_id=1, source_target_pairs={{0,32},{32,64},{64,96},{96,128},{128,160},{160,192},{192,224},{224... | collective-permute-start | bytes 73736 | tf_op jit(solution)/shard_map/ppermute | solution.py:317
  12.9 5.0 %collective-permute-start.1 = (f32[6,8,128]{2,1,0:T(8,128)S(1)}, f32[6,8,128]{2,1,0:T(8,128)S(1)}, u32[]{:S(2)}, u32[]{:S(2)}) collective-permute-start(f32[6,8,128]{2,1,0:T(8,128)S(1)} %get-tuple-element.16), channel_id=1, source_target_pairs={{0,224},{32,0},{64,32},{96,64},{128,96},{160,128},{192,160},{224,1... | collective-permute-start | bytes 73736 | tf_op jit(solution)/shard_map/ppermute | solution.py:317
  17.9 13.7 %copy-start.4 = (s32[32,8,128]{2,1,0:T(8,128)S(1)}, s32[32,8,128]{2,1,0:T(8,128)}, u32[]{:S(2)}) copy-start(s32[32,8,128]{2,1,0:T(8,128)} %sp.1) | copy-start | bytes 393220
  21.0 6.0 %collective-permute-start.10 = (f32[5,8,128]{2,1,0:T(8,128)S(1)}, f32[5,8,128]{2,1,0:T(8,128)S(1)}, u32[]{:S(2)}, u32[]{:S(2)}) collective-permute-start(f32[5,8,128]{2,1,0:T(8,128)S(1)} %get-tuple-element.25), channel_id=1, source_target_pairs={{0,1},{1,2},{2,3},{3,0},{4,5},{5,6},{6,7},{7,4},{8,9},{9,10},{10,1... | collective-permute-start | bytes 61448 | tf_op jit(solution)/shard_map/ppermute | solution.py:317
  21.1 9.2 %collective-permute-start.11 = (f32[5,8,128]{2,1,0:T(8,128)S(1)}, f32[5,8,128]{2,1,0:T(8,128)S(1)}, u32[]{:S(2)}, u32[]{:S(2)}) collective-permute-start(f32[5,8,128]{2,1,0:T(8,128)S(1)} %get-tuple-element.25), channel_id=1, source_target_pairs={{0,3},{1,0},{2,1},{3,2},{4,7},{5,4},{6,5},{7,6},{8,11},{9,8},{10,9... | collective-permute-start | bytes 61448 | tf_op jit(solution)/shard_map/ppermute | solution.py:317
  23.7 8.0 %collective-permute-start.8 = (f32[5,32,128]{2,1,0:T(8,128)S(1)}, f32[5,32,128]{2,1,0:T(8,128)S(1)}, u32[]{:S(2)}, u32[]{:S(2)}) collective-permute-start(f32[5,32,128]{2,1,0:T(8,128)S(1)} %get-tuple-element.23), channel_id=1, source_target_pairs={{0,4},{4,8},{8,12},{12,16},{16,20},{20,24},{24,28},{28,0},{1,5},{5... | collective-permute-start | bytes 245768 | tf_op jit(solution)/shard_map/ppermute | solution.py:317
  27.0 4.7 %collective-permute-start.9 = (f32[5,32,128]{2,1,0:T(8,128)S(1)}, f32[5,32,128]{2,1,0:T(8,128)S(1)}, u32[]{:S(2)}, u32[]{:S(2)}) collective-permute-start(f32[5,32,128]{2,1,0:T(8,128)S(1)} %get-tuple-element.24), channel_id=1, source_target_pairs={{0,28},{4,0},{8,4},{12,8},{16,12},{20,16},{24,20},{28,24},{1,29},{... | collective-permute-start | bytes 245768 | tf_op jit(solution)/shard_map/ppermute | solution.py:317
  27.0 4.6 %collective-permute-start.6 = (f32[5,8,128]{2,1,0:T(8,128)S(1)}, f32[5,8,128]{2,1,0:T(8,128)S(1)}, u32[]{:S(2)}, u32[]{:S(2)}) collective-permute-start(f32[5,8,128]{2,1,0:T(8,128)S(1)} %get-tuple-element.21), channel_id=1, source_target_pairs={{0,32},{32,64},{64,96},{96,128},{128,160},{160,192},{192,224},{224... | collective-permute-start | bytes 61448 | tf_op jit(solution)/shard_map/ppermute | solution.py:317
  27.0 4.6 %collective-permute-start.7 = (f32[5,8,128]{2,1,0:T(8,128)S(1)}, f32[5,8,128]{2,1,0:T(8,128)S(1)}, u32[]{:S(2)}, u32[]{:S(2)}) collective-permute-start(f32[5,8,128]{2,1,0:T(8,128)S(1)} %get-tuple-element.22), channel_id=1, source_target_pairs={{0,224},{32,0},{64,32},{96,64},{128,96},{160,128},{192,160},{224,1... | collective-permute-start | bytes 61448 | tf_op jit(solution)/shard_map/ppermute | solution.py:317
  38.4 3.5 %collective-permute-start.12 = (f32[1,128]{1,0:T(1,128)S(1)}, f32[1,128]{1,0:T(1,128)S(1)}, u32[]{:S(2)}, u32[]{:S(2)}) collective-permute-start(f32[1,128]{1,0:T(1,128)S(1)} %slice.42), channel_id=1, source_target_pairs={{0,224},{32,0},{64,32},{96,64},{128,96},{160,128},{192,160},{224,1... | collective-permute-start | bytes 1544 | tf_op jit(solution)/shard_map/ppermute | solution.py:317
  42.6 15.0 %all-to-all-start = ((f32[32,1,128]{2,1,0:T(1,128)}), f32[32,1,128]{2,1,0:T(1,128)S(1)}, u32[]{:S(2)}, u32[]{:S(2)}) async-start(f32[32,1,128]{2,1,0:T(1,128)} %bitcast.10), calls=%async_computation | async-start | bytes 32768 | tf_op jit(solution)/shard_map/all_to_all | solution.py:400

commit v2 on v1

--- a/solution.py
+++ b/solution.py
@@ -99,7 +99,7 @@
         return [a - b for a, b in zip(core, down)], x_down
 
     carry = step(0, (None, down_before), False)
-    carry = lax.fori_loop(1, rows, lambda row, c: step(row, c, True), carry)
+    carry = lax.fori_loop(1, rows, lambda row, c: step(row, c, True), carry, unroll=True)
     finish(rows - 1, [a + b for a, b in zip(carry[0], up_after)])
 
 
@@ -122,7 +122,7 @@
             put_faces(f, row, rows, u[f, row] if f < 5 else g[row], y_low, y_high, z_pack)
         return 0
 
-    lax.fori_loop(0, rows, body, 0)
+    lax.fori_loop(0, rows, body, 0, unroll=True)
 
 
 def half_kernel(

time: 59.2 us -> 52.5 us (0.89)
  Pallas kernels: 13.7 us -> 6.88 us
    pallas_call x1, Pallas kernels: 6.7 us -> 3.83 us  [local(): pl.pallas_call(step_kernel, out_shape=(struct(*conserved.shape), struct(r...]
    pallas_call x1, Pallas kernels: 2.59 us -> 0.31 us  [local(): pl.pallas_call(pack_kernel, out_shape=faces(6, rows), compiler_params=par...]
    pallas_call x1, Pallas kernels: 3.03 us -> 1.39 us  [local(): pl.pallas_call(half_kernel, out_shape=(struct(*conserved.shape),) + faces...]
where the time goes in v2:
time: 52.5 us; the launch traced here: 52.3 us
  starting transfers between devices  31.9 us (61%)
  waiting for transfers between devices  9.85 us (19%)
  Pallas kernels  6.88 us (13%)
  local copies, waits for them, and re-layouts  2.13 us (4%)
  between operations  0.78 us (1%)
  other arithmetic  0.76 us (1%)
    ppermute x13, starting transfers between devices, shifted(): lax.ppermute(value, axis, [(i, (i + steps) % size) for i in range(size)])  23.8 us
    all_to_all x1, starting transfers between devices, local(): lax.all_to_all(grouped.reshape(across_y * across_z, 1, LANES), ('gy', 'gz...  8.08 us
    all_to_all x1, waiting for transfers between devices, local(): lax.all_to_all(grouped.reshape(across_y * across_z, 1, LANES), ('gy', 'gz...  6.92 us
    pallas_call x1, Pallas kernels, local(): pl.pallas_call(step_kernel, out_shape=(struct(*conserved.shape), struct(r...  3.83 us
    ppermute x13, waiting for transfers between devices, shifted(): lax.ppermute(value, axis, [(i, (i + steps) % size) for i in range(size)])  2.93 us
    unnamed x14, local copies, waits for them, and re-layouts  2.01 us
    pallas_call x1, Pallas kernels, local(): pl.pallas_call(half_kernel, out_shape=(struct(*conserved.shape),) + faces...  1.39 us
    pallas_call x1, Pallas kernels, local(): pl.pallas_call(functools.partial(image_kernel, across_y, across_z), out_s...  1.34 us
  transfers between devices with their start and end apart: 14, of which 4 were waited for; matrix products, arithmetic and copies ran while one was open for 0% of the time, Pallas kernels for 0%

profile of v2, /device:TPU:1, one launch (start us, length us, event | category | flops | bytes accessed | tf_op | source)
XLA Modules:
  0.0 52.3 jit_solution(14252060239192219381)
XLA Ops:
  0.6 1.1 %copy-done = f32[5,32,8,128]{3,2,1,0:T(8,128)S(1)} copy-done((f32[5,32,8,128]{3,2,1,0:T(8,128)S(1)}, f32[5,32,8,128]{3,2,1,0:T(8,128)}, u32[]{:S(2)}) %copy-start) | copy-done | bytes 655384
  1.7 0.9 %copy-done.2 = f32[32,8,128]{2,1,0:T(8,128)S(1)} copy-done((f32[32,8,128]{2,1,0:T(8,128)S(1)}, f32[32,8,128]{2,1,0:T(8,128)}, u32[]{:S(2)}) %copy-start.2) | copy-done | bytes 131096
  2.6 0.3 pack.1
  3.0 2.2 %collective-permute-start.4 = (f32[6,8,128]{2,1,0:T(8,128)S(1)}, f32[6,8,128]{2,1,0:T(8,128)S(1)}, u32[]{:S(2)}, u32[]{:S(2)}) collective-permute-start(f32[6,8,128]{2,1,0:T(8,128)S(1)} %get-tuple-element.19), channel_id=1, source_target_pairs={{0,1},{1,2},{2,3},{3,0},{4,5},{5,6},{6,7},{7,4},{8,9},{9,10},{10,1... | collective-permute-start | bytes 73736 | tf_op jit(solution)/shard_map/ppermute | solution.py:317
  5.2 1.5 %collective-permute-start.5 = (f32[6,8,128]{2,1,0:T(8,128)S(1)}, f32[6,8,128]{2,1,0:T(8,128)S(1)}, u32[]{:S(2)}, u32[]{:S(2)}) collective-permute-start(f32[6,8,128]{2,1,0:T(8,128)S(1)} %get-tuple-element.19), channel_id=1, source_target_pairs={{0,3},{1,0},{2,1},{3,2},{4,7},{5,4},{6,5},{7,6},{8,11},{9,8},{10,9... | collective-permute-start | bytes 73736 | tf_op jit(solution)/shard_map/ppermute | solution.py:317
  6.7 2.2 %collective-permute-start.2 = (f32[6,32,128]{2,1,0:T(8,128)S(1)}, f32[6,32,128]{2,1,0:T(8,128)S(1)}, u32[]{:S(2)}, u32[]{:S(2)}) collective-permute-start(f32[6,32,128]{2,1,0:T(8,128)S(1)} %get-tuple-element.17), channel_id=1, source_target_pairs={{0,4},{4,8},{8,12},{12,16},{16,20},{20,24},{24,28},{28,0},{1,5},{5... | collective-permute-start | bytes 294920 | tf_op jit(solution)/shard_map/ppermute | solution.py:317
  8.9 0.6 %collective-permute-start.3 = (f32[6,32,128]{2,1,0:T(8,128)S(1)}, f32[6,32,128]{2,1,0:T(8,128)S(1)}, u32[]{:S(2)}, u32[]{:S(2)}) collective-permute-start(f32[6,32,128]{2,1,0:T(8,128)S(1)} %get-tuple-element.18), channel_id=1, source_target_pairs={{0,28},{4,0},{8,4},{12,8},{16,12},{20,16},{24,20},{28,24},{1,29},{... | collective-permute-start | bytes 294920 | tf_op jit(solution)/shard_map/ppermute | solution.py:317
  9.5 1.0 %collective-permute-start = (f32[6,8,128]{2,1,0:T(8,128)S(1)}, f32[6,8,128]{2,1,0:T(8,128)S(1)}, u32[]{:S(2)}, u32[]{:S(2)}) collective-permute-start(f32[6,8,128]{2,1,0:T(8,128)S(1)} %get-tuple-element.15), channel_id=1, source_target_pairs={{0,32},{32,64},{64,96},{96,128},{128,160},{160,192},{192,224},{224... | collective-permute-start | bytes 73736 | tf_op jit(solution)/shard_map/ppermute | solution.py:317
  10.7 4.0 %collective-permute-start.1 = (f32[6,8,128]{2,1,0:T(8,128)S(1)}, f32[6,8,128]{2,1,0:T(8,128)S(1)}, u32[]{:S(2)}, u32[]{:S(2)}) collective-permute-start(f32[6,8,128]{2,1,0:T(8,128)S(1)} %get-tuple-element.16), channel_id=1, source_target_pairs={{0,224},{32,0},{64,32},{96,64},{128,96},{160,128},{192,160},{224,1... | collective-permute-start | bytes 73736 | tf_op jit(solution)/shard_map/ppermute | solution.py:317
  14.7 0.9 %collective-permute-done.1.xp = f32[6,8,128]{2,1,0:T(8,128)S(1)} collective-permute-done((f32[6,8,128]{2,1,0:T(8,128)S(1)}, f32[6,8,128]{2,1,0:T(8,128)S(1)}, u32[]{:S(2)}, u32[]{:S(2)}) %collective-permute-start.1) | collective-permute-done | bytes 24608 | tf_op jit(solution)/shard_map/ppermute | solution.py:317
  15.7 1.4 %half.1 = (f32[5,32,8,128]{3,2,1,0:T(8,128)S(1)}, f32[5,8,128]{2,1,0:T(8,128)S(1)}, f32[5,8,128]{2,1,0:T(8,128)S(1)}, f32[5,32,128]{2,1,0:T(8,128)S(1)}, f32[5,3...) custom-call(f32[5,32,8,128]{3,2,1,0:T(8,128)S(1)} %copy-done.1, f32[32,8,128]{2,1,0:T(8,128)S(1)} %copy-done.3, ...), custom_call_target="tpu_custom_call" | custom-call | tf_op jit(solution)/shard_map/half/pallas_call | solution.py:367
  17.1 0.2 collective-permute-start.10
  17.3 2.5 %collective-permute-start.11 = (f32[5,8,128]{2,1,0:T(8,128)S(1)}, f32[5,8,128]{2,1,0:T(8,128)S(1)}, u32[]{:S(2)}, u32[]{:S(2)}) collective-permute-start(f32[5,8,128]{2,1,0:T(8,128)S(1)} %get-tuple-element.25), channel_id=1, source_target_pairs={{0,3},{1,0},{2,1},{3,2},{4,7},{5,4},{6,5},{7,6},{8,11},{9,8},{10,9... | collective-permute-start | bytes 61448 | tf_op jit(solution)/shard_map/ppermute | solution.py:317
  19.9 3.3 %collective-permute-start.8 = (f32[5,32,128]{2,1,0:T(8,128)S(1)}, f32[5,32,128]{2,1,0:T(8,128)S(1)}, u32[]{:S(2)}, u32[]{:S(2)}) collective-permute-start(f32[5,32,128]{2,1,0:T(8,128)S(1)} %get-tuple-element.23), channel_id=1, source_target_pairs={{0,4},{4,8},{8,12},{12,16},{16,20},{20,24},{24,28},{28,0},{1,5},{5... | collective-permute-start | bytes 245768 | tf_op jit(solution)/shard_map/ppermute | solution.py:317
  23.2 3.3 %collective-permute-start.7 = (f32[5,8,128]{2,1,0:T(8,128)S(1)}, f32[5,8,128]{2,1,0:T(8,128)S(1)}, u32[]{:S(2)}, u32[]{:S(2)}) collective-permute-start(f32[5,8,128]{2,1,0:T(8,128)S(1)} %get-tuple-element.22), channel_id=1, source_target_pairs={{0,224},{32,0},{64,32},{96,64},{128,96},{160,128},{192,160},{224,1... | collective-permute-start | bytes 61448 | tf_op jit(solution)/shard_map/ppermute | solution.py:317
  26.5 1.3 %collective-permute-done.6.xm = f32[5,8,128]{2,1,0:T(8,128)S(1)} collective-permute-done((f32[5,8,128]{2,1,0:T(8,128)S(1)}, f32[5,8,128]{2,1,0:T(8,128)S(1)}, u32[]{:S(2)}, u32[]{:S(2)}) %collective-permute-start.6) | collective-permute-done | bytes 20512 | tf_op jit(solution)/shard_map/ppermute | solution.py:317
  27.8 3.8 %step.1 = (f32[5,32,8,128]{3,2,1,0:T(8,128)}, f32[32,128]{1,0:T(8,128)S(1)}) custom-call(f32[5,32,8,128]{3,2,1,0:T(8,128)S(1)} %copy-done.1, f32[32,8,128]{2,1,0:T(8,128)S(1)} %copy-done.3, s32[32,8,128]{2,1,0:T(8,128)S(1)} %copy-done.4, f32[5,32,8,128]{3,2,1,0:T(8,128)S(1)} %get-tuple-element.20.h, f32[8,128]{1,0:T(8,128)S(1)} %slice_bitcast_fusion.5.gxm, ...), custom_call_target="tpu_custom_call" | custom-call | tf_op jit(solution)/shard_map/step/pallas_call | solution.py:375
  31.7 2.8 %collective-permute-start.12 = (f32[1,128]{1,0:T(1,128)S(1)}, f32[1,128]{1,0:T(1,128)S(1)}, u32[]{:S(2)}, u32[]{:S(2)}) collective-permute-start(f32[1,128]{1,0:T(1,128)S(1)} %slice.42), channel_id=1, source_target_pairs={{0,224},{32,0},{64,32},{96,64},{128,96},{160,128},{192,160},{224,1... | collective-permute-start | bytes 1544 | tf_op jit(solution)/shard_map/ppermute | solution.py:317
  34.5 0.1 pad.7.clone
  34.6 0.6 %collective-permute-done.12 = f32[1,128]{1,0:T(1,128)S(1)} collective-permute-done((f32[1,128]{1,0:T(1,128)S(1)}, f32[1,128]{1,0:T(1,128)S(1)}, u32[]{:S(2)}, u32[]{:S(2)}) %collective-permute-start.12) | collective-permute-done | bytes 544 | tf_op jit(solution)/shard_map/ppermute | solution.py:317
  35.2 0.7 %fusion.3 = f32[32,128]{1,0:T(8,128)} fusion(f32[1,128]{1,0:T(1,128)S(1)} %collective-permute-done.12, f32[31,128]{1,0:T(8,128)S(1)} %slice.41, f32[32,32]{1,0:T(8,128)S(1)} %bitcast.22, f32[128]{0:T(128)S(1)} %pad.7.clone), kind=kLoop, calls=%fused_computation.9 | loop fusion | flops 32768 | bytes 37376 | tf_op jit(solution)/shard_map/concatenate | solution.py:397
  35.9 8.1 %all-to-all-start = ((f32[32,1,128]{2,1,0:T(1,128)}), f32[32,1,128]{2,1,0:T(1,128)S(1)}, u32[]{:S(2)}, u32[]{:S(2)}) async-start(f32[32,1,128]{2,1,0:T(1,128)} %bitcast.10), calls=%async_computation | async-start | bytes 32768 | tf_op jit(solution)/shard_map/all_to_all | solution.py:400
  44.0 6.9 %all-to-all-done = f32[32,1,128]{2,1,0:T(1,128)S(1)} async-done(((f32[32,1,128]{2,1,0:T(1,128)}), f32[32,1,128]{2,1,0:T(1,128)S(1)}, u32[]{:S(2)}, u32[]{:S(2)}) %all-to-all-start) | async-done | bytes 16416 | tf_op jit(solution)/shard_map/all_to_all | solution.py:400
  50.9 1.3 %image.1 = f32[4,4,1920]{2,1,0:T(4,128)} custom-call(f32[1]{0:T(128)} %bitcast.9.flags, f32[32,128]{1,0:T(8,128)S(1)} %bitcast.21), custom_call_target="tpu_custom_call" | custom-call | tf_op jit(solution)/shard_map/image/pallas_call | solution.py:406
  (38 shorter events, 0.2 us)
Async XLA Ops:
  0.6 1.1 %copy-start = (f32[5,32,8,128]{3,2,1,0:T(8,128)S(1)}, f32[5,32,8,128]{3,2,1,0:T(8,128)}, u32[]{:S(2)}) copy-start(f32[5,32,8,128]{3,2,1,0:T(8,128)} %u.5) | copy-start | bytes 1966084
  1.7 0.9 %copy-start.2 = (f32[32,8,128]{2,1,0:T(8,128)S(1)}, f32[32,8,128]{2,1,0:T(8,128)}, u32[]{:S(2)}) copy-start(f32[32,8,128]{2,1,0:T(8,128)} %g.5) | copy-start | bytes 393220
  2.6 7.9 %copy-start.5 = (f32[4,3,256]{2,0,1:T(4,128)S(1)}, f32[4,3,256]{2,0,1:T(4,128)}, u32[]{:S(2)}) copy-start(f32[4,3,256]{2,0,1:T(4,128)} %param.8) | copy-start | bytes 36868
  2.6 7.9 %copy-start.6 = (f32[4,256]{1,0:T(4,128)S(1)}, f32[4,256]{1,0:T(4,128)}, u32[]{:S(2)}) copy-start(f32[4,256]{1,0:T(4,128)} %param.9) | copy-start | bytes 12292
  2.6 13.1 %copy-start.1 = (f32[5,32,8,128]{3,2,1,0:T(8,128)S(1)}, f32[5,32,8,128]{3,2,1,0:T(8,128)}, u32[]{:S(2)}) copy-start(f32[5,32,8,128]{3,2,1,0:T(8,128)} %u.5) | copy-start | bytes 1966084
  2.9 12.7 %copy-start.3 = (f32[32,8,128]{2,1,0:T(8,128)S(1)}, f32[32,8,128]{2,1,0:T(8,128)}, u32[]{:S(2)}) copy-start(f32[32,8,128]{2,1,0:T(8,128)} %g.5) | copy-start | bytes 393220
  3.0 11.7 %collective-permute-start.4 = (f32[6,8,128]{2,1,0:T(8,128)S(1)}, f32[6,8,128]{2,1,0:T(8,128)S(1)}, u32[]{:S(2)}, u32[]{:S(2)}) collective-permute-start(f32[6,8,128]{2,1,0:T(8,128)S(1)} %get-tuple-element.19), channel_id=1, source_target_pairs={{0,1},{1,2},{2,3},{3,0},{4,5},{5,6},{6,7},{7,4},{8,9},{9,10},{10,1... | collective-permute-start | bytes 73736 | tf_op jit(solution)/shard_map/ppermute | solution.py:317
  5.2 5.5 %collective-permute-start.5 = (f32[6,8,128]{2,1,0:T(8,128)S(1)}, f32[6,8,128]{2,1,0:T(8,128)S(1)}, u32[]{:S(2)}, u32[]{:S(2)}) collective-permute-start(f32[6,8,128]{2,1,0:T(8,128)S(1)} %get-tuple-element.19), channel_id=1, source_target_pairs={{0,3},{1,0},{2,1},{3,2},{4,7},{5,4},{6,5},{7,6},{8,11},{9,8},{10,9... | collective-permute-start | bytes 73736 | tf_op jit(solution)/shard_map/ppermute | solution.py:317
  6.7 9.0 %collective-permute-start.2 = (f32[6,32,128]{2,1,0:T(8,128)S(1)}, f32[6,32,128]{2,1,0:T(8,128)S(1)}, u32[]{:S(2)}, u32[]{:S(2)}) collective-permute-start(f32[6,32,128]{2,1,0:T(8,128)S(1)} %get-tuple-element.17), channel_id=1, source_target_pairs={{0,4},{4,8},{8,12},{12,16},{16,20},{20,24},{24,28},{28,0},{1,5},{5... | collective-permute-start | bytes 294920 | tf_op jit(solution)/shard_map/ppermute | solution.py:317
  8.9 6.8 %collective-permute-start.3 = (f32[6,32,128]{2,1,0:T(8,128)S(1)}, f32[6,32,128]{2,1,0:T(8,128)S(1)}, u32[]{:S(2)}, u32[]{:S(2)}) collective-permute-start(f32[6,32,128]{2,1,0:T(8,128)S(1)} %get-tuple-element.18), channel_id=1, source_target_pairs={{0,28},{4,0},{8,4},{12,8},{16,12},{20,16},{24,20},{28,24},{1,29},{... | collective-permute-start | bytes 294920 | tf_op jit(solution)/shard_map/ppermute | solution.py:317
  9.5 6.2 %collective-permute-start = (f32[6,8,128]{2,1,0:T(8,128)S(1)}, f32[6,8,128]{2,1,0:T(8,128)S(1)}, u32[]{:S(2)}, u32[]{:S(2)}) collective-permute-start(f32[6,8,128]{2,1,0:T(8,128)S(1)} %get-tuple-element.15), channel_id=1, source_target_pairs={{0,32},{32,64},{64,96},{96,128},{128,160},{160,192},{192,224},{224... | collective-permute-start | bytes 73736 | tf_op jit(solution)/shard_map/ppermute | solution.py:317
  10.7 5.0 %collective-permute-start.1 = (f32[6,8,128]{2,1,0:T(8,128)S(1)}, f32[6,8,128]{2,1,0:T(8,128)S(1)}, u32[]{:S(2)}, u32[]{:S(2)}) collective-permute-start(f32[6,8,128]{2,1,0:T(8,128)S(1)} %get-tuple-element.16), channel_id=1, source_target_pairs={{0,224},{32,0},{64,32},{96,64},{128,96},{160,128},{192,160},{224,1... | collective-permute-start | bytes 73736 | tf_op jit(solution)/shard_map/ppermute | solution.py:317
  15.7 12.1 %copy-start.4 = (s32[32,8,128]{2,1,0:T(8,128)S(1)}, s32[32,8,128]{2,1,0:T(8,128)}, u32[]{:S(2)}) copy-start(s32[32,8,128]{2,1,0:T(8,128)} %sp.1) | copy-start | bytes 393220
  17.1 6.1 %collective-permute-start.10 = (f32[5,8,128]{2,1,0:T(8,128)S(1)}, f32[5,8,128]{2,1,0:T(8,128)S(1)}, u32[]{:S(2)}, u32[]{:S(2)}) collective-permute-start(f32[5,8,128]{2,1,0:T(8,128)S(1)} %get-tuple-element.25), channel_id=1, source_target_pairs={{0,1},{1,2},{2,3},{3,0},{4,5},{5,6},{6,7},{7,4},{8,9},{9,10},{10,1... | collective-permute-start | bytes 61448 | tf_op jit(solution)/shard_map/ppermute | solution.py:317
  17.3 9.2 %collective-permute-start.11 = (f32[5,8,128]{2,1,0:T(8,128)S(1)}, f32[5,8,128]{2,1,0:T(8,128)S(1)}, u32[]{:S(2)}, u32[]{:S(2)}) collective-permute-start(f32[5,8,128]{2,1,0:T(8,128)S(1)} %get-tuple-element.25), channel_id=1, source_target_pairs={{0,3},{1,0},{2,1},{3,2},{4,7},{5,4},{6,5},{7,6},{8,11},{9,8},{10,9... | collective-permute-start | bytes 61448 | tf_op jit(solution)/shard_map/ppermute | solution.py:317
  19.9 8.0 %collective-permute-start.8 = (f32[5,32,128]{2,1,0:T(8,128)S(1)}, f32[5,32,128]{2,1,0:T(8,128)S(1)}, u32[]{:S(2)}, u32[]{:S(2)}) collective-permute-start(f32[5,32,128]{2,1,0:T(8,128)S(1)} %get-tuple-element.23), channel_id=1, source_target_pairs={{0,4},{4,8},{8,12},{12,16},{16,20},{20,24},{24,28},{28,0},{1,5},{5... | collective-permute-start | bytes 245768 | tf_op jit(solution)/shard_map/ppermute | solution.py:317
  23.2 4.7 %collective-permute-start.9 = (f32[5,32,128]{2,1,0:T(8,128)S(1)}, f32[5,32,128]{2,1,0:T(8,128)S(1)}, u32[]{:S(2)}, u32[]{:S(2)}) collective-permute-start(f32[5,32,128]{2,1,0:T(8,128)S(1)} %get-tuple-element.24), channel_id=1, source_target_pairs={{0,28},{4,0},{8,4},{12,8},{16,12},{20,16},{24,20},{28,24},{1,29},{... | collective-permute-start | bytes 245768 | tf_op jit(solution)/shard_map/ppermute | solution.py:317
  23.2 4.6 %collective-permute-start.6 = (f32[5,8,128]{2,1,0:T(8,128)S(1)}, f32[5,8,128]{2,1,0:T(8,128)S(1)}, u32[]{:S(2)}, u32[]{:S(2)}) collective-permute-start(f32[5,8,128]{2,1,0:T(8,128)S(1)} %get-tuple-element.21), channel_id=1, source_target_pairs={{0,32},{32,64},{64,96},{96,128},{128,160},{160,192},{192,224},{224... | collective-permute-start | bytes 61448 | tf_op jit(solution)/shard_map/ppermute | solution.py:317
  23.2 4.6 %collective-permute-start.7 = (f32[5,8,128]{2,1,0:T(8,128)S(1)}, f32[5,8,128]{2,1,0:T(8,128)S(1)}, u32[]{:S(2)}, u32[]{:S(2)}) collective-permute-start(f32[5,8,128]{2,1,0:T(8,128)S(1)} %get-tuple-element.22), channel_id=1, source_target_pairs={{0,224},{32,0},{64,32},{96,64},{128,96},{160,128},{192,160},{224,1... | collective-permute-start | bytes 61448 | tf_op jit(solution)/shard_map/ppermute | solution.py:317
  31.7 3.5 %collective-permute-start.12 = (f32[1,128]{1,0:T(1,128)S(1)}, f32[1,128]{1,0:T(1,128)S(1)}, u32[]{:S(2)}, u32[]{:S(2)}) collective-permute-start(f32[1,128]{1,0:T(1,128)S(1)} %slice.42), channel_id=1, source_target_pairs={{0,224},{32,0},{64,32},{96,64},{128,96},{160,128},{192,160},{224,1... | collective-permute-start | bytes 1544 | tf_op jit(solution)/shard_map/ppermute | solution.py:317
  35.9 15.0 %all-to-all-start = ((f32[32,1,128]{2,1,0:T(1,128)}), f32[32,1,128]{2,1,0:T(1,128)S(1)}, u32[]{:S(2)}, u32[]{:S(2)}) async-start(f32[32,1,128]{2,1,0:T(1,128)} %bitcast.10), calls=%async_computation | async-start | bytes 32768 | tf_op jit(solution)/shard_map/all_to_all | solution.py:400

commit v3 on v2

v3 whole, which is shorter than its diff:
```python
import functools

import jax
import jax.numpy as jnp
from jax import lax
from jax.experimental import pallas as pl
from jax.experimental.pallas import tpu as pltpu
from jax.sharding import PartitionSpec as P

SW = 1920
ZOOM = 4
CLASSES = 4
LUT = 256

dissipation = 3.0
courant = 0.11
density_low = 0.6
density_high = 1.6

F32 = jnp.float32
LANES = 128
SUBS = 8
VMEM_LIMIT = 48 * 1024 * 1024


def iota(shape, dim):
    return lax.broadcasted_iota(jnp.int32, shape, dim)


def halves(direction, cell):
    density, m1, m2, m3, energy, gamma = cell
    momenta = (m1, m2, m3)
    inverse = 1.0 / density
    kinetic = 0.5 * (m1 * m1 + m2 * m2 + m3 * m3) * inverse
    pressure = (gamma - 1.0) * (energy - kinetic)
    half_p = 0.5 * pressure
    scaled = [(0.5 * dissipation) * q for q in (density, m1, m2, m3, energy)]
    result = []
    for d in direction:
        half_v = 0.5 * momenta[d] * inverse
        flux = [0.5 * momenta[d]]
        for member in range(3):
            component = momenta[member] * half_v
            flux.append(component + half_p if member == d else component)
        flux.append((energy + pressure) * half_v)
        result.append(
            ([a - b for a, b in zip(flux, scaled)], [a + b for a, b in zip(flux, scaled)])
        )
    return result


def up_of(direction, cell):
    return halves((direction,), cell)[0][0]


def down_of(direction, cell):
    return halves((direction,), cell)[0][1]


def total_change(cell, pairs):
    result = []
    for f in range(5):
        total = (6.0 * 0.5 * dissipation) * cell[f]
        for above, below in pairs:
            total = total + (above[f] - below[f])
        result.append(total)
    return result


def lanes():
    return iota((SUBS, LANES), 1)


def subs():
    return iota((SUBS, LANES), 0)


def along_y(up, down, below, above):
    from_above = [
        jnp.where(subs() == SUBS - 1, above[f], pltpu.roll(up[f], SUBS - 1, 0)) for f in range(5)
    ]
    from_below = [jnp.where(subs() == 0, below[f], pltpu.roll(down[f], 1, 0)) for f in range(5)]
    return from_above, from_below


def along_z(up, down, below, above):
    from_above = [
        jnp.where(lanes() == LANES - 1, above[f], pltpu.roll(up[f], LANES - 1, 1)) for f in range(5)
    ]
    from_below = [jnp.where(lanes() == 0, below[f], pltpu.roll(down[f], 1, 1)) for f in range(5)]
    return from_above, from_below


HALO = 2
ABOVE = 3
FIRST_AT = 33
STRIP_AT = 70
MESSAGE_ROWS = 72


def row_of(u, g, xm, xp, f, row):
    own = g.shape[0] // SUBS
    place = row - HALO
    if place < 0:
        return xm[f * HALO + row]
    if place >= own:
        return xp[f * ABOVE + place - own]
    span = pl.ds(place * SUBS, SUBS)
    return u[f, span, :] if f < 5 else g[span, :]


def strips(load, rows, parts):
    up, down, inner = parts
    for row in rows:
        value = load(row)
        here = lanes() // 2 == row
        up = jnp.where(here, pltpu.roll(value, 2 * row + 2, 1), up)
        down = jnp.where(here, pltpu.roll(value, 2 * row, 1) if row else value, down)
        inner = jnp.where(here, pltpu.roll(value, 2 * row + 1, 1), inner)
    return up, down, inner


def own_strips_kernel(u, g, *parts):
    own = g.shape[0] // SUBS
    for f in range(6):
        result = strips(
            lambda row: row_of(u, g, None, None, f, row),
            range(HALO, HALO + own),
            [jnp.ones((SUBS, LANES), F32)] * 3,
        )
        for part, value in zip(parts, result):
            part[f] = value


def all_strips_kernel(own, xm, xp, own_up, own_down, own_inner, *parts):
    for f in range(6):
        result = (own_up[f], own_down[f], own_inner[f])
        result = strips(lambda row: xm[f * HALO + row], range(HALO), result)
        result = strips(
            lambda row: xp[f * ABOVE + row - HALO - own],
            range(HALO + own, HALO + own + ABOVE),
            result,
        )
        for part, value in zip(parts, result):
            part[f] = value


def strips_of(zm, zp, f):
    odd = lanes() % 2 == 1
    first = jnp.where(odd, zm[f], zp[f])
    second = jnp.where(odd, pltpu.roll(zm[f], 1, 1), pltpu.roll(zp[f], LANES - 1, 1))
    return first, second


def y_kernel(u, g, xm, xp, zm, zp, y_low, y_high):
    own = g.shape[0] // SUBS
    every = own + HALO + ABOVE
    for f in range(6):
        first, _ = strips_of(zm, zp, f)
        for message, near, far in ((y_low, 0, 1), (y_high, SUBS - 1, SUBS - 2)):
            for at, sub, start, stop in (
                (0, far, HALO, HALO + own + 1),
                (FIRST_AT, near, 0, every),
            ):
                for row in range(start, stop):
                    if HALO <= row < HALO + own:
                        continue
                    line = row_of(u, g, xm, xp, f, row)[sub : sub + 1, :]
                    message[f, pl.ds(at + row - start, 1), :] = line
                span = pl.ds(sub, own, stride=SUBS)
                block = u[f, span, :] if f < 5 else g[span, :]
                message[f, pl.ds(at + HALO - start, own), :] = block
            message[f, pl.ds(STRIP_AT, 1), :] = first[near : near + 1, :]
            message[f, pl.ds(STRIP_AT + 1, 1), :] = first[near : near + 1, :]


def sweep(load, first, last, y_below, y_above, z_edge, finish):
    down = down_of(0, load(first - 1))
    pending = None
    for row in range(first, last + 1):
        cell = load(row)
        (x_up, x_down), (y_up, y_down), (z_up, z_down) = halves((0, 1, 2), cell)
        if pending is not None:
            finish(row - 1, [a + b for a, b in zip(pending, x_up)])
        edge = [pltpu.roll(z_edge[f], LANES - 1 - 2 * row, 1) for f in range(5)]
        below = [y_below[f, pl.ds(row, 1), :] for f in range(5)]
        above = [y_above[f, pl.ds(row, 1), :] for f in range(5)]
        core = total_change(
            cell,
            (along_y(y_up, y_down, below, above), along_z(z_up, z_down, edge, edge)),
        )
        pending = [a - b for a, b in zip(core, down)]
        down = x_down
    finish(last, [a + b for a, b in zip(pending, up_of(0, load(last + 1)))])


def lookup(density, species, tables):
    position = (density - density_low) * ((LUT - 1) / (density_high - density_low))
    knot = jnp.clip(jnp.floor(position), 0.0, LUT - 1.0)
    offset = position - knot
    lower_weight = jnp.maximum(0.0, 1.0 - jnp.abs(offset))
    upper_weight = jnp.maximum(0.0, 1.0 - jnp.abs(offset - 1.0))
    index = knot.astype(jnp.int32)
    lane_index = index % LANES
    bits = (index >= LANES, species % 2 == 1, species >= 2)
    result = []
    for channel in range(4):
        total = None
        for side, weight in ((0, lower_weight), (1, upper_weight)):
            values = [
                jnp.take_along_axis(
                    tables[channel, side, k], lane_index, axis=1, mode="promise_in_bounds"
                )
                for k in range(8)
            ]
            for bit in bits:
                values = [
                    jnp.where(bit, values[k + 1], values[k]) for k in range(0, len(values), 2)
                ]
            term = weight * values[0]
            total = term if total is None else total + term
        result.append(total)
    return result


def spread_tables(lut_lower, lut_upper, tables):
    for channel in range(4):
        for k in range(8):
            for side, source in ((0, lut_lower), (1, lut_upper)):
                row = source[pl.ds(channel * 8 + k, 1), :]
                tables[channel, side, k] = jnp.broadcast_to(row, (SUBS, LANES))


def split_dot(value, weights):
    first = value.astype(jnp.bfloat16)
    rest = value - first.astype(F32)
    second = rest.astype(jnp.bfloat16)
    third = (rest - second.astype(F32)).astype(jnp.bfloat16)
    total = jnp.dot(first, weights, preferred_element_type=F32)
    total += jnp.dot(second, weights, preferred_element_type=F32)
    return total + jnp.dot(third, weights, preferred_element_type=F32)


def integrate(properties, grouped, rows):
    extinction = properties[3]
    below = (iota((LANES, LANES), 0) < iota((LANES, LANES), 1)).astype(jnp.bfloat16)
    before = split_dot(extinction, below)
    factor = (1.0 - jnp.exp(-extinction)) * jnp.exp(-before)
    gathered = []
    for channel in range(4):
        if channel < 3:
            weighted = properties[channel] * factor
        else:
            weighted = extinction
        summed = jnp.sum(weighted, axis=1, keepdims=True)
        if channel == 3:
            summed = jnp.exp(-summed)
        plane = jnp.zeros((SUBS, LANES), F32)
        for row in range(rows):
            plane = jnp.where(lanes() == row, summed[row * SUBS : (row + 1) * SUBS], plane)
        gathered.append(plane)
    following = [pltpu.roll(plane, LANES - 1, 1) for plane in gathered]
    block = jnp.concatenate(
        gathered + following + [jnp.zeros((LANES - 8 * SUBS, LANES), F32)], axis=0
    )
    grouped[...] = jnp.transpose(block)[: rows - 1]


def classify(sp, xp, tables, properties, own):
    for place in range(own + 1):
        span = pl.ds(place * SUBS, SUBS)
        kind = sp[span, :] if place < own else xp[6 * ABOVE].astype(jnp.int32)
        found = lookup(properties[0, span, :], kind, tables)
        for channel in range(4):
            properties[channel, span, :] = found[channel]


def step_kernel(
    u, g, sp, xm, xp, zm, zp, z_inner, y_low, y_high, ym, yp, lut_lower, lut_upper,
    grouped, h, y_below2, y_above2, z_edge2, y_below, y_above, z_edge, turned, tables, properties
):
    own = g.shape[0] // SUBS
    spread_tables(lut_lower, lut_upper, tables)
    odd = lanes() % 2 == 1

    for start in (1, 9, 17, 25, 28):
        span = pl.ds(FIRST_AT + start, SUBS)
        below = down_of(1, [ym[f, span, :] for f in range(6)])
        above = up_of(1, [yp[f, span, :] for f in range(6)])
        for f in range(5):
            y_below[f, pl.ds(start, SUBS), :] = below[f]
            y_above[f, pl.ds(start, SUBS), :] = above[f]

    pairs = [strips_of(zm, zp, f) for f in range(6)]
    first = [pair[0] for pair in pairs]
    second = [pair[1] for pair in pairs]
    inner = [z_inner[f] for f in range(6)]
    corner = [
        jnp.where(
            subs() == 0,
            ym[f, pl.ds(STRIP_AT, 1), :],
            jnp.where(subs() == SUBS - 1, yp[f, pl.ds(STRIP_AT, 1), :], 1.0),
        )
        for f in range(6)
    ]
    (corner_up, corner_down), (corner_zup, corner_zdown) = halves((1, 2), corner)
    (x_up, x_down), (y_up, y_down), (z_up, z_down) = halves((0, 1, 2), first)
    for f in range(5):
        z_edge[f] = jnp.where(odd, z_down[f], z_up[f])
    from_above = up_of(2, [jnp.where(odd, a, b) for a, b in zip(inner, second)])
    from_below = down_of(2, [jnp.where(odd, a, b) for a, b in zip(second, inner)])
    change = total_change(
        first,
        (
            (
                [pltpu.roll(q, LANES - 2, 1) for q in x_up],
                [pltpu.roll(q, 2, 1) for q in x_down],
            ),
            along_y(y_up, y_down, corner_down, corner_up),
            (from_above, from_below),
        ),
    )
    halfway = [first[f] - courant * change[f] for f in range(5)] + [first[5]]
    up, down = halves((2,), halfway)[0]
    for f in range(5):
        z_edge2[f] = jnp.where(odd, down[f], up[f])

    ends = [jnp.where(odd, corner_zdown[f], corner_zup[f]) for f in range(5)]
    turned[...] = jnp.transpose(
        jnp.concatenate(ends + [jnp.zeros((LANES - 5 * SUBS, LANES), F32)], axis=0)
    )
    for start in (2, 10, 18, 26, 27):
        z_high_end = turned[pl.ds(2 * start, SUBS, stride=2), :]
        z_low_end = turned[pl.ds(2 * start + 1, SUBS, stride=2), :]
        for message, mine, lower in ((ym, y_low, True), (yp, y_high, False)):
            at = FIRST_AT + start
            cell = [message[f, pl.ds(at, SUBS), :] for f in range(6)]
            x_up = up_of(0, [message[f, pl.ds(at + 1, SUBS), :] for f in range(6)])
            x_down = down_of(0, [message[f, pl.ds(at - 1, SUBS), :] for f in range(6)])
            near = [mine[f, pl.ds(at, SUBS), :] for f in range(6)]
            far = [message[f, pl.ds(start - HALO, SUBS), :] for f in range(6)]
            above, below = (near, far) if lower else (far, near)
            z_up, z_down = halves((2,), cell)[0]
            shift = 0 if lower else SUBS - 1
            low_end = [
                pltpu.roll(z_low_end, (LANES - f * SUBS - shift) % LANES, 1)
                if f * SUBS + shift
                else z_low_end
                for f in range(5)
            ]
            high_end = [
                pltpu.roll(z_high_end, LANES - 1 - f * SUBS - shift, 1) for f in range(5)
            ]
            change = total_change(
                cell,
                (
                    (x_up, x_down),
                    (up_of(1, above), down_of(1, below)),
                    along_z(z_up, z_down, low_end, high_end),
                ),
            )
            halfway = [cell[f] - courant * change[f] for f in range(5)] + [cell[5]]
            part = down_of(1, halfway) if lower else up_of(1, halfway)
            target = y_below2 if lower else y_above2
            for f in range(5):
                target[f, pl.ds(start, SUBS), :] = part[f]

    def at_first(row):
        return [row_of(u, g, xm, xp, f, row) for f in range(6)]

    def store_half(row, change):
        for f in range(5):
            h[f, pl.ds(row * SUBS, SUBS), :] = (
                row_of(u, g, xm, xp, f, row) - courant * change[f]
            )

    sweep(at_first, 1, HALO + own + 1, y_below, y_above, z_edge, store_half)

    def finish(row, change):
        value = 0.5 * (
            row_of(u, g, xm, xp, 0, row) + h[0, pl.ds(row * SUBS, SUBS), :] - courant * change[0]
        )
        properties[0, pl.ds((row - HALO) * SUBS, SUBS), :] = value

    def at_half(row):
        return half_row(h, g, xm, xp, row)

    sweep(at_half, HALO, HALO + own, y_below2, y_above2, z_edge2, finish)
    classify(sp, xp, tables, properties, own)
    integrate(properties, grouped, own + 1)


def half_row(h, g, xm, xp, row):
    return [h[f, pl.ds(row * SUBS, SUBS), :] for f in range(5)] + [
        row_of(None, g, xm, xp, 5, row)
    ]


def state_kernel(u, g, xm, xp, h, y_below2, y_above2, z_edge2, new):
    own = g.shape[0] // SUBS

    def finish(row, change):
        for f in range(5):
            before = row_of(u, g, xm, xp, f, row)
            new[f, pl.ds((row - HALO) * SUBS, SUBS), :] = 0.5 * (
                before + h[f, pl.ds(row * SUBS, SUBS), :] - courant * change[f]
            )

    def at_half(row):
        return half_row(h, g, xm, xp, row)

    sweep(at_half, HALO, HALO + own - 1, y_below2, y_above2, z_edge2, finish)


def image_kernel(across_y, across_z, flags, parts, out):
    lane = iota((across_y, LANES), 1)
    channel = (lane // 8) % 4
    total = None
    for k in reversed(range(across_z)):
        part = parts[pl.ds(k, across_y, stride=across_z), :]
        through = part
        for c in range(3):
            moved = pltpu.roll(part, LANES - (24 - 8 * c), 1)
            through = jnp.where(channel == c, moved, through)
        if total is None:
            total = part
        else:
            total = jnp.where(channel == 3, 0.0, part) + through * total
    total = jnp.where(channel == 3, 1.0 - total, total)
    keep = jnp.where(lane >= 32, flags[0], 1.0)
    total = jnp.where(lane < 64, total * keep, 0.0)
    sub8 = iota((8, LANES), 0)
    lane8 = iota((8, LANES), 1)
    moved = jnp.zeros((8, LANES), F32)
    for k in range(across_y):
        wide = jnp.broadcast_to(total[k : k + 1, :], (8, LANES))
        shifted = wide
        for bit in range(3):
            amount = (LANES - (8 << bit)) % LANES
            shifted = jnp.where(
                (sub8 >> bit) & 1 == 1, pltpu.roll(shifted, amount, 1), shifted
            )
        if k:
            shifted = pltpu.roll(shifted, 8 * k, 1)
        moved = jnp.where(lane8 // 8 == k, shifted, moved)
    columns = 8 * across_y
    moved = jnp.where(lane8 < columns, moved, 0.0)
    screen = jnp.concatenate(
        [
            (1.0 - q / ZOOM) * moved[c : c + 1] + (q / ZOOM) * moved[4 + c : 5 + c]
            for c in range(4)
            for q in range(ZOOM)
        ],
        axis=0,
    )
    zoom = SW // columns
    for tile in range(SW // LANES):
        pixel = iota((8, LANES), 1) + tile * LANES
        source = pixel // zoom
        offset = pixel.astype(F32) * (columns / SW) - source.astype(F32)
        lower = jnp.maximum(0.0, 1.0 - jnp.abs(offset))
        upper = jnp.maximum(0.0, 1.0 - jnp.abs(offset - 1.0))
        for half in range(2):
            block = screen[8 * half : 8 * half + 8]
            value = lower * jnp.take_along_axis(
                block, source, axis=1, mode="promise_in_bounds"
            ) + upper * jnp.take_along_axis(
                block, source + 1, axis=1, mode="promise_in_bounds"
            )
            for c in range(2):
                out[2 * half + c, :, pl.ds(tile * LANES, LANES)] = value[4 * c : 4 * c + 4]


def shifted(value, axis, steps):
    size = lax.axis_size(axis)
    return lax.ppermute(value, axis, [(i, (i + steps) % size) for i in range(size)])


def cost(size):
    return pl.CostEstimate(flops=size, bytes_accessed=size, transcendentals=0)


def struct(*shape):
    return jax.ShapeDtypeStruct(shape, F32)


def local(conserved, gamma_field, species, lut_color, lut_extinction):
    rows = conserved.shape[1]
    cells = rows * SUBS
    params = pltpu.CompilerParams(vmem_limit_bytes=VMEM_LIMIT)
    across_y = lax.axis_size("gy")
    across_z = lax.axis_size("gz")

    lut_table = jnp.concatenate([lut_color, lut_extinction[:, None, :]], axis=1)
    lut_lower = lut_table.transpose(1, 0, 2).reshape(32, LANES)
    lut_upper = (
        jnp.pad(lut_table[:, :, 1:], ((0, 0), (0, 0), (0, 1))).transpose(1, 0, 2).reshape(32, LANES)
    )

    x_low = jnp.concatenate(
        [
            conserved[:, :ABOVE].reshape(5 * ABOVE, SUBS, LANES),
            gamma_field[:ABOVE],
            species[:1].astype(F32),
        ],
        axis=0,
    )
    x_high = jnp.concatenate(
        [conserved[:, rows - HALO :].reshape(5 * HALO, SUBS, LANES), gamma_field[rows - HALO :]],
        axis=0,
    )
    x_low, x_high = lax.optimization_barrier((x_low, x_high))
    xm = shifted(x_high, "gx", 1)
    xp = shifted(x_low, "gx", -1)
    brick = (
        conserved.reshape(5, cells, LANES),
        gamma_field.reshape(cells, LANES),
    )
    strip = struct(6, SUBS, LANES)
    own_parts = pl.pallas_call(
        own_strips_kernel,
        out_shape=(strip, strip, strip),
        compiler_params=params,
        cost_estimate=cost(2_000_000),
        name="own_strips",
    )(*brick)
    z_up, z_down, z_inner = pl.pallas_call(
        functools.partial(all_strips_kernel, rows),
        out_shape=(strip, strip, strip),
        compiler_params=params,
        name="strips",
    )(xm, xp, *own_parts)
    zm = shifted(z_up, "gz", 1)
    zp = shifted(z_down, "gz", -1)
    message = struct(6, MESSAGE_ROWS, LANES)
    y_low, y_high = pl.pallas_call(
        y_kernel, out_shape=(message, message), compiler_params=params, name="layers"
    )(*brick, xm, xp, zm, zp)
    ym = shifted(y_high, "gy", 1)
    yp = shifted(y_low, "gy", -1)
    layer = pltpu.VMEM((5, 40, LANES), F32)
    grouped, *halves_found = pl.pallas_call(
        step_kernel,
        out_shape=(
            struct(rows, LANES),
            struct(5, cells + (HALO + ABOVE) * SUBS, LANES),
            struct(5, 40, LANES),
            struct(5, 40, LANES),
            struct(5, SUBS, LANES),
        ),
        scratch_shapes=[
            layer,
            layer,
            pltpu.VMEM((5, SUBS, LANES), F32),
            pltpu.VMEM((LANES, LANES), F32),
            pltpu.VMEM((4, 2, 8, SUBS, LANES), F32),
            pltpu.VMEM((4, cells + SUBS, LANES), F32),
        ],
        compiler_params=params,
        name="density",
    )(
        *brick,
        species.reshape(cells, LANES),
        xm,
        xp,
        zm,
        zp,
        z_inner,
        y_low,
        y_high,
        ym,
        yp,
        lut_lower,
        lut_upper,
    )
    new_state = pl.pallas_call(
        state_kernel,
        out_shape=struct(5, cells, LANES),
        compiler_params=params,
        cost_estimate=cost(6_000_000),
        name="state",
    )(*brick, xm, xp, *halves_found)
    merged = lax.all_to_all(
        grouped.reshape(across_y * across_z, 1, LANES), ("gy", "gz"), 0, 0, tiled=True
    ).reshape(across_y * across_z, LANES)
    place = lax.axis_index(("gx", "gy", "gz"))
    last = lax.axis_size(("gx", "gy", "gz")) - 1
    flags = jnp.where(place == last, 0.0, 1.0).reshape(1)
    image = pl.pallas_call(
        functools.partial(image_kernel, across_y, across_z),
        out_shape=struct(4, ZOOM, SW),
        in_specs=[
            pl.BlockSpec(memory_space=pltpu.SMEM),
            pl.BlockSpec(memory_space=pltpu.VMEM),
        ],
        compiler_params=params,
        name="image",
    )(flags, merged)
    return new_state.reshape(conserved.shape), image


def solution(mesh):
    return jax.shard_map(
        local,
        mesh=mesh,
        in_specs=(P(None, "gx", "gy", "gz"), P("gx", "gy", "gz"), P("gx", "gy", "gz"), P(), P()),
        out_specs=(P(None, "gx", "gy", "gz"), P(None, ("gx", "gy", "gz"), None)),
        check_vma=False,
    )
```

time: 52.5 us -> 47.4 us (0.903)
  starting transfers between devices: 31.9 us -> 20.8 us
  waiting for transfers between devices: 9.85 us -> 13.9 us
  Pallas kernels: 6.88 us -> 9.01 us
  other arithmetic: 0.76 us -> 0.1 us
  local copies, waits for them, and re-layouts: 2.13 us -> 2.69 us
    ppermute x13 -> x6, starting transfers between devices: 23.8 us -> 14 us  [shifted(): lax.ppermute(value, axis, [(i, (i + steps) % size) for i in range(size)])]
    ppermute x13 -> x6, waiting for transfers between devices: 2.93 us -> 8.75 us  [shifted(): lax.ppermute(value, axis, [(i, (i + steps) % size) for i in range(size)])]
    pallas_call x3 -> x5, Pallas kernels: 5.53 us -> 7.77 us  [the longest x1 5.16 us: local(): pl.pallas_call(step_kernel, out_shape=(struct(rows, LANES), struct(5, cel...]
    all_to_all x1, waiting for transfers between devices: 6.92 us -> 5.14 us  [local(): lax.all_to_all(grouped.reshape(across_y * across_z, 1, LANES), ('gy', 'gz...]
    all_to_all x1, starting transfers between devices: 8.08 us -> 6.84 us  [local(): lax.all_to_all(grouped.reshape(across_y * across_z, 1, LANES), ('gy', 'gz...]
    slice x2 -> x8, local copies, waits for them, and re-layouts: 0.01 us -> 0.69 us  [the longest x2 0.67 us: local(): gamma_field[:ABOVE]]
    concatenate x1 -> x2, other arithmetic: 0.68 us -> 0.01 us  [the longest x1 0.01 us: local(): jnp.concatenate([conserved[:, :ABOVE].reshape(5 * ABOVE, SUBS, LANES), ga...]
    unnamed x14 -> x12, local copies, waits for them, and re-layouts: 2.01 us -> 1.97 us
  transfers between devices with their start and end apart: 14 -> 7, of which waited for: 4 -> 5; matrix products, arithmetic and copies ran while one was open for 0% -> 0% of each run, Pallas kernels for 0% -> 5%
where the time goes in v3:
time: 47.4 us; the launch traced here: 47.2 us
  starting transfers between devices  20.8 us (44%)
  waiting for transfers between devices  13.9 us (29%)
  Pallas kernels  9.01 us (19%)
  local copies, waits for them, and re-layouts  2.69 us (6%)
  between operations  0.77 us (2%)
    ppermute x6, starting transfers between devices, shifted(): lax.ppermute(value, axis, [(i, (i + steps) % size) for i in range(size)])  14 us
    ppermute x6, waiting for transfers between devices, shifted(): lax.ppermute(value, axis, [(i, (i + steps) % size) for i in range(size)])  8.75 us
    all_to_all x1, starting transfers between devices, local(): lax.all_to_all(grouped.reshape(across_y * across_z, 1, LANES), ('gy', 'gz...  6.84 us
    pallas_call x1, Pallas kernels, local(): pl.pallas_call(step_kernel, out_shape=(struct(rows, LANES), struct(5, cel...  5.16 us
    all_to_all x1, waiting for transfers between devices, local(): lax.all_to_all(grouped.reshape(across_y * across_z, 1, LANES), ('gy', 'gz...  5.14 us
    unnamed x12, local copies, waits for them, and re-layouts  1.97 us
    pallas_call x1, Pallas kernels, local(): pl.pallas_call(state_kernel, out_shape=struct(5, cells, LANES), compiler_...  1.7 us
    pallas_call x1, Pallas kernels, local(): pl.pallas_call(functools.partial(image_kernel, across_y, across_z), out_s...  1.24 us
  transfers between devices with their start and end apart: 7, of which 5 were waited for; matrix products, arithmetic and copies ran while one was open for 0% of the time, Pallas kernels for 5%

profile of v3, /device:TPU:1, one launch (start us, length us, event | category | flops | bytes accessed | tf_op | source)
XLA Modules:
  0.0 47.2 jit_solution(7350857328678578061)
XLA Ops:
  0.6 0.0 slice-start.1
  0.7 0.0 slice-start.3
  0.7 0.9 %copy-done.3 = s32[32,8,128]{2,1,0:T(8,128)S(1)} copy-done((s32[32,8,128]{2,1,0:T(8,128)S(1)}, s32[32,8,128]{2,1,0:T(8,128)}, u32[]{:S(2)}) %copy-start.3) | copy-done | bytes 131096
  1.6 0.7 %slice-done.2 = f32[3,8,128]{2,1,0:T(8,128)S(1)} async-done(((f32[32,8,128]{2,1,0:T(8,128)}), f32[3,8,128]{2,1,0:T(8,128)S(1)}, s32[]{:S(2)}) %slice-start.2) | async-done | bytes 12312 | tf_op jit(solution)/shard_map/slice | solution.py:503
  2.3 6.4 %collective-permute-start.1 = (f32[19,8,128]{2,1,0:T(8,128)S(1)}, f32[19,8,128]{2,1,0:T(8,128)S(1)}, u32[]{:S(2)}, u32[]{:S(2)}) collective-permute-start(f32[19,8,128]{2,1,0:T(8,128)S(1)} %pad_maximum_fusion), channel_id=1, source_target_pairs={{0,224},{32,0},{64,32},{96,64},{128,96},{160,128},{192,160},{224,1... | collective-permute-start | bytes 233480 | tf_op jit(solution)/shard_map/ppermute | solution.py:476
  8.7 1.1 %copy-done = f32[5,32,8,128]{3,2,1,0:T(8,128)S(1)} copy-done((f32[5,32,8,128]{3,2,1,0:T(8,128)S(1)}, f32[5,32,8,128]{3,2,1,0:T(8,128)}, u32[]{:S(2)}) %copy-start) | copy-done | bytes 655384
  9.8 0.7 %own_strips.1 = (f32[6,8,128]{2,1,0:T(8,128)S(1)}, f32[6,8,128]{2,1,0:T(8,128)S(1)}, f32[6,8,128]{2,1,0:T(8,128)S(1)}) custom-call(f32[5,256,128]{2,1,0:T(8,128)S(1)} %bitcast.16, f32[256,128]{1,0:T(8,128)S(1)} %bitcast.22), custom_call_target="tpu_custom_call" | custom-call | flops 2000000 | bytes 2000000 | tf_op jit(solution)/shard_map/own_strips/pallas_call | solution.py:520
  10.4 2.4 %collective-permute-done.xm = f32[12,8,128]{2,1,0:T(8,128)S(1)} collective-permute-done((f32[12,8,128]{2,1,0:T(8,128)S(1)}, f32[12,8,128]{2,1,0:T(8,128)S(1)}, u32[]{:S(2)}, u32[]{:S(2)}) %collective-permute-start) | collective-permute-done | bytes 49184 | tf_op jit(solution)/shard_map/ppermute | solution.py:476
  12.8 0.1 strips.1
  13.0 0.0 copy-start.5
  13.0 1.4 %collective-permute-start.2 = (f32[6,8,128]{2,1,0:T(8,128)S(1)}, f32[6,8,128]{2,1,0:T(8,128)S(1)}, u32[]{:S(2)}, u32[]{:S(2)}) collective-permute-start(f32[6,8,128]{2,1,0:T(8,128)S(1)} %get-tuple-element.22), channel_id=1, source_target_pairs={{0,1},{1,2},{2,3},{3,0},{4,5},{5,6},{6,7},{7,4},{8,9},{9,10},{10,1... | collective-permute-start | bytes 73736 | tf_op jit(solution)/shard_map/ppermute | solution.py:476
  14.4 1.5 %collective-permute-start.3 = (f32[6,8,128]{2,1,0:T(8,128)S(1)}, f32[6,8,128]{2,1,0:T(8,128)S(1)}, u32[]{:S(2)}, u32[]{:S(2)}) collective-permute-start(f32[6,8,128]{2,1,0:T(8,128)S(1)} %get-tuple-element.23), channel_id=1, source_target_pairs={{0,3},{1,0},{2,1},{3,2},{4,7},{5,4},{6,5},{7,6},{8,11},{9,8},{10,9... | collective-permute-start | bytes 73736 | tf_op jit(solution)/shard_map/ppermute | solution.py:476
  15.9 0.1 fusion
  16.0 1.0 %collective-permute-done.2.zm = f32[6,8,128]{2,1,0:T(8,128)S(1)} collective-permute-done((f32[6,8,128]{2,1,0:T(8,128)S(1)}, f32[6,8,128]{2,1,0:T(8,128)S(1)}, u32[]{:S(2)}, u32[]{:S(2)}) %collective-permute-start.2) | collective-permute-done | bytes 24608 | tf_op jit(solution)/shard_map/ppermute | solution.py:476
  17.0 0.0 collective-permute-done.3.zp
  17.1 0.1 layers.1
  17.1 4.6 %collective-permute-start.4 = (f32[6,72,128]{2,1,0:T(8,128)S(1)}, f32[6,72,128]{2,1,0:T(8,128)S(1)}, u32[]{:S(2)}, u32[]{:S(2)}) collective-permute-start(f32[6,72,128]{2,1,0:T(8,128)S(1)} %get-tuple-element.26.y_high), channel_id=1, source_target_pairs={{0,4},{4,8},{8,12},{12,16},{16,20},{20,24},{24,28},{28,0},{1,5},{5... | collective-permute-start | bytes 663560 | tf_op jit(solution)/shard_map/ppermute | solution.py:476
  21.8 2.8 %collective-permute-done.4.ym = f32[6,72,128]{2,1,0:T(8,128)S(1)} collective-permute-done((f32[6,72,128]{2,1,0:T(8,128)S(1)}, f32[6,72,128]{2,1,0:T(8,128)S(1)}, u32[]{:S(2)}, u32[]{:S(2)}) %collective-permute-start.4) | collective-permute-done | bytes 221216 | tf_op jit(solution)/shard_map/ppermute | solution.py:476
  24.7 2.5 %collective-permute-done.5.yp = f32[6,72,128]{2,1,0:T(8,128)S(1)} collective-permute-done((f32[6,72,128]{2,1,0:T(8,128)S(1)}, f32[6,72,128]{2,1,0:T(8,128)S(1)}, u32[]{:S(2)}, u32[]{:S(2)}) %collective-permute-start.5) | collective-permute-done | bytes 221216 | tf_op jit(solution)/shard_map/ppermute | solution.py:476
  27.1 5.2 %density.1 = (f32[32,128]{1,0:T(8,128)}, f32[5,296,128]{2,1,0:T(8,128)S(1)}, f32[5,40,128]{2,1,0:T(8,128)S(1)}, f32[5,40,128]{2,1,0:T(8,128)S(1)}, f32[5,8,128]{2,1,0:T(8,128)S(1)}) custom-call(f32[5,256,128]{2,1,0:T(8,128)S(1)} %bitcast.18, f32[256,128]{1,0:T(8,128)S(1)} %bitcast.24, s32[256,128]{1,0:T(8,128)S(1)} %bitcast.26, ...), custom_call_target="tpu_custom_call" | custom-call | tf_op jit(solution)/shard_map/density/pallas_call | solution.py:542
  32.3 6.8 %all-to-all-start = ((f32[32,1,128]{2,1,0:T(1,128)}), f32[32,1,128]{2,1,0:T(1,128)S(1)}, u32[]{:S(2)}, u32[]{:S(2)}) async-start(f32[32,1,128]{2,1,0:T(1,128)} %bitcast.11), calls=%async_computation | async-start | bytes 32768 | tf_op jit(solution)/shard_map/all_to_all | solution.py:583
  39.2 1.7 %state.1 = f32[5,256,128]{2,1,0:T(8,128)} custom-call(f32[5,256,128]{2,1,0:T(8,128)S(1)} %bitcast.19, f32[256,128]{1,0:T(8,128)S(1)} %bitcast.25, f32[12,8,128]{2,1,0:T(8,128)S(1)} %collective-permute-done.xm, f32[19,8,128]{2,1,0:T(8,128)S(1)} %collective-permute-done.1.xp, f32[5,296,128]{2,1,0:T(8,128)S(1)} %get-tuple-element.27.h, ...), custom_call_target="tpu_custom_call" | custom-call | flops 6000000 | bytes 6000000 | tf_op jit(solution)/shard_map/state/pallas_call | solution.py:576
  40.9 5.1 %all-to-all-done = f32[32,1,128]{2,1,0:T(1,128)S(1)} async-done(((f32[32,1,128]{2,1,0:T(1,128)}), f32[32,1,128]{2,1,0:T(1,128)S(1)}, u32[]{:S(2)}, u32[]{:S(2)}) %all-to-all-start) | async-done | bytes 16416 | tf_op jit(solution)/shard_map/all_to_all | solution.py:583
  46.0 1.2 %image.1 = f32[4,4,1920]{2,1,0:T(4,128)} custom-call(f32[1]{0:T(128)} %bitcast.9.flags, f32[32,128]{1,0:T(8,128)S(1)} %bitcast.27), custom_call_target="tpu_custom_call" | custom-call | tf_op jit(solution)/shard_map/image/pallas_call | solution.py:589
  (24 shorter events, 0.1 us)
Async XLA Ops:
  0.6 0.9 %copy-start.3 = (s32[32,8,128]{2,1,0:T(8,128)S(1)}, s32[32,8,128]{2,1,0:T(8,128)}, u32[]{:S(2)}) copy-start(s32[32,8,128]{2,1,0:T(8,128)} %param.7) | copy-start | bytes 393220
  0.6 0.9 %slice-start.1 = ((f32[5,32,8,128]{3,2,1,0:T(8,128)}), f32[5,2,8,128]{3,2,1,0:T(8,128)S(1)}, s32[]{:S(2)}) async-start(f32[5,32,8,128]{3,2,1,0:T(8,128)} %param.5), calls=%async_computation.2 | async-start | bytes 81920 | tf_op jit(solution)/shard_map/slice | solution.py:509
  0.7 0.9 %slice-start.3 = ((f32[32,8,128]{2,1,0:T(8,128)}), f32[2,8,128]{2,1,0:T(8,128)S(1)}, s32[]{:S(2)}) async-start(f32[32,8,128]{2,1,0:T(8,128)} %param.6), calls=%async_computation.4 | async-start | bytes 16384 | tf_op jit(solution)/shard_map/slice | solution.py:509
  0.7 0.9 %slice-start = ((f32[5,32,8,128]{3,2,1,0:T(8,128)}), f32[5,3,8,128]{3,2,1,0:T(8,128)S(1)}, s32[]{:S(2)}) async-start(f32[5,32,8,128]{3,2,1,0:T(8,128)} %param.5), calls=%async_computation.1 | async-start | bytes 122880 | tf_op jit(solution)/shard_map/slice | solution.py:502
  1.5 0.7 %slice-start.2 = ((f32[32,8,128]{2,1,0:T(8,128)}), f32[3,8,128]{2,1,0:T(8,128)S(1)}, s32[]{:S(2)}) async-start(f32[32,8,128]{2,1,0:T(8,128)} %param.6), calls=%async_computation.3 | async-start | bytes 24576 | tf_op jit(solution)/shard_map/slice | solution.py:503
  1.6 7.1 %copy-start.2 = (f32[32,8,128]{2,1,0:T(8,128)S(1)}, f32[32,8,128]{2,1,0:T(8,128)}, u32[]{:S(2)}) copy-start(f32[32,8,128]{2,1,0:T(8,128)} %param.6) | copy-start | bytes 393220
  2.3 10.6 %collective-permute-start.1 = (f32[19,8,128]{2,1,0:T(8,128)S(1)}, f32[19,8,128]{2,1,0:T(8,128)S(1)}, u32[]{:S(2)}, u32[]{:S(2)}) collective-permute-start(f32[19,8,128]{2,1,0:T(8,128)S(1)} %pad_maximum_fusion), channel_id=1, source_target_pairs={{0,224},{32,0},{64,32},{96,64},{128,96},{160,128},{192,160},{224,1... | collective-permute-start | bytes 233480 | tf_op jit(solution)/shard_map/ppermute | solution.py:476
  8.7 4.2 %collective-permute-start = (f32[12,8,128]{2,1,0:T(8,128)S(1)}, f32[12,8,128]{2,1,0:T(8,128)S(1)}, u32[]{:S(2)}, u32[]{:S(2)}) collective-permute-start(f32[12,8,128]{2,1,0:T(8,128)S(1)} %pad_maximum_fusion.1), channel_id=1, source_target_pairs={{0,32},{32,64},{64,96},{96,128},{128,160},{160,192},{192,224},{224... | collective-permute-start | bytes 147464 | tf_op jit(solution)/shard_map/ppermute | solution.py:476
  8.7 1.1 %copy-start = (f32[5,32,8,128]{3,2,1,0:T(8,128)S(1)}, f32[5,32,8,128]{3,2,1,0:T(8,128)}, u32[]{:S(2)}) copy-start(f32[5,32,8,128]{3,2,1,0:T(8,128)} %param.5) | copy-start | bytes 1966084
  9.8 7.3 %copy-start.1 = (f32[5,32,8,128]{3,2,1,0:T(8,128)S(1)}, f32[5,32,8,128]{3,2,1,0:T(8,128)}, u32[]{:S(2)}) copy-start(f32[5,32,8,128]{3,2,1,0:T(8,128)} %param.5) | copy-start | bytes 1966084
  12.8 3.1 %copy-start.4 = (f32[4,3,256]{2,0,1:T(4,128)S(1)}, f32[4,3,256]{2,0,1:T(4,128)}, u32[]{:S(2)}) copy-start(f32[4,3,256]{2,0,1:T(4,128)} %param.8) | copy-start | bytes 36868
  13.0 2.9 %copy-start.5 = (f32[4,256]{1,0:T(4,128)S(1)}, f32[4,256]{1,0:T(4,128)}, u32[]{:S(2)}) copy-start(f32[4,256]{1,0:T(4,128)} %param.9) | copy-start | bytes 12292
  13.0 4.0 %collective-permute-start.2 = (f32[6,8,128]{2,1,0:T(8,128)S(1)}, f32[6,8,128]{2,1,0:T(8,128)S(1)}, u32[]{:S(2)}, u32[]{:S(2)}) collective-permute-start(f32[6,8,128]{2,1,0:T(8,128)S(1)} %get-tuple-element.22), channel_id=1, source_target_pairs={{0,1},{1,2},{2,3},{3,0},{4,5},{5,6},{6,7},{7,4},{8,9},{9,10},{10,1... | collective-permute-start | bytes 73736 | tf_op jit(solution)/shard_map/ppermute | solution.py:476
  14.4 2.7 %collective-permute-start.3 = (f32[6,8,128]{2,1,0:T(8,128)S(1)}, f32[6,8,128]{2,1,0:T(8,128)S(1)}, u32[]{:S(2)}, u32[]{:S(2)}) collective-permute-start(f32[6,8,128]{2,1,0:T(8,128)S(1)} %get-tuple-element.23), channel_id=1, source_target_pairs={{0,3},{1,0},{2,1},{3,2},{4,7},{5,4},{6,5},{7,6},{8,11},{9,8},{10,9... | collective-permute-start | bytes 73736 | tf_op jit(solution)/shard_map/ppermute | solution.py:476
  17.1 7.5 %collective-permute-start.4 = (f32[6,72,128]{2,1,0:T(8,128)S(1)}, f32[6,72,128]{2,1,0:T(8,128)S(1)}, u32[]{:S(2)}, u32[]{:S(2)}) collective-permute-start(f32[6,72,128]{2,1,0:T(8,128)S(1)} %get-tuple-element.26.y_high), channel_id=1, source_target_pairs={{0,4},{4,8},{8,12},{12,16},{16,20},{20,24},{24,28},{28,0},{1,5},{5... | collective-permute-start | bytes 663560 | tf_op jit(solution)/shard_map/ppermute | solution.py:476
  21.8 5.4 %collective-permute-start.5 = (f32[6,72,128]{2,1,0:T(8,128)S(1)}, f32[6,72,128]{2,1,0:T(8,128)S(1)}, u32[]{:S(2)}, u32[]{:S(2)}) collective-permute-start(f32[6,72,128]{2,1,0:T(8,128)S(1)} %get-tuple-element.25.y_low), channel_id=1, source_target_pairs={{0,28},{4,0},{8,4},{12,8},{16,12},{20,16},{24,20},{28,24},{1,29},{... | collective-permute-start | bytes 663560 | tf_op jit(solution)/shard_map/ppermute | solution.py:476
  32.3 13.7 %all-to-all-start = ((f32[32,1,128]{2,1,0:T(1,128)}), f32[32,1,128]{2,1,0:T(1,128)S(1)}, u32[]{:S(2)}, u32[]{:S(2)}) async-start(f32[32,1,128]{2,1,0:T(1,128)} %bitcast.11), calls=%async_computation | async-start | bytes 32768 | tf_op jit(solution)/shard_map/all_to_all | solution.py:583

commit v4 on v3

--- a/solution.py
+++ b/solution.py
@@ -11,6 +11,7 @@
 ZOOM = 4
 CLASSES = 4
 LUT = 256
+FIXED = 65535
 
 dissipation = 3.0
 courant = 0.11
@@ -109,6 +110,25 @@
     return u[f, span, :] if f < 5 else g[span, :]
 
 
+def x_kernel(u, g, sp, x_low, x_high, kinds, semaphores):
+    own = u.shape[1]
+    moves = []
+    for f in range(6):
+        source = u.at[f] if f < 5 else g
+        moves.append((source.at[pl.ds(0, ABOVE)], x_low.at[pl.ds(f * ABOVE, ABOVE)]))
+        moves.append((source.at[pl.ds(own - HALO, HALO)], x_high.at[pl.ds(f * HALO, HALO)]))
+    moves.append((sp.at[0], kinds))
+    copies = [
+        pltpu.make_async_copy(source, target, semaphores.at[k])
+        for k, (source, target) in enumerate(moves)
+    ]
+    for copy in copies:
+        copy.start()
+    for copy in copies:
+        copy.wait()
+    x_low[6 * ABOVE] = kinds[...].astype(F32)
+
+
 def strips(load, rows, parts):
     up, down, inner = parts
     for row in rows:
@@ -183,8 +203,11 @@
         if pending is not None:
             finish(row - 1, [a + b for a, b in zip(pending, x_up)])
         edge = [pltpu.roll(z_edge[f], LANES - 1 - 2 * row, 1) for f in range(5)]
-        below = [y_below[f, pl.ds(row, 1), :] for f in range(5)]
-        above = [y_above[f, pl.ds(row, 1), :] for f in range(5)]
+        if y_below is None:
+            below = above = [0.0] * 5
+        else:
+            below = [y_below[f, pl.ds(row, 1), :] for f in range(5)]
+            above = [y_above[f, pl.ds(row, 1), :] for f in range(5)]
         core = total_change(
             cell,
             (along_y(y_up, y_down, below, above), along_z(z_up, z_down, edge, edge)),
@@ -194,7 +217,7 @@
     finish(last, [a + b for a, b in zip(pending, up_of(0, load(last + 1)))])
 
 
-def lookup(density, species, tables):
+def lookup(density, species, colors, extinctions):
     position = (density - density_low) * ((LUT - 1) / (density_high - density_low))
     knot = jnp.clip(jnp.floor(position), 0.0, LUT - 1.0)
     offset = position - knot
@@ -203,32 +226,39 @@
     index = knot.astype(jnp.int32)
     lane_index = index % LANES
     bits = (index >= LANES, species % 2 == 1, species >= 2)
+
+    def pick(table):
+        values = [
+            jnp.take_along_axis(table(k), lane_index, axis=1, mode="promise_in_bounds")
+            for k in range(8)
+        ]
+        for bit in bits:
+            values = [jnp.where(bit, values[k + 1], values[k]) for k in range(0, len(values), 2)]
+        return values[0]
+
     result = []
-    for channel in range(4):
-        total = None
-        for side, weight in ((0, lower_weight), (1, upper_weight)):
-            values = [
-                jnp.take_along_axis(
-                    tables[channel, side, k], lane_index, axis=1, mode="promise_in_bounds"
-                )
-                for k in range(8)
-            ]
-            for bit in bits:
-                values = [
-                    jnp.where(bit, values[k + 1], values[k]) for k in range(0, len(values), 2)
-                ]
-            term = weight * values[0]
-            total = term if total is None else total + term
-        result.append(total)
+    lower_scaled = lower_weight * (1.0 / FIXED)
+    upper_scaled = upper_weight * (1.0 / FIXED)
+    for channel in range(3):
+        both = pick(lambda k: colors[channel, k])
+        result.append(
+            lower_scaled * (both & FIXED).astype(F32)
+            + upper_scaled * lax.shift_right_logical(both, 16).astype(F32)
+        )
+    result.append(
+        lower_weight * pick(lambda k: extinctions[0, k])
+        + upper_weight * pick(lambda k: extinctions[1, k])
+    )
     return result
 
 
-def spread_tables(lut_lower, lut_upper, tables):
-    for channel in range(4):
-        for k in range(8):
-            for side, source in ((0, lut_lower), (1, lut_upper)):
-                row = source[pl.ds(channel * 8 + k, 1), :]
-                tables[channel, side, k] = jnp.broadcast_to(row, (SUBS, LANES))
+def classify(sp, xp, colors, extinctions, properties, own):
+    for place in range(own + 1):
+        span = pl.ds(place * SUBS, SUBS)
+        kind = sp[span, :] if place < own else xp[6 * ABOVE].astype(jnp.int32)
+        found = lookup(properties[0, span, :], kind, colors, extinctions)
+        for channel in range(4):
+            properties[channel, span, :] = found[channel]
 
 
 def split_dot(value, weights):
@@ -241,7 +271,7 @@
     return total + jnp.dot(third, weights, preferred_element_type=F32)
 
 
-def integrate(properties, grouped, rows):
+def integrate(properties, grouped, rows, keep):
     extinction = properties[3]
     below = (iota((LANES, LANES), 0) < iota((LANES, LANES), 1)).astype(jnp.bfloat16)
     before = split_dot(extinction, below)
@@ -257,7 +287,10 @@
             summed = jnp.exp(-summed)
         plane = jnp.zeros((SUBS, LANES), F32)
         for row in range(rows):
-            plane = jnp.where(lanes() == row, summed[row * SUBS : (row + 1) * SUBS], plane)
+            part = summed[row * SUBS : (row + 1) * SUBS]
+            if row == rows - 1:
+                part = part * keep + (1.0 - keep if channel == 3 else 0.0)
+            plane = jnp.where(lanes() == row, part, plane)
         gathered.append(plane)
     following = [pltpu.roll(plane, LANES - 1, 1) for plane in gathered]
     block = jnp.concatenate(
@@ -266,21 +299,34 @@
     grouped[...] = jnp.transpose(block)[: rows - 1]
 
 
-def classify(sp, xp, tables, properties, own):
-    for place in range(own + 1):
-        span = pl.ds(place * SUBS, SUBS)
-        kind = sp[span, :] if place < own else xp[6 * ABOVE].astype(jnp.int32)
-        found = lookup(properties[0, span, :], kind, tables)
-        for channel in range(4):
-            properties[channel, span, :] = found[channel]
+def half_kernel(u, g, xm, xp, zm, zp, color_rows, extinction_rows, h, colors, extinctions, z_edge):
+    own = g.shape[0] // SUBS
+    for k in range(24):
+        colors[k // 8, k % 8] = jnp.broadcast_to(color_rows[pl.ds(k, 1), :], (SUBS, LANES))
+    for k in range(16):
+        row = extinction_rows[pl.ds(k, 1), :]
+        extinctions[k // 8, k % 8] = jnp.broadcast_to(row, (SUBS, LANES))
+    up, down = halves((2,), [strips_of(zm, zp, f)[0] for f in range(6)])[0]
+    for f in range(5):
+        z_edge[f] = jnp.where(lanes() % 2 == 1, down[f], up[f])
+
+    def at_first(row):
+        return [row_of(u, g, xm, xp, f, row) for f in range(6)]
+
+    def store_half(row, change):
+        for f in range(5):
+            h[f, pl.ds(row * SUBS, SUBS), :] = (
+                row_of(u, g, xm, xp, f, row) - courant * change[f]
+            )
+
+    sweep(at_first, 1, HALO + own + 1, None, None, z_edge, store_half)
 
 
 def step_kernel(
-    u, g, sp, xm, xp, zm, zp, z_inner, y_low, y_high, ym, yp, lut_lower, lut_upper,
-    grouped, h, y_below2, y_above2, z_edge2, y_below, y_above, z_edge, turned, tables, properties
+    keep, u, g, sp, xm, xp, zm, zp, z_inner, y_low, y_high, ym, yp, partial, colors, extinctions,
+    grouped, h, y_below2, y_above2, z_edge2, y_below, y_above, turned, properties
 ):
     own = g.shape[0] // SUBS
-    spread_tables(lut_lower, lut_upper, tables)
     odd = lanes() % 2 == 1
 
     for start in (1, 9, 17, 25, 28):
@@ -288,8 +334,8 @@
         below = down_of(1, [ym[f, span, :] for f in range(6)])
         above = up_of(1, [yp[f, span, :] for f in range(6)])
         for f in range(5):
-            y_below[f, pl.ds(start, SUBS), :] = below[f]
-            y_above[f, pl.ds(start, SUBS), :] = above[f]
+            y_below[f, pl.ds(start, SUBS), :] = courant * below[f]
+            y_above[f, pl.ds(start, SUBS), :] = -courant * above[f]
 
     pairs = [strips_of(zm, zp, f) for f in range(6)]
     first = [pair[0] for pair in pairs]
@@ -305,8 +351,6 @@
     ]
     (corner_up, corner_down), (corner_zup, corner_zdown) = halves((1, 2), corner)
     (x_up, x_down), (y_up, y_down), (z_up, z_down) = halves((0, 1, 2), first)
-    for f in range(5):
-        z_edge[f] = jnp.where(odd, z_down[f], z_up[f])
     from_above = up_of(2, [jnp.where(odd, a, b) for a, b in zip(inner, second)])
     from_below = down_of(2, [jnp.where(odd, a, b) for a, b in zip(second, inner)])
     change = total_change(
@@ -365,16 +409,13 @@
             for f in range(5):
                 target[f, pl.ds(start, SUBS), :] = part[f]
 
-    def at_first(row):
-        return [row_of(u, g, xm, xp, f, row) for f in range(6)]
-
-    def store_half(row, change):
+    for row in range(1, HALO + own + 2):
+        span = pl.ds(row * SUBS, SUBS)
         for f in range(5):
-            h[f, pl.ds(row * SUBS, SUBS), :] = (
-                row_of(u, g, xm, xp, f, row) - courant * change[f]
-            )
-
-    sweep(at_first, 1, HALO + own + 1, y_below, y_above, z_edge, store_half)
+            low = y_below[f, pl.ds(row, 1), :]
+            high = y_above[f, pl.ds(row, 1), :]
+            added = jnp.where(subs() == 0, low, jnp.where(subs() == SUBS - 1, high, 0.0))
+            h[f, span, :] = partial[f, span, :] + added
 
     def finish(row, change):
         value = 0.5 * (
@@ -386,8 +427,8 @@
         return half_row(h, g, xm, xp, row)
 
     sweep(at_half, HALO, HALO + own, y_below2, y_above2, z_edge2, finish)
-    classify(sp, xp, tables, properties, own)
-    integrate(properties, grouped, own + 1)
+    classify(sp, xp, colors, extinctions, properties, own)
+    integrate(properties, grouped, own + 1, keep[0])
 
 
 def half_row(h, g, xm, xp, row):
@@ -412,7 +453,7 @@
     sweep(at_half, HALO, HALO + own - 1, y_below2, y_above2, z_edge2, finish)
 
 
-def image_kernel(across_y, across_z, flags, parts, out):
+def image_kernel(across_y, across_z, parts, out):
     lane = iota((across_y, LANES), 1)
     channel = (lane // 8) % 4
     total = None
@@ -427,8 +468,6 @@
         else:
             total = jnp.where(channel == 3, 0.0, part) + through * total
     total = jnp.where(channel == 3, 1.0 - total, total)
-    keep = jnp.where(lane >= 32, flags[0], 1.0)
-    total = jnp.where(lane < 64, total * keep, 0.0)
     sub8 = iota((8, LANES), 0)
     lane8 = iota((8, LANES), 1)
     moved = jnp.zeros((8, LANES), F32)
@@ -491,25 +530,22 @@
     across_y = lax.axis_size("gy")
     across_z = lax.axis_size("gz")
 
-    lut_table = jnp.concatenate([lut_color, lut_extinction[:, None, :]], axis=1)
-    lut_lower = lut_table.transpose(1, 0, 2).reshape(32, LANES)
-    lut_upper = (
-        jnp.pad(lut_table[:, :, 1:], ((0, 0), (0, 0), (0, 1))).transpose(1, 0, 2).reshape(32, LANES)
-    )
-
-    x_low = jnp.concatenate(
-        [
-            conserved[:, :ABOVE].reshape(5 * ABOVE, SUBS, LANES),
-            gamma_field[:ABOVE],
-            species[:1].astype(F32),
-        ],
-        axis=0,
-    )
-    x_high = jnp.concatenate(
-        [conserved[:, rows - HALO :].reshape(5 * HALO, SUBS, LANES), gamma_field[rows - HALO :]],
-        axis=0,
-    )
-    x_low, x_high = lax.optimization_barrier((x_low, x_high))
+    fixed = jnp.round(jnp.clip(lut_color, 0.0, 1.0) * FIXED).astype(jnp.int32)
+    following = jnp.pad(fixed[:, :, 1:], ((0, 0), (0, 0), (0, 1)))
+    color_rows = (fixed + lax.shift_left(following, 16)).transpose(1, 0, 2).reshape(24, LANES)
+    extinction_rows = jnp.stack(
+        [lut_extinction, jnp.pad(lut_extinction[:, 1:], ((0, 0), (0, 1)))]
+    ).reshape(16, LANES)
+
+    in_hbm = pl.BlockSpec(memory_space=pltpu.HBM)
+    x_low, x_high = pl.pallas_call(
+        x_kernel,
+        out_shape=(struct(6 * ABOVE + 1, SUBS, LANES), struct(6 * HALO, SUBS, LANES)),
+        in_specs=[in_hbm, in_hbm, in_hbm],
+        scratch_shapes=[pltpu.VMEM((SUBS, LANES), jnp.int32), pltpu.SemaphoreType.DMA((13,))],
+        compiler_params=pltpu.CompilerParams(vmem_limit_bytes=60 * 1024 * 1024),
+        name="x_layers",
+    )(conserved, gamma_field, species)
     xm = shifted(x_high, "gx", 1)
     xp = shifted(x_low, "gx", -1)
     brick = (
@@ -538,12 +574,29 @@
     )(*brick, xm, xp, zm, zp)
     ym = shifted(y_high, "gy", 1)
     yp = shifted(y_low, "gy", -1)
+    every = cells + (HALO + ABOVE) * SUBS
+    partial, colors, extinctions = pl.pallas_call(
+        half_kernel,
+        out_shape=(
+            struct(5, every, LANES),
+            jax.ShapeDtypeStruct((3, 8, SUBS, LANES), jnp.int32),
+            struct(2, 8, SUBS, LANES),
+        ),
+        scratch_shapes=[pltpu.VMEM((5, SUBS, LANES), F32)],
+        compiler_params=params,
+        cost_estimate=cost(4_000_000),
+        name="half",
+    )(*brick, xm, xp, zm, zp, color_rows, extinction_rows)
     layer = pltpu.VMEM((5, 40, LANES), F32)
+    place = lax.axis_index("gx")
+    keep = jnp.where(place == lax.axis_size("gx") - 1, 0.0, 1.0).reshape(1)
+    vmem = pl.BlockSpec(memory_space=pltpu.VMEM)
     grouped, *halves_found = pl.pallas_call(
         step_kernel,
+        in_specs=[pl.BlockSpec(memory_space=pltpu.SMEM)] + [vmem] * 15,
         out_shape=(
             struct(rows, LANES),
-            struct(5, cells + (HALO + ABOVE) * SUBS, LANES),
+            struct(5, every, LANES),
             struct(5, 40, LANES),
             struct(5, 40, LANES),
             struct(5, SUBS, LANES),
@@ -551,14 +604,13 @@
         scratch_shapes=[
             layer,
             layer,
-            pltpu.VMEM((5, SUBS, LANES), F32),
             pltpu.VMEM((LANES, LANES), F32),
-            pltpu.VMEM((4, 2, 8, SUBS, LANES), F32),
             pltpu.VMEM((4, cells + SUBS, LANES), F32),
         ],
         compiler_params=params,
         name="density",
     )(
+        keep,
         *brick,
         species.reshape(cells, LANES),
         xm,
@@ -570,8 +622,9 @@
         y_high,
         ym,
         yp,
-        lut_lower,
-        lut_upper,
+        partial,
+        colors,
+        extinctions,
     )
     new_state = pl.pallas_call(
         state_kernel,
@@ -583,19 +636,12 @@
     merged = lax.all_to_all(
         grouped.reshape(across_y * across_z, 1, LANES), ("gy", "gz"), 0, 0, tiled=True
     ).reshape(across_y * across_z, LANES)
-    place = lax.axis_index(("gx", "gy", "gz"))
-    last = lax.axis_size(("gx", "gy", "gz")) - 1
-    flags = jnp.where(place == last, 0.0, 1.0).reshape(1)
     image = pl.pallas_call(
         functools.partial(image_kernel, across_y, across_z),
         out_shape=struct(4, ZOOM, SW),
-        in_specs=[
-            pl.BlockSpec(memory_space=pltpu.SMEM),
-            pl.BlockSpec(memory_space=pltpu.VMEM),
-        ],
         compiler_params=params,
         name="image",
-    )(flags, merged)
+    )(merged)
     return new_state.reshape(conserved.shape), image
 
 

time: 47.4 us -> 41.7 us (0.88)
  waiting for transfers between devices: 13.9 us -> 10.2 us
  local copies, waits for them, and re-layouts: 2.69 us -> 0.2 us
  Pallas kernels: 9.01 us -> 9.7 us
    ppermute x6, waiting for transfers between devices: 8.75 us -> 5.03 us  [shifted(): lax.ppermute(value, axis, [(i, (i + steps) % size) for i in range(size)])]
    unnamed x12 -> x10, local copies, waits for them, and re-layouts: 1.97 us -> 0.02 us
    pallas_call x1 -> x3, Pallas kernels: 5.16 us -> 5.84 us  [the longest x1 3.37 us: local(): pl.pallas_call(step_kernel, in_specs=[pl.BlockSpec(memory_space=pltpu.SME...]
    slice x8 -> x2, local copies, waits for them, and re-layouts: 0.69 us -> 0.14 us  [the longest x1 0.07 us: local(): following = jnp.pad(fixed[:, :, 1:], ((0, 0), (0, 0), (0, 1)))]
  transfers between devices with their start and end apart: 7 -> 7, of which waited for: 5 -> 5; matrix products, arithmetic and copies ran while one was open for 0% -> 0% of each run, Pallas kernels for 5% -> 8%
where the time goes in v4:
time: 41.7 us; the launch traced here: 41.6 us
  starting transfers between devices  20.7 us (50%)
  waiting for transfers between devices  10.2 us (24%)
  Pallas kernels  9.7 us (23%)
  between operations  0.75 us (2%)
    ppermute x6, starting transfers between devices, shifted(): lax.ppermute(value, axis, [(i, (i + steps) % size) for i in range(size)])  13.6 us
    all_to_all x1, starting transfers between devices, local(): lax.all_to_all(grouped.reshape(across_y * across_z, 1, LANES), ('gy', 'gz...  7.16 us
    all_to_all x1, waiting for transfers between devices, local(): lax.all_to_all(grouped.reshape(across_y * across_z, 1, LANES), ('gy', 'gz...  5.14 us
    ppermute x6, waiting for transfers between devices, shifted(): lax.ppermute(value, axis, [(i, (i + steps) % size) for i in range(size)])  5.03 us
    pallas_call x1, Pallas kernels, local(): pl.pallas_call(step_kernel, in_specs=[pl.BlockSpec(memory_space=pltpu.SME...  3.37 us
    pallas_call x1, Pallas kernels, local(): pl.pallas_call(state_kernel, out_shape=struct(5, cells, LANES), compiler_...  1.71 us
    pallas_call x1, Pallas kernels, local(): pl.pallas_call(x_kernel, out_shape=(struct(6 * ABOVE + 1, SUBS, LANES), s...  1.63 us
    pallas_call x1, Pallas kernels, local(): pl.pallas_call(functools.partial(image_kernel, across_y, across_z), out_s...  1.24 us
  transfers between devices with their start and end apart: 7, of which 5 were waited for; matrix products, arithmetic and copies ran while one was open for 0% of the time, Pallas kernels for 8%

profile of v4, /device:TPU:1, one launch (start us, length us, event | category | flops | bytes accessed | tf_op | source)
XLA Modules:
  0.0 41.6 jit_solution(8748741928405374239)
XLA Ops:
  0.7 1.6 %x_layers.1 = (f32[19,8,128]{2,1,0:T(8,128)}, f32[12,8,128]{2,1,0:T(8,128)}) custom-call(f32[5,32,8,128]{3,2,1,0:T(8,128)} %u.1, f32[32,8,128]{2,1,0:T(8,128)} %g.1, s32[32,8,128]{2,1,0:T(8,128)} %sp.1), custom_call_target="tpu_custom_call" | custom-call | tf_op jit(solution)/shard_map/x_layers/pallas_call | solution.py:541
  2.3 2.5 %collective-permute-start = (f32[12,8,128]{2,1,0:T(8,128)}, f32[12,8,128]{2,1,0:T(8,128)S(1)}, u32[]{:S(2)}, u32[]{:S(2)}) collective-permute-start(f32[12,8,128]{2,1,0:T(8,128)} %get-tuple-element.20), channel_id=1, source_target_pairs={{0,32},{32,64},{64,96},{96,128},{128,160},{160,192},{192,224},{224... | collective-permute-start | bytes 147464 | tf_op jit(solution)/shard_map/ppermute | solution.py:515
  4.8 4.0 %collective-permute-start.1 = (f32[19,8,128]{2,1,0:T(8,128)}, f32[19,8,128]{2,1,0:T(8,128)S(1)}, u32[]{:S(2)}, u32[]{:S(2)}) collective-permute-start(f32[19,8,128]{2,1,0:T(8,128)} %get-tuple-element.21), channel_id=1, source_target_pairs={{0,224},{32,0},{64,32},{96,64},{128,96},{160,128},{192,160},{224,1... | collective-permute-start | bytes 233480 | tf_op jit(solution)/shard_map/ppermute | solution.py:515
  8.9 0.1 slice.7
  9.0 0.7 %own_strips.1 = (f32[6,8,128]{2,1,0:T(8,128)S(1)}, f32[6,8,128]{2,1,0:T(8,128)S(1)}, f32[6,8,128]{2,1,0:T(8,128)S(1)}) custom-call(f32[5,256,128]{2,1,0:T(8,128)S(1)} %bitcast.14, f32[256,128]{1,0:T(8,128)S(1)} %bitcast.19), custom_call_target="tpu_custom_call" | custom-call | flops 2000000 | bytes 2000000 | tf_op jit(solution)/shard_map/own_strips/pallas_call | solution.py:556
  9.7 0.8 %collective-permute-done.xm = f32[12,8,128]{2,1,0:T(8,128)S(1)} collective-permute-done((f32[12,8,128]{2,1,0:T(8,128)}, f32[12,8,128]{2,1,0:T(8,128)S(1)}, u32[]{:S(2)}, u32[]{:S(2)}) %collective-permute-start) | collective-permute-done | bytes 49184 | tf_op jit(solution)/shard_map/ppermute | solution.py:515
  10.5 0.2 collective-permute-done.1.xp
  10.6 0.1 strips.1
  10.8 1.4 %collective-permute-start.2 = (f32[6,8,128]{2,1,0:T(8,128)S(1)}, f32[6,8,128]{2,1,0:T(8,128)S(1)}, u32[]{:S(2)}, u32[]{:S(2)}) collective-permute-start(f32[6,8,128]{2,1,0:T(8,128)S(1)} %get-tuple-element.25), channel_id=1, source_target_pairs={{0,1},{1,2},{2,3},{3,0},{4,5},{5,6},{6,7},{7,4},{8,9},{9,10},{10,1... | collective-permute-start | bytes 73736 | tf_op jit(solution)/shard_map/ppermute | solution.py:515
  12.2 1.5 %collective-permute-start.3 = (f32[6,8,128]{2,1,0:T(8,128)S(1)}, f32[6,8,128]{2,1,0:T(8,128)S(1)}, u32[]{:S(2)}, u32[]{:S(2)}) collective-permute-start(f32[6,8,128]{2,1,0:T(8,128)S(1)} %get-tuple-element.26), channel_id=1, source_target_pairs={{0,3},{1,0},{2,1},{3,2},{4,7},{5,4},{6,5},{7,6},{8,11},{9,8},{10,9... | collective-permute-start | bytes 73736 | tf_op jit(solution)/shard_map/ppermute | solution.py:515
  13.7 0.1 slice.8
  13.8 1.0 %collective-permute-done.2.zm = f32[6,8,128]{2,1,0:T(8,128)S(1)} collective-permute-done((f32[6,8,128]{2,1,0:T(8,128)S(1)}, f32[6,8,128]{2,1,0:T(8,128)S(1)}, u32[]{:S(2)}, u32[]{:S(2)}) %collective-permute-start.2) | collective-permute-done | bytes 24608 | tf_op jit(solution)/shard_map/ppermute | solution.py:515
  14.8 0.0 collective-permute-done.3.zp
  14.8 0.1 layers.1
  14.9 3.0 %collective-permute-start.5 = (f32[6,72,128]{2,1,0:T(8,128)S(1)}, f32[6,72,128]{2,1,0:T(8,128)S(1)}, u32[]{:S(2)}, u32[]{:S(2)}) collective-permute-start(f32[6,72,128]{2,1,0:T(8,128)S(1)} %get-tuple-element.28.y_low), channel_id=1, source_target_pairs={{0,28},{4,0},{8,4},{12,8},{16,12},{20,16},{24,20},{28,24},{1,29},{... | collective-permute-start | bytes 663560 | tf_op jit(solution)/shard_map/ppermute | solution.py:515
  17.9 1.1 %collective-permute-start.4 = (f32[6,72,128]{2,1,0:T(8,128)S(1)}, f32[6,72,128]{2,1,0:T(8,128)S(1)}, u32[]{:S(2)}, u32[]{:S(2)}) collective-permute-start(f32[6,72,128]{2,1,0:T(8,128)S(1)} %get-tuple-element.29.y_high), channel_id=1, source_target_pairs={{0,4},{4,8},{8,12},{12,16},{16,20},{20,24},{24,28},{28,0},{1,5},{5... | collective-permute-start | bytes 663560 | tf_op jit(solution)/shard_map/ppermute | solution.py:515
  19.1 0.0 copy-start.2
  19.1 0.8 %half.1 = (f32[5,296,128]{2,1,0:T(8,128)S(1)}, s32[3,8,8,128]{3,2,1,0:T(8,128)S(1)}, f32[2,8,8,128]{3,2,1,0:T(8,128)S(1)}) custom-call(f32[5,256,128]{2,1,0:T(8,128)S(1)} %bitcast.16, f32[256,128]{1,0:T(8,128)S(1)} %bitcast.21, f32[12,8,128]{2,1,0:T(8,128)S(1)} %collective-permute-done.xm, f32[19,8,128]{2,1,0:T(8,128)S(1)} %collective-permute-done.1.xp, ...), custom_call_target="tpu_custom_call" | custom-call | flops 4000000 | bytes 4000000 | tf_op jit(solution)/shard_map/half/pallas_call | solution.py:578
  19.9 3.0 %collective-permute-done.5.yp = f32[6,72,128]{2,1,0:T(8,128)S(1)} collective-permute-done((f32[6,72,128]{2,1,0:T(8,128)S(1)}, f32[6,72,128]{2,1,0:T(8,128)S(1)}, u32[]{:S(2)}, u32[]{:S(2)}) %collective-permute-start.5) | collective-permute-done | bytes 221216 | tf_op jit(solution)/shard_map/ppermute | solution.py:515
  22.9 3.4 %density.1 = (f32[32,128]{1,0:T(8,128)}, f32[5,296,128]{2,1,0:T(8,128)S(1)}, f32[5,40,128]{2,1,0:T(8,128)S(1)}, f32[5,40,128]{2,1,0:T(8,128)S(1)}, f32[5,8,128]{2,1,0:T(8,128)S(1)}) custom-call(f32[1]{0:T(128)} %bitcast.2.keep, f32[5,256,128]{2,1,0:T(8,128)S(1)} %bitcast.17, f32[256,128]{1,0:T(8,128)S(1)} %bitcast.22, s32[256,128]{1,0:T(8,128)S(1)} %bitcast.24, ...), custom_call_target="tpu_custom_call" | custom-call | tf_op jit(solution)/shard_map/density/pallas_call | solution.py:594
  26.3 7.2 %all-to-all-start = ((f32[32,1,128]{2,1,0:T(1,128)}), f32[32,1,128]{2,1,0:T(1,128)S(1)}, u32[]{:S(2)}, u32[]{:S(2)}) async-start(f32[32,1,128]{2,1,0:T(1,128)} %bitcast.9), calls=%async_computation | async-start | bytes 32768 | tf_op jit(solution)/shard_map/all_to_all | solution.py:636
  33.5 1.7 %state.1 = f32[5,256,128]{2,1,0:T(8,128)} custom-call(f32[5,256,128]{2,1,0:T(8,128)S(1)} %bitcast.18, f32[256,128]{1,0:T(8,128)S(1)} %bitcast.23, f32[12,8,128]{2,1,0:T(8,128)S(1)} %collective-permute-done.xm, f32[19,8,128]{2,1,0:T(8,128)S(1)} %collective-permute-done.1.xp, f32[5,296,128]{2,1,0:T(8,128)S(1)} %get-tuple-element.33.h, ...), custom_call_target="tpu_custom_call" | custom-call | flops 6000000 | bytes 6000000 | tf_op jit(solution)/shard_map/state/pallas_call | solution.py:629
  35.2 5.1 %all-to-all-done = f32[32,1,128]{2,1,0:T(1,128)S(1)} async-done(((f32[32,1,128]{2,1,0:T(1,128)}), f32[32,1,128]{2,1,0:T(1,128)S(1)}, u32[]{:S(2)}, u32[]{:S(2)}) %all-to-all-start) | async-done | bytes 16416 | tf_op jit(solution)/shard_map/all_to_all | solution.py:636
  40.3 1.2 %image.1 = f32[4,4,1920]{2,1,0:T(4,128)} custom-call(f32[32,128]{1,0:T(8,128)S(1)} %bitcast.25), custom_call_target="tpu_custom_call" | custom-call | tf_op jit(solution)/shard_map/image/pallas_call | solution.py:639
  (16 shorter events, 0.1 us)
Async XLA Ops:
  0.6 8.3 %copy-start = (f32[5,32,8,128]{3,2,1,0:T(8,128)S(1)}, f32[5,32,8,128]{3,2,1,0:T(8,128)}, u32[]{:S(2)}) copy-start(f32[5,32,8,128]{3,2,1,0:T(8,128)} %u.1) | copy-start | bytes 1966084
  0.6 8.2 %copy-start.4 = (f32[4,256]{1,0:T(4,128)S(1)}, f32[4,256]{1,0:T(4,128)}, u32[]{:S(2)}) copy-start(f32[4,256]{1,0:T(4,128)} %param.9) | copy-start | bytes 12292
  0.7 8.3 %copy-start.3 = (f32[4,3,256]{2,0,1:T(4,128)S(1)}, f32[4,3,256]{2,0,1:T(4,128)}, u32[]{:S(2)}) copy-start(f32[4,3,256]{2,0,1:T(4,128)} %param.8) | copy-start | bytes 36868
  0.7 8.3 %copy-start.1 = (f32[32,8,128]{2,1,0:T(8,128)S(1)}, f32[32,8,128]{2,1,0:T(8,128)}, u32[]{:S(2)}) copy-start(f32[32,8,128]{2,1,0:T(8,128)} %g.1) | copy-start | bytes 393220
  2.3 8.2 %collective-permute-start = (f32[12,8,128]{2,1,0:T(8,128)}, f32[12,8,128]{2,1,0:T(8,128)S(1)}, u32[]{:S(2)}, u32[]{:S(2)}) collective-permute-start(f32[12,8,128]{2,1,0:T(8,128)} %get-tuple-element.20), channel_id=1, source_target_pairs={{0,32},{32,64},{64,96},{96,128},{128,160},{160,192},{192,224},{224... | collective-permute-start | bytes 147464 | tf_op jit(solution)/shard_map/ppermute | solution.py:515
  4.8 5.8 %collective-permute-start.1 = (f32[19,8,128]{2,1,0:T(8,128)}, f32[19,8,128]{2,1,0:T(8,128)S(1)}, u32[]{:S(2)}, u32[]{:S(2)}) collective-permute-start(f32[19,8,128]{2,1,0:T(8,128)} %get-tuple-element.21), channel_id=1, source_target_pairs={{0,224},{32,0},{64,32},{96,64},{128,96},{160,128},{192,160},{224,1... | collective-permute-start | bytes 233480 | tf_op jit(solution)/shard_map/ppermute | solution.py:515
  10.8 4.0 %collective-permute-start.2 = (f32[6,8,128]{2,1,0:T(8,128)S(1)}, f32[6,8,128]{2,1,0:T(8,128)S(1)}, u32[]{:S(2)}, u32[]{:S(2)}) collective-permute-start(f32[6,8,128]{2,1,0:T(8,128)S(1)} %get-tuple-element.25), channel_id=1, source_target_pairs={{0,1},{1,2},{2,3},{3,0},{4,5},{5,6},{6,7},{7,4},{8,9},{9,10},{10,1... | collective-permute-start | bytes 73736 | tf_op jit(solution)/shard_map/ppermute | solution.py:515
  12.2 2.7 %collective-permute-start.3 = (f32[6,8,128]{2,1,0:T(8,128)S(1)}, f32[6,8,128]{2,1,0:T(8,128)S(1)}, u32[]{:S(2)}, u32[]{:S(2)}) collective-permute-start(f32[6,8,128]{2,1,0:T(8,128)S(1)} %get-tuple-element.26), channel_id=1, source_target_pairs={{0,3},{1,0},{2,1},{3,2},{4,7},{5,4},{6,5},{7,6},{8,11},{9,8},{10,9... | collective-permute-start | bytes 73736 | tf_op jit(solution)/shard_map/ppermute | solution.py:515
  14.9 8.0 %collective-permute-start.5 = (f32[6,72,128]{2,1,0:T(8,128)S(1)}, f32[6,72,128]{2,1,0:T(8,128)S(1)}, u32[]{:S(2)}, u32[]{:S(2)}) collective-permute-start(f32[6,72,128]{2,1,0:T(8,128)S(1)} %get-tuple-element.28.y_low), channel_id=1, source_target_pairs={{0,28},{4,0},{8,4},{12,8},{16,12},{20,16},{24,20},{28,24},{1,29},{... | collective-permute-start | bytes 663560 | tf_op jit(solution)/shard_map/ppermute | solution.py:515
  17.9 5.0 %collective-permute-start.4 = (f32[6,72,128]{2,1,0:T(8,128)S(1)}, f32[6,72,128]{2,1,0:T(8,128)S(1)}, u32[]{:S(2)}, u32[]{:S(2)}) collective-permute-start(f32[6,72,128]{2,1,0:T(8,128)S(1)} %get-tuple-element.29.y_high), channel_id=1, source_target_pairs={{0,4},{4,8},{8,12},{12,16},{16,20},{20,24},{24,28},{28,0},{1,5},{5... | collective-permute-start | bytes 663560 | tf_op jit(solution)/shard_map/ppermute | solution.py:515
  19.1 3.9 %copy-start.2 = (s32[32,8,128]{2,1,0:T(8,128)S(1)}, s32[32,8,128]{2,1,0:T(8,128)}, u32[]{:S(2)}) copy-start(s32[32,8,128]{2,1,0:T(8,128)} %sp.1) | copy-start | bytes 393220
  26.3 14.0 %all-to-all-start = ((f32[32,1,128]{2,1,0:T(1,128)}), f32[32,1,128]{2,1,0:T(1,128)S(1)}, u32[]{:S(2)}, u32[]{:S(2)}) async-start(f32[32,1,128]{2,1,0:T(1,128)} %bitcast.9), calls=%async_computation | async-start | bytes 32768 | tf_op jit(solution)/shard_map/all_to_all | solution.py:636

commit v5 on v4

--- a/solution.py
+++ b/solution.py
@@ -12,6 +12,7 @@
 CLASSES = 4
 LUT = 256
 FIXED = 65535
+EXTINCTION_TOP = 0.01
 
 dissipation = 3.0
 courant = 0.11
@@ -217,7 +218,7 @@
     finish(last, [a + b for a, b in zip(pending, up_of(0, load(last + 1)))])
 
 
-def lookup(density, species, colors, extinctions):
+def lookup(density, species, tables):
     position = (density - density_low) * ((LUT - 1) / (density_high - density_low))
     knot = jnp.clip(jnp.floor(position), 0.0, LUT - 1.0)
     offset = position - knot
@@ -236,27 +237,29 @@
             values = [jnp.where(bit, values[k + 1], values[k]) for k in range(0, len(values), 2)]
         return values[0]
 
+    def knots(channel):
+        both = pick(lambda k: tables[channel, k])
+        return (both & FIXED).astype(F32), lax.shift_right_logical(both, 16).astype(F32)
+
     result = []
     lower_scaled = lower_weight * (1.0 / FIXED)
     upper_scaled = upper_weight * (1.0 / FIXED)
     for channel in range(3):
-        both = pick(lambda k: colors[channel, k])
-        result.append(
-            lower_scaled * (both & FIXED).astype(F32)
-            + upper_scaled * lax.shift_right_logical(both, 16).astype(F32)
-        )
+        lower, upper = knots(channel)
+        result.append(lower_scaled * lower + upper_scaled * upper)
+    lower, upper = knots(3)
+    scale = EXTINCTION_TOP / (FIXED * FIXED)
     result.append(
-        lower_weight * pick(lambda k: extinctions[0, k])
-        + upper_weight * pick(lambda k: extinctions[1, k])
+        (lower_weight * scale) * (lower * lower) + (upper_weight * scale) * (upper * upper)
     )
     return result
 
 
-def classify(sp, xp, colors, extinctions, properties, own):
+def classify(sp, xp, tables, properties, own):
     for place in range(own + 1):
         span = pl.ds(place * SUBS, SUBS)
         kind = sp[span, :] if place < own else xp[6 * ABOVE].astype(jnp.int32)
-        found = lookup(properties[0, span, :], kind, colors, extinctions)
+        found = lookup(properties[0, span, :], kind, tables)
         for channel in range(4):
             properties[channel, span, :] = found[channel]
 
@@ -299,13 +302,10 @@
     grouped[...] = jnp.transpose(block)[: rows - 1]
 
 
-def half_kernel(u, g, xm, xp, zm, zp, color_rows, extinction_rows, h, colors, extinctions, z_edge):
+def half_kernel(u, g, xm, xp, zm, zp, table_rows, h, tables, z_edge):
     own = g.shape[0] // SUBS
-    for k in range(24):
-        colors[k // 8, k % 8] = jnp.broadcast_to(color_rows[pl.ds(k, 1), :], (SUBS, LANES))
-    for k in range(16):
-        row = extinction_rows[pl.ds(k, 1), :]
-        extinctions[k // 8, k % 8] = jnp.broadcast_to(row, (SUBS, LANES))
+    for k in range(32):
+        tables[k // 8, k % 8] = jnp.broadcast_to(table_rows[pl.ds(k, 1), :], (SUBS, LANES))
     up, down = halves((2,), [strips_of(zm, zp, f)[0] for f in range(6)])[0]
     for f in range(5):
         z_edge[f] = jnp.where(lanes() % 2 == 1, down[f], up[f])
@@ -323,7 +323,7 @@
 
 
 def step_kernel(
-    keep, u, g, sp, xm, xp, zm, zp, z_inner, y_low, y_high, ym, yp, partial, colors, extinctions,
+    keep, u, g, sp, xm, xp, zm, zp, z_inner, y_low, y_high, ym, yp, partial, tables,
     grouped, h, y_below2, y_above2, z_edge2, y_below, y_above, turned, properties
 ):
     own = g.shape[0] // SUBS
@@ -427,7 +427,7 @@
         return half_row(h, g, xm, xp, row)
 
     sweep(at_half, HALO, HALO + own, y_below2, y_above2, z_edge2, finish)
-    classify(sp, xp, colors, extinctions, properties, own)
+    classify(sp, xp, tables, properties, own)
     integrate(properties, grouped, own + 1, keep[0])
 
 
@@ -495,8 +495,9 @@
     zoom = SW // columns
     for tile in range(SW // LANES):
         pixel = iota((8, LANES), 1) + tile * LANES
-        source = pixel // zoom
-        offset = pixel.astype(F32) * (columns / SW) - source.astype(F32)
+        whole = jnp.floor((pixel.astype(F32) + 0.5) * (1.0 / zoom))
+        source = whole.astype(jnp.int32)
+        offset = pixel.astype(F32) * (columns / SW) - whole
         lower = jnp.maximum(0.0, 1.0 - jnp.abs(offset))
         upper = jnp.maximum(0.0, 1.0 - jnp.abs(offset - 1.0))
         for half in range(2):
@@ -530,12 +531,11 @@
     across_y = lax.axis_size("gy")
     across_z = lax.axis_size("gz")
 
-    fixed = jnp.round(jnp.clip(lut_color, 0.0, 1.0) * FIXED).astype(jnp.int32)
+    roots = jnp.sqrt(jnp.clip(lut_extinction, 0.0, EXTINCTION_TOP) * (1.0 / EXTINCTION_TOP))
+    values = jnp.concatenate([jnp.clip(lut_color, 0.0, 1.0), roots[:, None, :]], axis=1)
+    fixed = jnp.round(values * FIXED).astype(jnp.int32)
     following = jnp.pad(fixed[:, :, 1:], ((0, 0), (0, 0), (0, 1)))
-    color_rows = (fixed + lax.shift_left(following, 16)).transpose(1, 0, 2).reshape(24, LANES)
-    extinction_rows = jnp.stack(
-        [lut_extinction, jnp.pad(lut_extinction[:, 1:], ((0, 0), (0, 1)))]
-    ).reshape(16, LANES)
+    table_rows = (fixed + lax.shift_left(following, 16)).transpose(1, 0, 2).reshape(32, LANES)
 
     in_hbm = pl.BlockSpec(memory_space=pltpu.HBM)
     x_low, x_high = pl.pallas_call(
@@ -543,9 +543,12 @@
         out_shape=(struct(6 * ABOVE + 1, SUBS, LANES), struct(6 * HALO, SUBS, LANES)),
         in_specs=[in_hbm, in_hbm, in_hbm],
         scratch_shapes=[pltpu.VMEM((SUBS, LANES), jnp.int32), pltpu.SemaphoreType.DMA((13,))],
-        compiler_params=pltpu.CompilerParams(vmem_limit_bytes=60 * 1024 * 1024),
+        compiler_params=pltpu.CompilerParams(vmem_limit_bytes=VMEM_LIMIT),
         name="x_layers",
-    )(conserved, gamma_field, species)
+    )(*[pltpu.with_memory_space_constraint(q, pltpu.HBM) for q in (conserved, gamma_field, species)])
+    x_low, x_high, conserved, gamma_field = lax.optimization_barrier(
+        (x_low, x_high, conserved, gamma_field)
+    )
     xm = shifted(x_high, "gx", 1)
     xp = shifted(x_low, "gx", -1)
     brick = (
@@ -575,25 +578,24 @@
     ym = shifted(y_high, "gy", 1)
     yp = shifted(y_low, "gy", -1)
     every = cells + (HALO + ABOVE) * SUBS
-    partial, colors, extinctions = pl.pallas_call(
+    partial, tables = pl.pallas_call(
         half_kernel,
         out_shape=(
             struct(5, every, LANES),
-            jax.ShapeDtypeStruct((3, 8, SUBS, LANES), jnp.int32),
-            struct(2, 8, SUBS, LANES),
+            jax.ShapeDtypeStruct((4, 8, SUBS, LANES), jnp.int32),
         ),
         scratch_shapes=[pltpu.VMEM((5, SUBS, LANES), F32)],
         compiler_params=params,
         cost_estimate=cost(4_000_000),
         name="half",
-    )(*brick, xm, xp, zm, zp, color_rows, extinction_rows)
+    )(*brick, xm, xp, zm, zp, table_rows)
     layer = pltpu.VMEM((5, 40, LANES), F32)
     place = lax.axis_index("gx")
     keep = jnp.where(place == lax.axis_size("gx") - 1, 0.0, 1.0).reshape(1)
     vmem = pl.BlockSpec(memory_space=pltpu.VMEM)
     grouped, *halves_found = pl.pallas_call(
         step_kernel,
-        in_specs=[pl.BlockSpec(memory_space=pltpu.SMEM)] + [vmem] * 15,
+        in_specs=[pl.BlockSpec(memory_space=pltpu.SMEM)] + [vmem] * 14,
         out_shape=(
             struct(rows, LANES),
             struct(5, every, LANES),
@@ -623,8 +625,7 @@
         ym,
         yp,
         partial,
-        colors,
-        extinctions,
+        tables,
     )
     new_state = pl.pallas_call(
         state_kernel,

time: 41.7 us -> 40.5 us (0.971)
  Pallas kernels: 9.7 us -> 8.75 us
    pallas_call x1, Pallas kernels: 1.63 us -> 1 us  [local(): pl.pallas_call(x_kernel, out_shape=(struct(6 * ABOVE + 1, SUBS, LANES), s...]
where the time goes in v5:
time: 40.5 us; the launch traced here: 40.3 us
  starting transfers between devices  20.7 us (51%)
  waiting for transfers between devices  9.93 us (25%)
  Pallas kernels  8.75 us (22%)
  between operations  0.74 us (2%)
    ppermute x6, starting transfers between devices, shifted(): lax.ppermute(value, axis, [(i, (i + steps) % size) for i in range(size)])  13.6 us
    all_to_all x1, starting transfers between devices, local(): lax.all_to_all(grouped.reshape(across_y * across_z, 1, LANES), ('gy', 'gz...  7.16 us
    all_to_all x1, waiting for transfers between devices, local(): lax.all_to_all(grouped.reshape(across_y * across_z, 1, LANES), ('gy', 'gz...  5.14 us
    ppermute x6, waiting for transfers between devices, shifted(): lax.ppermute(value, axis, [(i, (i + steps) % size) for i in range(size)])  4.79 us
    pallas_call x1, Pallas kernels, local(): pl.pallas_call(step_kernel, in_specs=[pl.BlockSpec(memory_space=pltpu.SME...  3.06 us
    pallas_call x1, Pallas kernels, local(): pl.pallas_call(state_kernel, out_shape=struct(5, cells, LANES), compiler_...  1.71 us
    pallas_call x1, Pallas kernels, local(): pl.pallas_call(functools.partial(image_kernel, across_y, across_z), out_s...  1.24 us
    pallas_call x1, Pallas kernels, local(): pl.pallas_call(x_kernel, out_shape=(struct(6 * ABOVE + 1, SUBS, LANES), s...  1 us
  transfers between devices with their start and end apart: 7, of which 5 were waited for; matrix products, arithmetic and copies ran while one was open for 0% of the time, Pallas kernels for 8%

profile of v5, /device:TPU:1, one launch (start us, length us, event | category | flops | bytes accessed | tf_op | source)
XLA Modules:
  0.0 40.3 jit_solution(4917683503264035155)
XLA Ops:
  0.7 1.0 %x_layers.1 = (f32[19,8,128]{2,1,0:T(8,128)S(1)}, f32[12,8,128]{2,1,0:T(8,128)S(1)}) custom-call(f32[5,32,8,128]{3,2,1,0:T(8,128)} %u.1, f32[32,8,128]{2,1,0:T(8,128)} %g.1, s32[32,8,128]{2,1,0:T(8,128)} %sp.1), custom_call_target="tpu_custom_call" | custom-call | tf_op jit(solution)/shard_map/x_layers/pallas_call | solution.py:541
  1.7 2.5 %collective-permute-start = (f32[12,8,128]{2,1,0:T(8,128)S(1)}, f32[12,8,128]{2,1,0:T(8,128)S(1)}, u32[]{:S(2)}, u32[]{:S(2)}) collective-permute-start(f32[12,8,128]{2,1,0:T(8,128)S(1)} %get-tuple-element.27), channel_id=1, source_target_pairs={{0,32},{32,64},{64,96},{96,128},{128,160},{160,192},{192,224},{224... | collective-permute-start | bytes 147464 | tf_op jit(solution)/shard_map/ppermute | solution.py:516
  4.2 4.0 %collective-permute-start.1 = (f32[19,8,128]{2,1,0:T(8,128)S(1)}, f32[19,8,128]{2,1,0:T(8,128)S(1)}, u32[]{:S(2)}, u32[]{:S(2)}) collective-permute-start(f32[19,8,128]{2,1,0:T(8,128)S(1)} %get-tuple-element.28), channel_id=1, source_target_pairs={{0,224},{32,0},{64,32},{96,64},{128,96},{160,128},{192,160},{224,1... | collective-permute-start | bytes 233480 | tf_op jit(solution)/shard_map/ppermute | solution.py:516
  8.3 0.7 %own_strips.1 = (f32[6,8,128]{2,1,0:T(8,128)S(1)}, f32[6,8,128]{2,1,0:T(8,128)S(1)}, f32[6,8,128]{2,1,0:T(8,128)S(1)}) custom-call(f32[5,256,128]{2,1,0:T(8,128)S(1)} %bitcast.13, f32[256,128]{1,0:T(8,128)S(1)} %bitcast.18), custom_call_target="tpu_custom_call" | custom-call | flops 2000000 | bytes 2000000 | tf_op jit(solution)/shard_map/own_strips/pallas_call | solution.py:559
  8.9 0.7 %collective-permute-done.xm = f32[12,8,128]{2,1,0:T(8,128)S(1)} collective-permute-done((f32[12,8,128]{2,1,0:T(8,128)S(1)}, f32[12,8,128]{2,1,0:T(8,128)S(1)}, u32[]{:S(2)}, u32[]{:S(2)}) %collective-permute-start) | collective-permute-done | bytes 49184 | tf_op jit(solution)/shard_map/ppermute | solution.py:516
  9.6 0.1 collective-permute-done.1.xp
  9.7 0.1 strips.1
  9.8 1.4 %collective-permute-start.2 = (f32[6,8,128]{2,1,0:T(8,128)S(1)}, f32[6,8,128]{2,1,0:T(8,128)S(1)}, u32[]{:S(2)}, u32[]{:S(2)}) collective-permute-start(f32[6,8,128]{2,1,0:T(8,128)S(1)} %get-tuple-element.32), channel_id=1, source_target_pairs={{0,1},{1,2},{2,3},{3,0},{4,5},{5,6},{6,7},{7,4},{8,9},{9,10},{10,1... | collective-permute-start | bytes 73736 | tf_op jit(solution)/shard_map/ppermute | solution.py:516
  11.2 1.5 %collective-permute-start.3 = (f32[6,8,128]{2,1,0:T(8,128)S(1)}, f32[6,8,128]{2,1,0:T(8,128)S(1)}, u32[]{:S(2)}, u32[]{:S(2)}) collective-permute-start(f32[6,8,128]{2,1,0:T(8,128)S(1)} %get-tuple-element.33), channel_id=1, source_target_pairs={{0,3},{1,0},{2,1},{3,2},{4,7},{5,4},{6,5},{7,6},{8,11},{9,8},{10,9... | collective-permute-start | bytes 73736 | tf_op jit(solution)/shard_map/ppermute | solution.py:516
  12.8 1.1 %collective-permute-done.2.zm = f32[6,8,128]{2,1,0:T(8,128)S(1)} collective-permute-done((f32[6,8,128]{2,1,0:T(8,128)S(1)}, f32[6,8,128]{2,1,0:T(8,128)S(1)}, u32[]{:S(2)}, u32[]{:S(2)}) %collective-permute-start.2) | collective-permute-done | bytes 24608 | tf_op jit(solution)/shard_map/ppermute | solution.py:516
  13.9 0.0 collective-permute-done.3.zp
  13.9 0.1 layers.1
  14.0 3.0 %collective-permute-start.5 = (f32[6,72,128]{2,1,0:T(8,128)S(1)}, f32[6,72,128]{2,1,0:T(8,128)S(1)}, u32[]{:S(2)}, u32[]{:S(2)}) collective-permute-start(f32[6,72,128]{2,1,0:T(8,128)S(1)} %get-tuple-element.35.y_low), channel_id=1, source_target_pairs={{0,28},{4,0},{8,4},{12,8},{16,12},{20,16},{24,20},{28,24},{1,29},{... | collective-permute-start | bytes 663560 | tf_op jit(solution)/shard_map/ppermute | solution.py:516
  17.0 1.1 %collective-permute-start.4 = (f32[6,72,128]{2,1,0:T(8,128)S(1)}, f32[6,72,128]{2,1,0:T(8,128)S(1)}, u32[]{:S(2)}, u32[]{:S(2)}) collective-permute-start(f32[6,72,128]{2,1,0:T(8,128)S(1)} %get-tuple-element.36.y_high), channel_id=1, source_target_pairs={{0,4},{4,8},{8,12},{12,16},{16,20},{20,24},{24,28},{28,0},{1,5},{5... | collective-permute-start | bytes 663560 | tf_op jit(solution)/shard_map/ppermute | solution.py:516
  18.1 0.1 slice.4
  18.2 0.0 copy-start.2
  18.2 0.8 %half.1 = (f32[5,296,128]{2,1,0:T(8,128)S(1)}, s32[4,8,8,128]{3,2,1,0:T(8,128)S(1)}) custom-call(f32[5,256,128]{2,1,0:T(8,128)S(1)} %bitcast.15, f32[256,128]{1,0:T(8,128)S(1)} %bitcast.20, f32[12,8,128]{2,1,0:T(8,128)S(1)} %collective-permute-done.xm, f32[19,8,128]{2,1,0:T(8,128)S(1)} %collective-permute-done.1.xp, ...), custom_call_target="tpu_custom_call" | custom-call | flops 4000000 | bytes 4000000 | tf_op jit(solution)/shard_map/half/pallas_call | solution.py:581
  19.1 2.9 %collective-permute-done.5.yp = f32[6,72,128]{2,1,0:T(8,128)S(1)} collective-permute-done((f32[6,72,128]{2,1,0:T(8,128)S(1)}, f32[6,72,128]{2,1,0:T(8,128)S(1)}, u32[]{:S(2)}, u32[]{:S(2)}) %collective-permute-start.5) | collective-permute-done | bytes 221216 | tf_op jit(solution)/shard_map/ppermute | solution.py:516
  22.0 0.0 collective-permute-done.4.ym
  22.0 3.1 %density.1 = (f32[32,128]{1,0:T(8,128)}, f32[5,296,128]{2,1,0:T(8,128)S(1)}, f32[5,40,128]{2,1,0:T(8,128)S(1)}, f32[5,40,128]{2,1,0:T(8,128)S(1)}, f32[5,8,128]{2,1,0:T(8,128)S(1)}) custom-call(f32[1]{0:T(128)} %bitcast.2.keep, f32[5,256,128]{2,1,0:T(8,128)S(1)} %bitcast.16, f32[256,128]{1,0:T(8,128)S(1)} %bitcast.21, s32[256,128]{1,0:T(8,128)S(1)} %bitcast.23, ...), custom_call_target="tpu_custom_call" | custom-call | tf_op jit(solution)/shard_map/density/pallas_call | solution.py:596
  25.0 7.2 %all-to-all-start = ((f32[32,1,128]{2,1,0:T(1,128)}), f32[32,1,128]{2,1,0:T(1,128)S(1)}, u32[]{:S(2)}, u32[]{:S(2)}) async-start(f32[32,1,128]{2,1,0:T(1,128)} %bitcast.8), calls=%async_computation | async-start | bytes 32768 | tf_op jit(solution)/shard_map/all_to_all | solution.py:637
  32.2 1.7 %state.1 = f32[5,256,128]{2,1,0:T(8,128)} custom-call(f32[5,256,128]{2,1,0:T(8,128)S(1)} %bitcast.17, f32[256,128]{1,0:T(8,128)S(1)} %bitcast.22, f32[12,8,128]{2,1,0:T(8,128)S(1)} %collective-permute-done.xm, f32[19,8,128]{2,1,0:T(8,128)S(1)} %collective-permute-done.1.xp, f32[5,296,128]{2,1,0:T(8,128)S(1)} %get-tuple-element.39.h, ...), custom_call_target="tpu_custom_call" | custom-call | flops 6000000 | bytes 6000000 | tf_op jit(solution)/shard_map/state/pallas_call | solution.py:630
  33.9 5.1 %all-to-all-done = f32[32,1,128]{2,1,0:T(1,128)S(1)} async-done(((f32[32,1,128]{2,1,0:T(1,128)}), f32[32,1,128]{2,1,0:T(1,128)S(1)}, u32[]{:S(2)}, u32[]{:S(2)}) %all-to-all-start) | async-done | bytes 16416 | tf_op jit(solution)/shard_map/all_to_all | solution.py:637
  39.1 1.2 %image.1 = f32[4,4,1920]{2,1,0:T(4,128)} custom-call(f32[32,128]{1,0:T(8,128)S(1)} %bitcast.24), custom_call_target="tpu_custom_call" | custom-call | tf_op jit(solution)/shard_map/image/pallas_call | solution.py:640
  (14 shorter events, 0.1 us)
Async XLA Ops:
  0.6 7.6 %copy-start.1 = (f32[32,8,128]{2,1,0:T(8,128)S(1)}, f32[32,8,128]{2,1,0:T(8,128)}, u32[]{:S(2)}) copy-start(f32[32,8,128]{2,1,0:T(8,128)} %g.1) | copy-start | bytes 393220
  0.6 7.6 %copy-start = (f32[5,32,8,128]{3,2,1,0:T(8,128)S(1)}, f32[5,32,8,128]{3,2,1,0:T(8,128)}, u32[]{:S(2)}) copy-start(f32[5,32,8,128]{3,2,1,0:T(8,128)} %u.1) | copy-start | bytes 1966084
  0.6 7.6 %copy-start.3 = (f32[4,3,256]{2,0,1:T(4,128)S(1)}, f32[4,3,256]{2,0,1:T(4,128)}, u32[]{:S(2)}) copy-start(f32[4,3,256]{2,0,1:T(4,128)} %param.8) | copy-start | bytes 36868
  1.7 8.0 %collective-permute-start = (f32[12,8,128]{2,1,0:T(8,128)S(1)}, f32[12,8,128]{2,1,0:T(8,128)S(1)}, u32[]{:S(2)}, u32[]{:S(2)}) collective-permute-start(f32[12,8,128]{2,1,0:T(8,128)S(1)} %get-tuple-element.27), channel_id=1, source_target_pairs={{0,32},{32,64},{64,96},{96,128},{128,160},{160,192},{192,224},{224... | collective-permute-start | bytes 147464 | tf_op jit(solution)/shard_map/ppermute | solution.py:516
  4.2 5.5 %collective-permute-start.1 = (f32[19,8,128]{2,1,0:T(8,128)S(1)}, f32[19,8,128]{2,1,0:T(8,128)S(1)}, u32[]{:S(2)}, u32[]{:S(2)}) collective-permute-start(f32[19,8,128]{2,1,0:T(8,128)S(1)} %get-tuple-element.28), channel_id=1, source_target_pairs={{0,224},{32,0},{64,32},{96,64},{128,96},{160,128},{192,160},{224,1... | collective-permute-start | bytes 233480 | tf_op jit(solution)/shard_map/ppermute | solution.py:516
  9.7 3.1 %copy-start.4 = (f32[4,256]{1,0:T(4,128)S(1)}, f32[4,256]{1,0:T(4,128)}, u32[]{:S(2)}) copy-start(f32[4,256]{1,0:T(4,128)} %param.9) | copy-start | bytes 12292
  9.8 4.0 %collective-permute-start.2 = (f32[6,8,128]{2,1,0:T(8,128)S(1)}, f32[6,8,128]{2,1,0:T(8,128)S(1)}, u32[]{:S(2)}, u32[]{:S(2)}) collective-permute-start(f32[6,8,128]{2,1,0:T(8,128)S(1)} %get-tuple-element.32), channel_id=1, source_target_pairs={{0,1},{1,2},{2,3},{3,0},{4,5},{5,6},{6,7},{7,4},{8,9},{9,10},{10,1... | collective-permute-start | bytes 73736 | tf_op jit(solution)/shard_map/ppermute | solution.py:516
  11.2 2.7 %collective-permute-start.3 = (f32[6,8,128]{2,1,0:T(8,128)S(1)}, f32[6,8,128]{2,1,0:T(8,128)S(1)}, u32[]{:S(2)}, u32[]{:S(2)}) collective-permute-start(f32[6,8,128]{2,1,0:T(8,128)S(1)} %get-tuple-element.33), channel_id=1, source_target_pairs={{0,3},{1,0},{2,1},{3,2},{4,7},{5,4},{6,5},{7,6},{8,11},{9,8},{10,9... | collective-permute-start | bytes 73736 | tf_op jit(solution)/shard_map/ppermute | solution.py:516
  14.0 8.0 %collective-permute-start.5 = (f32[6,72,128]{2,1,0:T(8,128)S(1)}, f32[6,72,128]{2,1,0:T(8,128)S(1)}, u32[]{:S(2)}, u32[]{:S(2)}) collective-permute-start(f32[6,72,128]{2,1,0:T(8,128)S(1)} %get-tuple-element.35.y_low), channel_id=1, source_target_pairs={{0,28},{4,0},{8,4},{12,8},{16,12},{20,16},{24,20},{28,24},{1,29},{... | collective-permute-start | bytes 663560 | tf_op jit(solution)/shard_map/ppermute | solution.py:516
  17.0 5.0 %collective-permute-start.4 = (f32[6,72,128]{2,1,0:T(8,128)S(1)}, f32[6,72,128]{2,1,0:T(8,128)S(1)}, u32[]{:S(2)}, u32[]{:S(2)}) collective-permute-start(f32[6,72,128]{2,1,0:T(8,128)S(1)} %get-tuple-element.36.y_high), channel_id=1, source_target_pairs={{0,4},{4,8},{8,12},{12,16},{16,20},{20,24},{24,28},{28,0},{1,5},{5... | collective-permute-start | bytes 663560 | tf_op jit(solution)/shard_map/ppermute | solution.py:516
  18.2 3.8 %copy-start.2 = (s32[32,8,128]{2,1,0:T(8,128)S(1)}, s32[32,8,128]{2,1,0:T(8,128)}, u32[]{:S(2)}) copy-start(s32[32,8,128]{2,1,0:T(8,128)} %sp.1) | copy-start | bytes 393220
  25.0 14.0 %all-to-all-start = ((f32[32,1,128]{2,1,0:T(1,128)}), f32[32,1,128]{2,1,0:T(1,128)S(1)}, u32[]{:S(2)}, u32[]{:S(2)}) async-start(f32[32,1,128]{2,1,0:T(1,128)} %bitcast.8), calls=%async_computation | async-start | bytes 32768 | tf_op jit(solution)/shard_map/all_to_all | solution.py:637

commit v6 on v5

--- a/solution.py
+++ b/solution.py
@@ -22,7 +22,7 @@
 F32 = jnp.float32
 LANES = 128
 SUBS = 8
-VMEM_LIMIT = 48 * 1024 * 1024
+VMEM_LIMIT = 51 * 1024 * 1024
 
 
 def iota(shape, dim):
@@ -173,26 +173,40 @@
     return first, second
 
 
-def y_kernel(u, g, xm, xp, zm, zp, y_low, y_high):
+def y_kernel(u, g, xm, xp, zm, zp, partial, y_low, y_high, h):
     own = g.shape[0] // SUBS
     every = own + HALO + ABOVE
+    odd = lanes() % 2 == 1
+    ends = (lanes() == 0) | (lanes() == LANES - 1)
+    first = [strips_of(zm, zp, f)[0] for f in range(6)]
+    up, down = halves((2,), first)[0]
+    for f in range(5):
+        added = courant * jnp.where(odd, down[f], -up[f])
+        for row in (0, every - 1):
+            h[f, pl.ds(row * SUBS, SUBS), :] = jnp.ones((SUBS, LANES), F32)
+        for row in range(1, every - 1):
+            span = pl.ds(row * SUBS, SUBS)
+            end = pltpu.roll(added, LANES - 1 - 2 * row, 1)
+            h[f, span, :] = partial[f, span, :] + jnp.where(ends, end, 0.0)
     for f in range(6):
-        first, _ = strips_of(zm, zp, f)
-        for message, near, far in ((y_low, 0, 1), (y_high, SUBS - 1, SUBS - 2)):
-            for at, sub, start, stop in (
-                (0, far, HALO, HALO + own + 1),
-                (FIRST_AT, near, 0, every),
-            ):
-                for row in range(start, stop):
-                    if HALO <= row < HALO + own:
-                        continue
-                    line = row_of(u, g, xm, xp, f, row)[sub : sub + 1, :]
-                    message[f, pl.ds(at + row - start, 1), :] = line
-                span = pl.ds(sub, own, stride=SUBS)
-                block = u[f, span, :] if f < 5 else g[span, :]
-                message[f, pl.ds(at + HALO - start, own), :] = block
-            message[f, pl.ds(STRIP_AT, 1), :] = first[near : near + 1, :]
-            message[f, pl.ds(STRIP_AT + 1, 1), :] = first[near : near + 1, :]
+        for message, near in ((y_low, 0), (y_high, SUBS - 1)):
+            for row in range(every):
+                if HALO <= row < HALO + own:
+                    continue
+                line = row_of(u, g, xm, xp, f, row)[near : near + 1, :]
+                message[f, pl.ds(FIRST_AT + row, 1), :] = line
+            span = pl.ds(near, own, stride=SUBS)
+            block = u[f, span, :] if f < 5 else g[span, :]
+            message[f, pl.ds(FIRST_AT + HALO, own), :] = block
+            if f < 5:
+                message[f, pl.ds(0, own), :] = h[f, pl.ds(HALO * SUBS + near, own, stride=SUBS), :]
+                last = (HALO + own) * SUBS + near
+                message[f, pl.ds(own, 1), :] = h[f, pl.ds(last, 1), :]
+            else:
+                message[f, pl.ds(0, own + 1), :] = jnp.ones((own + 1, LANES), F32)
+            strip = first[f][near : near + 1, :]
+            message[f, pl.ds(STRIP_AT, 1), :] = strip
+            message[f, pl.ds(STRIP_AT + 1, 1), :] = strip
 
 
 def sweep(load, first, last, y_below, y_above, z_edge, finish):
@@ -203,7 +217,10 @@
         (x_up, x_down), (y_up, y_down), (z_up, z_down) = halves((0, 1, 2), cell)
         if pending is not None:
             finish(row - 1, [a + b for a, b in zip(pending, x_up)])
-        edge = [pltpu.roll(z_edge[f], LANES - 1 - 2 * row, 1) for f in range(5)]
+        if z_edge is None:
+            edge = [0.0] * 5
+        else:
+            edge = [pltpu.roll(z_edge[f], LANES - 1 - 2 * row, 1) for f in range(5)]
         if y_below is None:
             below = above = [0.0] * 5
         else:
@@ -302,14 +319,10 @@
     grouped[...] = jnp.transpose(block)[: rows - 1]
 
 
-def half_kernel(u, g, xm, xp, zm, zp, table_rows, h, tables, z_edge):
+def half_kernel(u, g, xm, xp, table_rows, h, tables):
     own = g.shape[0] // SUBS
     for k in range(32):
         tables[k // 8, k % 8] = jnp.broadcast_to(table_rows[pl.ds(k, 1), :], (SUBS, LANES))
-    up, down = halves((2,), [strips_of(zm, zp, f)[0] for f in range(6)])[0]
-    for f in range(5):
-        z_edge[f] = jnp.where(lanes() % 2 == 1, down[f], up[f])
-
     def at_first(row):
         return [row_of(u, g, xm, xp, f, row) for f in range(6)]
 
@@ -319,12 +332,12 @@
                 row_of(u, g, xm, xp, f, row) - courant * change[f]
             )
 
-    sweep(at_first, 1, HALO + own + 1, None, None, z_edge, store_half)
+    sweep(at_first, 1, HALO + own + 1, None, None, None, store_half)
 
 
 def step_kernel(
     keep, u, g, sp, xm, xp, zm, zp, z_inner, y_low, y_high, ym, yp, partial, tables,
-    grouped, h, y_below2, y_above2, z_edge2, y_below, y_above, turned, properties
+    grouped, h, y_below2, y_above2, z_edge2, y_below, y_above, properties
 ):
     own = g.shape[0] // SUBS
     odd = lanes() % 2 == 1
@@ -349,8 +362,8 @@
         )
         for f in range(6)
     ]
-    (corner_up, corner_down), (corner_zup, corner_zdown) = halves((1, 2), corner)
-    (x_up, x_down), (y_up, y_down), (z_up, z_down) = halves((0, 1, 2), first)
+    corner_up, corner_down = halves((1,), corner)[0]
+    (x_up, x_down), (y_up, y_down) = halves((0, 1), first)
     from_above = up_of(2, [jnp.where(odd, a, b) for a, b in zip(inner, second)])
     from_below = down_of(2, [jnp.where(odd, a, b) for a, b in zip(second, inner)])
     change = total_change(
@@ -369,45 +382,18 @@
     for f in range(5):
         z_edge2[f] = jnp.where(odd, down[f], up[f])
 
-    ends = [jnp.where(odd, corner_zdown[f], corner_zup[f]) for f in range(5)]
-    turned[...] = jnp.transpose(
-        jnp.concatenate(ends + [jnp.zeros((LANES - 5 * SUBS, LANES), F32)], axis=0)
-    )
     for start in (2, 10, 18, 26, 27):
-        z_high_end = turned[pl.ds(2 * start, SUBS, stride=2), :]
-        z_low_end = turned[pl.ds(2 * start + 1, SUBS, stride=2), :]
-        for message, mine, lower in ((ym, y_low, True), (yp, y_high, False)):
-            at = FIRST_AT + start
-            cell = [message[f, pl.ds(at, SUBS), :] for f in range(6)]
-            x_up = up_of(0, [message[f, pl.ds(at + 1, SUBS), :] for f in range(6)])
-            x_down = down_of(0, [message[f, pl.ds(at - 1, SUBS), :] for f in range(6)])
-            near = [mine[f, pl.ds(at, SUBS), :] for f in range(6)]
-            far = [message[f, pl.ds(start - HALO, SUBS), :] for f in range(6)]
-            above, below = (near, far) if lower else (far, near)
-            z_up, z_down = halves((2,), cell)[0]
-            shift = 0 if lower else SUBS - 1
-            low_end = [
-                pltpu.roll(z_low_end, (LANES - f * SUBS - shift) % LANES, 1)
-                if f * SUBS + shift
-                else z_low_end
-                for f in range(5)
-            ]
-            high_end = [
-                pltpu.roll(z_high_end, LANES - 1 - f * SUBS - shift, 1) for f in range(5)
-            ]
-            change = total_change(
-                cell,
-                (
-                    (x_up, x_down),
-                    (up_of(1, above), down_of(1, below)),
-                    along_z(z_up, z_down, low_end, high_end),
-                ),
-            )
-            halfway = [cell[f] - courant * change[f] for f in range(5)] + [cell[5]]
-            part = down_of(1, halfway) if lower else up_of(1, halfway)
-            target = y_below2 if lower else y_above2
-            for f in range(5):
-                target[f, pl.ds(start, SUBS), :] = part[f]
+        span = pl.ds(FIRST_AT + start, SUBS)
+        before = pl.ds(start - HALO, SUBS)
+        near = up_of(1, [y_low[f, span, :] for f in range(6)])
+        halfway = [ym[f, before, :] - courant * near[f] for f in range(5)] + [ym[5, span, :]]
+        part = down_of(1, halfway)
+        near = down_of(1, [y_high[f, span, :] for f in range(6)])
+        halfway = [yp[f, before, :] + courant * near[f] for f in range(5)] + [yp[5, span, :]]
+        above = up_of(1, halfway)
+        for f in range(5):
+            y_below2[f, pl.ds(start, SUBS), :] = part[f]
+            y_above2[f, pl.ds(start, SUBS), :] = above[f]
 
     for row in range(1, HALO + own + 2):
         span = pl.ds(row * SUBS, SUBS)
@@ -571,12 +557,6 @@
     )(xm, xp, *own_parts)
     zm = shifted(z_up, "gz", 1)
     zp = shifted(z_down, "gz", -1)
-    message = struct(6, MESSAGE_ROWS, LANES)
-    y_low, y_high = pl.pallas_call(
-        y_kernel, out_shape=(message, message), compiler_params=params, name="layers"
-    )(*brick, xm, xp, zm, zp)
-    ym = shifted(y_high, "gy", 1)
-    yp = shifted(y_low, "gy", -1)
     every = cells + (HALO + ABOVE) * SUBS
     partial, tables = pl.pallas_call(
         half_kernel,
@@ -584,11 +564,19 @@
             struct(5, every, LANES),
             jax.ShapeDtypeStruct((4, 8, SUBS, LANES), jnp.int32),
         ),
-        scratch_shapes=[pltpu.VMEM((5, SUBS, LANES), F32)],
         compiler_params=params,
         cost_estimate=cost(4_000_000),
         name="half",
-    )(*brick, xm, xp, zm, zp, table_rows)
+    )(*brick, xm, xp, table_rows)
+    message = struct(6, MESSAGE_ROWS, LANES)
+    y_low, y_high, partial = pl.pallas_call(
+        y_kernel,
+        out_shape=(message, message, struct(5, every, LANES)),
+        compiler_params=params,
+        name="layers",
+    )(*brick, xm, xp, zm, zp, partial)
+    ym = shifted(y_high, "gy", 1)
+    yp = shifted(y_low, "gy", -1)
     layer = pltpu.VMEM((5, 40, LANES), F32)
     place = lax.axis_index("gx")
     keep = jnp.where(place == lax.axis_size("gx") - 1, 0.0, 1.0).reshape(1)
@@ -606,7 +594,6 @@
         scratch_shapes=[
             layer,
             layer,
-            pltpu.VMEM((LANES, LANES), F32),
             pltpu.VMEM((4, cells + SUBS, LANES), F32),
         ],
         compiler_params=params,

time: 40.5 us -> 42.4 us (1.047)
  local copies, waits for them, and re-layouts: 0.11 us -> 2.1 us
  waiting for transfers between devices: 9.93 us -> 8.89 us
  Pallas kernels: 8.75 us -> 9.74 us
    unnamed x10 -> x14, local copies, waits for them, and re-layouts: 0.02 us -> 2.01 us
    all_to_all x1, waiting for transfers between devices: 5.14 us -> 4.05 us  [local(): lax.all_to_all(grouped.reshape(across_y * across_z, 1, LANES), ('gy', 'gz...]
    pallas_call x1, Pallas kernels: 3.06 us -> 3.89 us  [local(): pl.pallas_call(step_kernel, in_specs=[pl.BlockSpec(memory_space=pltpu.SME...]
where the time goes in v6:
time: 42.4 us; the launch traced here: 42.2 us
  starting transfers between devices  20.7 us (49%)
  Pallas kernels  9.74 us (23%)
  waiting for transfers between devices  8.89 us (21%)
  local copies, waits for them, and re-layouts  2.1 us (5%)
  between operations  0.76 us (2%)
    ppermute x6, starting transfers between devices, shifted(): lax.ppermute(value, axis, [(i, (i + steps) % size) for i in range(size)])  13.5 us
    all_to_all x1, starting transfers between devices, local(): lax.all_to_all(grouped.reshape(across_y * across_z, 1, LANES), ('gy', 'gz...  7.14 us
    ppermute x6, waiting for transfers between devices, shifted(): lax.ppermute(value, axis, [(i, (i + steps) % size) for i in range(size)])  4.84 us
    all_to_all x1, waiting for transfers between devices, local(): lax.all_to_all(grouped.reshape(across_y * across_z, 1, LANES), ('gy', 'gz...  4.05 us
    pallas_call x1, Pallas kernels, local(): pl.pallas_call(step_kernel, in_specs=[pl.BlockSpec(memory_space=pltpu.SME...  3.89 us
    unnamed x14, local copies, waits for them, and re-layouts  2.01 us
    pallas_call x1, Pallas kernels, local(): pl.pallas_call(state_kernel, out_shape=struct(5, cells, LANES), compiler_...  1.67 us
    pallas_call x1, Pallas kernels, local(): pl.pallas_call(functools.partial(image_kernel, across_y, across_z), out_s...  1.24 us
  transfers between devices with their start and end apart: 7, of which 5 were waited for; matrix products, arithmetic and copies ran while one was open for 0% of the time, Pallas kernels for 8%

profile of v6, /device:TPU:1, one launch (start us, length us, event | category | flops | bytes accessed | tf_op | source)
XLA Modules:
  0.0 42.2 jit_solution(14759806770552251152)
XLA Ops:
  0.7 1.0 %x_layers.1 = (f32[19,8,128]{2,1,0:T(8,128)S(1)}, f32[12,8,128]{2,1,0:T(8,128)S(1)}) custom-call(f32[5,32,8,128]{3,2,1,0:T(8,128)} %u.1, f32[32,8,128]{2,1,0:T(8,128)} %g.1, s32[32,8,128]{2,1,0:T(8,128)} %sp.1), custom_call_target="tpu_custom_call" | custom-call | tf_op jit(solution)/shard_map/x_layers/pallas_call | solution.py:527
  1.7 2.5 %collective-permute-start = (f32[12,8,128]{2,1,0:T(8,128)S(1)}, f32[12,8,128]{2,1,0:T(8,128)S(1)}, u32[]{:S(2)}, u32[]{:S(2)}) collective-permute-start(f32[12,8,128]{2,1,0:T(8,128)S(1)} %get-tuple-element.28), channel_id=1, source_target_pairs={{0,32},{32,64},{64,96},{96,128},{128,160},{160,192},{192,224},{224... | collective-permute-start | bytes 147464 | tf_op jit(solution)/shard_map/ppermute | solution.py:502
  4.2 4.0 %collective-permute-start.1 = (f32[19,8,128]{2,1,0:T(8,128)S(1)}, f32[19,8,128]{2,1,0:T(8,128)S(1)}, u32[]{:S(2)}, u32[]{:S(2)}) collective-permute-start(f32[19,8,128]{2,1,0:T(8,128)S(1)} %get-tuple-element.29), channel_id=1, source_target_pairs={{0,224},{32,0},{64,32},{96,64},{128,96},{160,128},{192,160},{224,1... | collective-permute-start | bytes 233480 | tf_op jit(solution)/shard_map/ppermute | solution.py:502
  8.3 0.1 slice.4
  8.4 0.7 %own_strips.1 = (f32[6,8,128]{2,1,0:T(8,128)S(1)}, f32[6,8,128]{2,1,0:T(8,128)S(1)}, f32[6,8,128]{2,1,0:T(8,128)S(1)}) custom-call(f32[5,256,128]{2,1,0:T(8,128)S(1)} %bitcast.13, f32[256,128]{1,0:T(8,128)S(1)} %bitcast.18), custom_call_target="tpu_custom_call" | custom-call | flops 2000000 | bytes 2000000 | tf_op jit(solution)/shard_map/own_strips/pallas_call | solution.py:545
  9.0 0.6 %collective-permute-done.xm = f32[12,8,128]{2,1,0:T(8,128)S(1)} collective-permute-done((f32[12,8,128]{2,1,0:T(8,128)S(1)}, f32[12,8,128]{2,1,0:T(8,128)S(1)}, u32[]{:S(2)}, u32[]{:S(2)}) %collective-permute-start) | collective-permute-done | bytes 49184 | tf_op jit(solution)/shard_map/ppermute | solution.py:502
  9.6 0.1 collective-permute-done.1.xp
  9.7 0.1 strips.1
  9.8 1.4 %collective-permute-start.2 = (f32[6,8,128]{2,1,0:T(8,128)S(1)}, f32[6,8,128]{2,1,0:T(8,128)S(1)}, u32[]{:S(2)}, u32[]{:S(2)}) collective-permute-start(f32[6,8,128]{2,1,0:T(8,128)S(1)} %get-tuple-element.33), channel_id=1, source_target_pairs={{0,1},{1,2},{2,3},{3,0},{4,5},{5,6},{6,7},{7,4},{8,9},{9,10},{10,1... | collective-permute-start | bytes 73736 | tf_op jit(solution)/shard_map/ppermute | solution.py:502
  11.2 1.5 %collective-permute-start.3 = (f32[6,8,128]{2,1,0:T(8,128)S(1)}, f32[6,8,128]{2,1,0:T(8,128)S(1)}, u32[]{:S(2)}, u32[]{:S(2)}) collective-permute-start(f32[6,8,128]{2,1,0:T(8,128)S(1)} %get-tuple-element.34), channel_id=1, source_target_pairs={{0,3},{1,0},{2,1},{3,2},{4,7},{5,4},{6,5},{7,6},{8,11},{9,8},{10,9... | collective-permute-start | bytes 73736 | tf_op jit(solution)/shard_map/ppermute | solution.py:502
  12.8 0.8 %half.1 = (f32[5,296,128]{2,1,0:T(8,128)S(1)}, s32[4,8,8,128]{3,2,1,0:T(8,128)S(1)}) custom-call(f32[5,256,128]{2,1,0:T(8,128)S(1)} %bitcast.14, f32[256,128]{1,0:T(8,128)S(1)} %bitcast.19, f32[12,8,128]{2,1,0:T(8,128)S(1)} %collective-permute-done.xm, f32[19,8,128]{2,1,0:T(8,128)S(1)} %collective-permute-done.1.xp, s32[32,128]{1,0:T(8,128)S(1)} %reshape.32.table_rows), custom_call_target="tpu_custom_call" | custom-call | flops 4000000 | bytes 4000000 | tf_op jit(solution)/shard_map/half/pallas_call | solution.py:561
  13.6 0.3 collective-permute-done.2.zm
  13.9 0.0 collective-permute-done.3.zp
  13.9 0.3 layers.1
  14.2 0.9 %copy-done.2 = f32[5,296,128]{2,1,0:T(8,128)} copy-done((f32[5,296,128]{2,1,0:T(8,128)}, f32[5,296,128]{2,1,0:T(8,128)S(1)}, u32[]{:S(2)}) %copy-start.2) | copy-done | bytes 757784
  15.1 3.0 %collective-permute-start.5 = (f32[6,72,128]{2,1,0:T(8,128)S(1)}, f32[6,72,128]{2,1,0:T(8,128)S(1)}, u32[]{:S(2)}, u32[]{:S(2)}) collective-permute-start(f32[6,72,128]{2,1,0:T(8,128)S(1)} %get-tuple-element.37.y_low), channel_id=1, source_target_pairs={{0,28},{4,0},{8,4},{12,8},{16,12},{20,16},{24,20},{28,24},{1,29},{... | collective-permute-start | bytes 663560 | tf_op jit(solution)/shard_map/ppermute | solution.py:502
  18.0 1.1 %collective-permute-start.4 = (f32[6,72,128]{2,1,0:T(8,128)S(1)}, f32[6,72,128]{2,1,0:T(8,128)S(1)}, u32[]{:S(2)}, u32[]{:S(2)}) collective-permute-start(f32[6,72,128]{2,1,0:T(8,128)S(1)} %get-tuple-element.38.y_high), channel_id=1, source_target_pairs={{0,4},{4,8},{8,12},{12,16},{16,20},{20,24},{24,28},{28,0},{1,5},{5... | collective-permute-start | bytes 663560 | tf_op jit(solution)/shard_map/ppermute | solution.py:502
  19.1 3.9 %collective-permute-done.5.yp = f32[6,72,128]{2,1,0:T(8,128)S(1)} collective-permute-done((f32[6,72,128]{2,1,0:T(8,128)S(1)}, f32[6,72,128]{2,1,0:T(8,128)S(1)}, u32[]{:S(2)}, u32[]{:S(2)}) %collective-permute-start.5) | collective-permute-done | bytes 221216 | tf_op jit(solution)/shard_map/ppermute | solution.py:502
  23.1 3.9 %density.1 = (f32[32,128]{1,0:T(8,128)}, f32[5,296,128]{2,1,0:T(8,128)}, f32[5,40,128]{2,1,0:T(8,128)S(1)}, f32[5,40,128]{2,1,0:T(8,128)S(1)}, f32[5,8,128]{2,1,0:T(8,128)S(1)}) custom-call(f32[1]{0:T(128)} %bitcast.2.keep, f32[5,256,128]{2,1,0:T(8,128)S(1)} %bitcast.16, f32[256,128]{1,0:T(8,128)S(1)} %bitcast.21, s32[256,128]{1,0:T(8,128)S(1)} %bitcast.23, ...), custom_call_target="tpu_custom_call" | custom-call | tf_op jit(solution)/shard_map/density/pallas_call | solution.py:584
  27.0 7.1 %all-to-all-start = ((f32[32,1,128]{2,1,0:T(1,128)}), f32[32,1,128]{2,1,0:T(1,128)S(1)}, u32[]{:S(2)}, u32[]{:S(2)}) async-start(f32[32,1,128]{2,1,0:T(1,128)} %bitcast.8), calls=%async_computation | async-start | bytes 32768 | tf_op jit(solution)/shard_map/all_to_all | solution.py:624
  34.1 1.1 %copy-done.3 = f32[5,296,128]{2,1,0:T(8,128)S(1)} copy-done((f32[5,296,128]{2,1,0:T(8,128)S(1)}, f32[5,296,128]{2,1,0:T(8,128)}, u32[]{:S(2)}) %copy-start.3) | copy-done | bytes 757784
  35.2 1.7 %state.1 = f32[5,256,128]{2,1,0:T(8,128)} custom-call(f32[5,256,128]{2,1,0:T(8,128)S(1)} %bitcast.17, f32[256,128]{1,0:T(8,128)S(1)} %bitcast.22, f32[12,8,128]{2,1,0:T(8,128)S(1)} %collective-permute-done.xm, f32[19,8,128]{2,1,0:T(8,128)S(1)} %collective-permute-done.1.xp, f32[5,296,128]{2,1,0:T(8,128)S(1)} %copy-done.3, ...), custom_call_target="tpu_custom_call" | custom-call | flops 6000000 | bytes 6000000 | tf_op jit(solution)/shard_map/state/pallas_call | solution.py:617
  36.9 4.1 %all-to-all-done = f32[32,1,128]{2,1,0:T(1,128)S(1)} async-done(((f32[32,1,128]{2,1,0:T(1,128)}), f32[32,1,128]{2,1,0:T(1,128)S(1)}, u32[]{:S(2)}, u32[]{:S(2)}) %all-to-all-start) | async-done | bytes 16416 | tf_op jit(solution)/shard_map/all_to_all | solution.py:624
  41.0 1.2 %image.1 = f32[4,4,1920]{2,1,0:T(4,128)} custom-call(f32[32,128]{1,0:T(8,128)S(1)} %bitcast.24), custom_call_target="tpu_custom_call" | custom-call | tf_op jit(solution)/shard_map/image/pallas_call | solution.py:627
  (18 shorter events, 0.1 us)
Async XLA Ops:
  0.6 7.7 %copy-start = (f32[5,32,8,128]{3,2,1,0:T(8,128)S(1)}, f32[5,32,8,128]{3,2,1,0:T(8,128)}, u32[]{:S(2)}) copy-start(f32[5,32,8,128]{3,2,1,0:T(8,128)} %u.1) | copy-start | bytes 1966084
  0.6 7.6 %copy-start.6 = (f32[4,256]{1,0:T(4,128)S(1)}, f32[4,256]{1,0:T(4,128)}, u32[]{:S(2)}) copy-start(f32[4,256]{1,0:T(4,128)} %param.9) | copy-start | bytes 12292
  0.7 7.6 %copy-start.5 = (f32[4,3,256]{2,0,1:T(4,128)S(1)}, f32[4,3,256]{2,0,1:T(4,128)}, u32[]{:S(2)}) copy-start(f32[4,3,256]{2,0,1:T(4,128)} %param.8) | copy-start | bytes 36868
  0.7 7.7 %copy-start.1 = (f32[32,8,128]{2,1,0:T(8,128)S(1)}, f32[32,8,128]{2,1,0:T(8,128)}, u32[]{:S(2)}) copy-start(f32[32,8,128]{2,1,0:T(8,128)} %g.1) | copy-start | bytes 393220
  1.7 8.0 %collective-permute-start = (f32[12,8,128]{2,1,0:T(8,128)S(1)}, f32[12,8,128]{2,1,0:T(8,128)S(1)}, u32[]{:S(2)}, u32[]{:S(2)}) collective-permute-start(f32[12,8,128]{2,1,0:T(8,128)S(1)} %get-tuple-element.28), channel_id=1, source_target_pairs={{0,32},{32,64},{64,96},{96,128},{128,160},{160,192},{192,224},{224... | collective-permute-start | bytes 147464 | tf_op jit(solution)/shard_map/ppermute | solution.py:502
  4.2 5.5 %collective-permute-start.1 = (f32[19,8,128]{2,1,0:T(8,128)S(1)}, f32[19,8,128]{2,1,0:T(8,128)S(1)}, u32[]{:S(2)}, u32[]{:S(2)}) collective-permute-start(f32[19,8,128]{2,1,0:T(8,128)S(1)} %get-tuple-element.29), channel_id=1, source_target_pairs={{0,224},{32,0},{64,32},{96,64},{128,96},{160,128},{192,160},{224,1... | collective-permute-start | bytes 233480 | tf_op jit(solution)/shard_map/ppermute | solution.py:502
  9.8 4.0 %collective-permute-start.2 = (f32[6,8,128]{2,1,0:T(8,128)S(1)}, f32[6,8,128]{2,1,0:T(8,128)S(1)}, u32[]{:S(2)}, u32[]{:S(2)}) collective-permute-start(f32[6,8,128]{2,1,0:T(8,128)S(1)} %get-tuple-element.33), channel_id=1, source_target_pairs={{0,1},{1,2},{2,3},{3,0},{4,5},{5,6},{6,7},{7,4},{8,9},{9,10},{10,1... | collective-permute-start | bytes 73736 | tf_op jit(solution)/shard_map/ppermute | solution.py:502
  11.2 2.7 %collective-permute-start.3 = (f32[6,8,128]{2,1,0:T(8,128)S(1)}, f32[6,8,128]{2,1,0:T(8,128)S(1)}, u32[]{:S(2)}, u32[]{:S(2)}) collective-permute-start(f32[6,8,128]{2,1,0:T(8,128)S(1)} %get-tuple-element.34), channel_id=1, source_target_pairs={{0,3},{1,0},{2,1},{3,2},{4,7},{5,4},{6,5},{7,6},{8,11},{9,8},{10,9... | collective-permute-start | bytes 73736 | tf_op jit(solution)/shard_map/ppermute | solution.py:502
  13.9 9.2 %copy-start.4 = (s32[32,8,128]{2,1,0:T(8,128)S(1)}, s32[32,8,128]{2,1,0:T(8,128)}, u32[]{:S(2)}) copy-start(s32[32,8,128]{2,1,0:T(8,128)} %sp.1) | copy-start | bytes 393220
  14.2 0.9 %copy-start.2 = (f32[5,296,128]{2,1,0:T(8,128)}, f32[5,296,128]{2,1,0:T(8,128)S(1)}, u32[]{:S(2)}) copy-start(f32[5,296,128]{2,1,0:T(8,128)S(1)} %get-tuple-element.39.partial) | copy-start | bytes 2273284
  15.1 8.0 %collective-permute-start.5 = (f32[6,72,128]{2,1,0:T(8,128)S(1)}, f32[6,72,128]{2,1,0:T(8,128)S(1)}, u32[]{:S(2)}, u32[]{:S(2)}) collective-permute-start(f32[6,72,128]{2,1,0:T(8,128)S(1)} %get-tuple-element.37.y_low), channel_id=1, source_target_pairs={{0,28},{4,0},{8,4},{12,8},{16,12},{20,16},{24,20},{28,24},{1,29},{... | collective-permute-start | bytes 663560 | tf_op jit(solution)/shard_map/ppermute | solution.py:502
  18.0 5.0 %collective-permute-start.4 = (f32[6,72,128]{2,1,0:T(8,128)S(1)}, f32[6,72,128]{2,1,0:T(8,128)S(1)}, u32[]{:S(2)}, u32[]{:S(2)}) collective-permute-start(f32[6,72,128]{2,1,0:T(8,128)S(1)} %get-tuple-element.38.y_high), channel_id=1, source_target_pairs={{0,4},{4,8},{8,12},{12,16},{16,20},{20,24},{24,28},{28,0},{1,5},{5... | collective-permute-start | bytes 663560 | tf_op jit(solution)/shard_map/ppermute | solution.py:502
  27.0 14.0 %all-to-all-start = ((f32[32,1,128]{2,1,0:T(1,128)}), f32[32,1,128]{2,1,0:T(1,128)S(1)}, u32[]{:S(2)}, u32[]{:S(2)}) async-start(f32[32,1,128]{2,1,0:T(1,128)} %bitcast.8), calls=%async_computation | async-start | bytes 32768 | tf_op jit(solution)/shard_map/all_to_all | solution.py:624
  34.1 1.1 %copy-start.3 = (f32[5,296,128]{2,1,0:T(8,128)S(1)}, f32[5,296,128]{2,1,0:T(8,128)}, u32[]{:S(2)}) copy-start(f32[5,296,128]{2,1,0:T(8,128)} %get-tuple-element.41.h) | copy-start | bytes 2273284

commit v7 on v6

--- a/solution.py
+++ b/solution.py
@@ -173,12 +173,17 @@
     return first, second
 
 
-def y_kernel(u, g, xm, xp, zm, zp, partial, y_low, y_high, h):
+def y_kernel(u, g, xm, xp, zm, zp, partial, y_low, y_high, h, strip_pairs):
     own = g.shape[0] // SUBS
     every = own + HALO + ABOVE
     odd = lanes() % 2 == 1
     ends = (lanes() == 0) | (lanes() == LANES - 1)
-    first = [strips_of(zm, zp, f)[0] for f in range(6)]
+    first = []
+    for f in range(6):
+        near, far = strips_of(zm, zp, f)
+        first.append(near)
+        strip_pairs[f] = near
+        strip_pairs[6 + f] = far
     up, down = halves((2,), first)[0]
     for f in range(5):
         added = courant * jnp.where(odd, down[f], -up[f])
@@ -336,7 +341,7 @@
 
 
 def step_kernel(
-    keep, u, g, sp, xm, xp, zm, zp, z_inner, y_low, y_high, ym, yp, partial, tables,
+    keep, u, g, sp, xm, xp, strip_pairs, z_inner, y_low, y_high, ym, yp, partial, tables,
     grouped, h, y_below2, y_above2, z_edge2, y_below, y_above, properties
 ):
     own = g.shape[0] // SUBS
@@ -350,9 +355,8 @@
             y_below[f, pl.ds(start, SUBS), :] = courant * below[f]
             y_above[f, pl.ds(start, SUBS), :] = -courant * above[f]
 
-    pairs = [strips_of(zm, zp, f) for f in range(6)]
-    first = [pair[0] for pair in pairs]
-    second = [pair[1] for pair in pairs]
+    first = [strip_pairs[f] for f in range(6)]
+    second = [strip_pairs[6 + f] for f in range(6)]
     inner = [z_inner[f] for f in range(6)]
     corner = [
         jnp.where(
@@ -510,6 +514,10 @@
     return jax.ShapeDtypeStruct(shape, F32)
 
 
+def kept(*shape):
+    return pltpu.VMEM(shape, F32)
+
+
 def local(conserved, gamma_field, species, lut_color, lut_extinction):
     rows = conserved.shape[1]
     cells = rows * SUBS
@@ -551,7 +559,7 @@
     )(*brick)
     z_up, z_down, z_inner = pl.pallas_call(
         functools.partial(all_strips_kernel, rows),
-        out_shape=(strip, strip, strip),
+        out_shape=(strip, strip, kept(6, SUBS, LANES)),
         compiler_params=params,
         name="strips",
     )(xm, xp, *own_parts)
@@ -561,17 +569,17 @@
     partial, tables = pl.pallas_call(
         half_kernel,
         out_shape=(
-            struct(5, every, LANES),
-            jax.ShapeDtypeStruct((4, 8, SUBS, LANES), jnp.int32),
+            kept(5, every, LANES),
+            pltpu.VMEM((4, 8, SUBS, LANES), jnp.int32),
         ),
         compiler_params=params,
         cost_estimate=cost(4_000_000),
         name="half",
     )(*brick, xm, xp, table_rows)
     message = struct(6, MESSAGE_ROWS, LANES)
-    y_low, y_high, partial = pl.pallas_call(
+    y_low, y_high, partial, strip_pairs = pl.pallas_call(
         y_kernel,
-        out_shape=(message, message, struct(5, every, LANES)),
+        out_shape=(message, message, kept(5, every, LANES), kept(12, SUBS, LANES)),
         compiler_params=params,
         name="layers",
     )(*brick, xm, xp, zm, zp, partial)
@@ -583,13 +591,13 @@
     vmem = pl.BlockSpec(memory_space=pltpu.VMEM)
     grouped, *halves_found = pl.pallas_call(
         step_kernel,
-        in_specs=[pl.BlockSpec(memory_space=pltpu.SMEM)] + [vmem] * 14,
+        in_specs=[pl.BlockSpec(memory_space=pltpu.SMEM)] + [vmem] * 13,
         out_shape=(
-            struct(rows, LANES),
-            struct(5, every, LANES),
-            struct(5, 40, LANES),
-            struct(5, 40, LANES),
-            struct(5, SUBS, LANES),
+            kept(rows, LANES),
+            kept(5, every, LANES),
+            kept(5, 40, LANES),
+            kept(5, 40, LANES),
+            kept(5, SUBS, LANES),
         ),
         scratch_shapes=[
             layer,
@@ -604,8 +612,7 @@
         species.reshape(cells, LANES),
         xm,
         xp,
-        zm,
-        zp,
+        strip_pairs,
         z_inner,
         y_low,
         y_high,

time: 42.4 us -> 42.6 us (level)
  local copies, waits for them, and re-layouts: 2.1 us -> 0.99 us
  waiting for transfers between devices: 8.89 us -> 9.96 us
    unnamed x14, local copies, waits for them, and re-layouts: 2.01 us -> 0.9 us
    all_to_all x1, waiting for transfers between devices: 4.05 us -> 5.13 us  [local(): lax.all_to_all(grouped.reshape(across_y * across_z, 1, LANES), ('gy', 'gz...]
where the time goes in v7:
time: 42.6 us; the launch traced here: 42.5 us
  starting transfers between devices  20.7 us (49%)
  Pallas kernels  10.1 us (24%)
  waiting for transfers between devices  9.96 us (23%)
  local copies, waits for them, and re-layouts  0.99 us (2%)
  between operations  0.76 us (2%)
    ppermute x6, starting transfers between devices, shifted(): lax.ppermute(value, axis, [(i, (i + steps) % size) for i in range(size)])  13.5 us
    all_to_all x1, starting transfers between devices, local(): lax.all_to_all(grouped.reshape(across_y * across_z, 1, LANES), ('gy', 'gz...  7.13 us
    all_to_all x1, waiting for transfers between devices, local(): lax.all_to_all(grouped.reshape(across_y * across_z, 1, LANES), ('gy', 'gz...  5.13 us
    ppermute x6, waiting for transfers between devices, shifted(): lax.ppermute(value, axis, [(i, (i + steps) % size) for i in range(size)])  4.84 us
    pallas_call x1, Pallas kernels, local(): pl.pallas_call(step_kernel, in_specs=[pl.BlockSpec(memory_space=pltpu.SME...  4.16 us
    pallas_call x1, Pallas kernels, local(): pl.pallas_call(state_kernel, out_shape=struct(5, cells, LANES), compiler_...  1.71 us
    pallas_call x1, Pallas kernels, local(): pl.pallas_call(functools.partial(image_kernel, across_y, across_z), out_s...  1.24 us
    pallas_call x1, Pallas kernels, local(): pl.pallas_call(x_kernel, out_shape=(struct(6 * ABOVE + 1, SUBS, LANES), s...  0.98 us
  transfers between devices with their start and end apart: 7, of which 5 were waited for; matrix products, arithmetic and copies ran while one was open for 0% of the time, Pallas kernels for 8%

profile of v7, /device:TPU:1, one launch (start us, length us, event | category | flops | bytes accessed | tf_op | source)
XLA Modules:
  0.0 42.5 jit_solution(5756554101024682227)
XLA Ops:
  0.6 0.0 copy-start
  0.7 1.0 %x_layers.1 = (f32[19,8,128]{2,1,0:T(8,128)S(1)}, f32[12,8,128]{2,1,0:T(8,128)S(1)}) custom-call(f32[5,32,8,128]{3,2,1,0:T(8,128)} %u.1, f32[32,8,128]{2,1,0:T(8,128)} %g.1, s32[32,8,128]{2,1,0:T(8,128)} %sp.1), custom_call_target="tpu_custom_call" | custom-call | tf_op jit(solution)/shard_map/x_layers/pallas_call | solution.py:535
  1.7 2.5 %collective-permute-start = (f32[12,8,128]{2,1,0:T(8,128)S(1)}, f32[12,8,128]{2,1,0:T(8,128)S(1)}, u32[]{:S(2)}, u32[]{:S(2)}) collective-permute-start(f32[12,8,128]{2,1,0:T(8,128)S(1)} %get-tuple-element.29), channel_id=1, source_target_pairs={{0,32},{32,64},{64,96},{96,128},{128,160},{160,192},{192,224},{224... | collective-permute-start | bytes 147464 | tf_op jit(solution)/shard_map/ppermute | solution.py:506
  4.2 4.0 %collective-permute-start.1 = (f32[19,8,128]{2,1,0:T(8,128)S(1)}, f32[19,8,128]{2,1,0:T(8,128)S(1)}, u32[]{:S(2)}, u32[]{:S(2)}) collective-permute-start(f32[19,8,128]{2,1,0:T(8,128)S(1)} %get-tuple-element.30), channel_id=1, source_target_pairs={{0,224},{32,0},{64,32},{96,64},{128,96},{160,128},{192,160},{224,1... | collective-permute-start | bytes 233480 | tf_op jit(solution)/shard_map/ppermute | solution.py:506
  8.3 0.1 slice.4
  8.4 0.7 %own_strips.1 = (f32[6,8,128]{2,1,0:T(8,128)S(1)}, f32[6,8,128]{2,1,0:T(8,128)S(1)}, f32[6,8,128]{2,1,0:T(8,128)S(1)}) custom-call(f32[5,256,128]{2,1,0:T(8,128)S(1)} %bitcast.14, f32[256,128]{1,0:T(8,128)S(1)} %bitcast.18), custom_call_target="tpu_custom_call" | custom-call | flops 2000000 | bytes 2000000 | tf_op jit(solution)/shard_map/own_strips/pallas_call | solution.py:553
  9.0 0.6 %collective-permute-done.xm = f32[12,8,128]{2,1,0:T(8,128)S(1)} collective-permute-done((f32[12,8,128]{2,1,0:T(8,128)S(1)}, f32[12,8,128]{2,1,0:T(8,128)S(1)}, u32[]{:S(2)}, u32[]{:S(2)}) %collective-permute-start) | collective-permute-done | bytes 49184 | tf_op jit(solution)/shard_map/ppermute | solution.py:506
  9.6 0.1 collective-permute-done.1.xp
  9.7 0.1 strips.1
  9.8 1.4 %collective-permute-start.2 = (f32[6,8,128]{2,1,0:T(8,128)S(1)}, f32[6,8,128]{2,1,0:T(8,128)S(1)}, u32[]{:S(2)}, u32[]{:S(2)}) collective-permute-start(f32[6,8,128]{2,1,0:T(8,128)S(1)} %get-tuple-element.34), channel_id=1, source_target_pairs={{0,1},{1,2},{2,3},{3,0},{4,5},{5,6},{6,7},{7,4},{8,9},{9,10},{10,1... | collective-permute-start | bytes 73736 | tf_op jit(solution)/shard_map/ppermute | solution.py:506
  11.2 1.5 %collective-permute-start.3 = (f32[6,8,128]{2,1,0:T(8,128)S(1)}, f32[6,8,128]{2,1,0:T(8,128)S(1)}, u32[]{:S(2)}, u32[]{:S(2)}) collective-permute-start(f32[6,8,128]{2,1,0:T(8,128)S(1)} %get-tuple-element.35), channel_id=1, source_target_pairs={{0,3},{1,0},{2,1},{3,2},{4,7},{5,4},{6,5},{7,6},{8,11},{9,8},{10,9... | collective-permute-start | bytes 73736 | tf_op jit(solution)/shard_map/ppermute | solution.py:506
  12.8 0.8 %half.1 = (f32[5,296,128]{2,1,0:T(8,128)S(1)}, s32[4,8,8,128]{3,2,1,0:T(8,128)S(1)}) custom-call(f32[5,256,128]{2,1,0:T(8,128)S(1)} %bitcast.15, f32[256,128]{1,0:T(8,128)S(1)} %bitcast.19, f32[12,8,128]{2,1,0:T(8,128)S(1)} %collective-permute-done.xm, f32[19,8,128]{2,1,0:T(8,128)S(1)} %collective-permute-done.1.xp, s32[32,128]{1,0:T(8,128)S(1)} %reshape.32.table_rows), custom_call_target="tpu_custom_call" | custom-call | flops 4000000 | bytes 4000000 | tf_op jit(solution)/shard_map/half/pallas_call | solution.py:569
  13.6 0.3 collective-permute-done.2.zm
  13.9 0.0 collective-permute-done.3.zp
  13.9 0.3 layers.1
  14.2 0.9 %copy-done.3 = f32[5,296,128]{2,1,0:T(8,128)} copy-done((f32[5,296,128]{2,1,0:T(8,128)}, f32[5,296,128]{2,1,0:T(8,128)S(1)}, u32[]{:S(2)}) %copy-start.3) | copy-done | bytes 757784
  15.1 3.0 %collective-permute-start.5 = (f32[6,72,128]{2,1,0:T(8,128)S(1)}, f32[6,72,128]{2,1,0:T(8,128)S(1)}, u32[]{:S(2)}, u32[]{:S(2)}) collective-permute-start(f32[6,72,128]{2,1,0:T(8,128)S(1)} %get-tuple-element.39.y_low), channel_id=1, source_target_pairs={{0,28},{4,0},{8,4},{12,8},{16,12},{20,16},{24,20},{28,24},{1,29},{... | collective-permute-start | bytes 663560 | tf_op jit(solution)/shard_map/ppermute | solution.py:506
  18.1 1.1 %collective-permute-start.4 = (f32[6,72,128]{2,1,0:T(8,128)S(1)}, f32[6,72,128]{2,1,0:T(8,128)S(1)}, u32[]{:S(2)}, u32[]{:S(2)}) collective-permute-start(f32[6,72,128]{2,1,0:T(8,128)S(1)} %get-tuple-element.40.y_high), channel_id=1, source_target_pairs={{0,4},{4,8},{8,12},{12,16},{16,20},{20,24},{24,28},{28,0},{1,5},{5... | collective-permute-start | bytes 663560 | tf_op jit(solution)/shard_map/ppermute | solution.py:506
  19.2 3.9 %collective-permute-done.5.yp = f32[6,72,128]{2,1,0:T(8,128)S(1)} collective-permute-done((f32[6,72,128]{2,1,0:T(8,128)S(1)}, f32[6,72,128]{2,1,0:T(8,128)S(1)}, u32[]{:S(2)}, u32[]{:S(2)}) %collective-permute-start.5) | collective-permute-done | bytes 221216 | tf_op jit(solution)/shard_map/ppermute | solution.py:506
  23.1 4.2 %density.1 = (f32[32,128]{1,0:T(8,128)}, f32[5,296,128]{2,1,0:T(8,128)S(1)}, f32[5,40,128]{2,1,0:T(8,128)S(1)}, f32[5,40,128]{2,1,0:T(8,128)S(1)}, f32[5,8,128]{2,1,0:T(8,128)S(1)}) custom-call(f32[1]{0:T(128)} %bitcast.2.keep, f32[5,256,128]{2,1,0:T(8,128)} %bitcast.13, f32[256,128]{1,0:T(8,128)S(1)} %bitcast.21, s32[256,128]{1,0:T(8,128)S(1)} %bitcast.23, ...), custom_call_target="tpu_custom_call" | custom-call | tf_op jit(solution)/shard_map/density/pallas_call | solution.py:592
  27.2 7.1 %all-to-all-start = ((f32[32,1,128]{2,1,0:T(1,128)}), f32[32,1,128]{2,1,0:T(1,128)S(1)}, u32[]{:S(2)}, u32[]{:S(2)}) async-start(f32[32,1,128]{2,1,0:T(1,128)} %bitcast.8), calls=%async_computation | async-start | bytes 32768 | tf_op jit(solution)/shard_map/all_to_all | solution.py:631
  34.4 1.7 %state.1 = f32[5,256,128]{2,1,0:T(8,128)} custom-call(f32[5,256,128]{2,1,0:T(8,128)S(1)} %bitcast.17, f32[256,128]{1,0:T(8,128)S(1)} %bitcast.22, f32[12,8,128]{2,1,0:T(8,128)S(1)} %collective-permute-done.xm, f32[19,8,128]{2,1,0:T(8,128)S(1)} %collective-permute-done.1.xp, f32[5,296,128]{2,1,0:T(8,128)S(1)} %get-tuple-element.43.h, ...), custom_call_target="tpu_custom_call" | custom-call | flops 6000000 | bytes 6000000 | tf_op jit(solution)/shard_map/state/pallas_call | solution.py:624
  36.1 5.1 %all-to-all-done = f32[32,1,128]{2,1,0:T(1,128)S(1)} async-done(((f32[32,1,128]{2,1,0:T(1,128)}), f32[32,1,128]{2,1,0:T(1,128)S(1)}, u32[]{:S(2)}, u32[]{:S(2)}) %all-to-all-start) | async-done | bytes 16416 | tf_op jit(solution)/shard_map/all_to_all | solution.py:631
  41.2 1.2 %image.1 = f32[4,4,1920]{2,1,0:T(4,128)} custom-call(f32[32,128]{1,0:T(8,128)S(1)} %bitcast.24), custom_call_target="tpu_custom_call" | custom-call | tf_op jit(solution)/shard_map/image/pallas_call | solution.py:634
  (18 shorter events, 0.1 us)
Async XLA Ops:
  0.6 7.7 %copy-start = (f32[5,32,8,128]{3,2,1,0:T(8,128)S(1)}, f32[5,32,8,128]{3,2,1,0:T(8,128)}, u32[]{:S(2)}) copy-start(f32[5,32,8,128]{3,2,1,0:T(8,128)} %u.1) | copy-start | bytes 1966084
  0.6 7.6 %copy-start.6 = (f32[4,256]{1,0:T(4,128)S(1)}, f32[4,256]{1,0:T(4,128)}, u32[]{:S(2)}) copy-start(f32[4,256]{1,0:T(4,128)} %param.9) | copy-start | bytes 12292
  0.7 7.6 %copy-start.5 = (f32[4,3,256]{2,0,1:T(4,128)S(1)}, f32[4,3,256]{2,0,1:T(4,128)}, u32[]{:S(2)}) copy-start(f32[4,3,256]{2,0,1:T(4,128)} %param.8) | copy-start | bytes 36868
  0.7 7.7 %copy-start.2 = (f32[32,8,128]{2,1,0:T(8,128)S(1)}, f32[32,8,128]{2,1,0:T(8,128)}, u32[]{:S(2)}) copy-start(f32[32,8,128]{2,1,0:T(8,128)} %g.1) | copy-start | bytes 393220
  1.7 8.0 %collective-permute-start = (f32[12,8,128]{2,1,0:T(8,128)S(1)}, f32[12,8,128]{2,1,0:T(8,128)S(1)}, u32[]{:S(2)}, u32[]{:S(2)}) collective-permute-start(f32[12,8,128]{2,1,0:T(8,128)S(1)} %get-tuple-element.29), channel_id=1, source_target_pairs={{0,32},{32,64},{64,96},{96,128},{128,160},{160,192},{192,224},{224... | collective-permute-start | bytes 147464 | tf_op jit(solution)/shard_map/ppermute | solution.py:506
  4.2 5.5 %collective-permute-start.1 = (f32[19,8,128]{2,1,0:T(8,128)S(1)}, f32[19,8,128]{2,1,0:T(8,128)S(1)}, u32[]{:S(2)}, u32[]{:S(2)}) collective-permute-start(f32[19,8,128]{2,1,0:T(8,128)S(1)} %get-tuple-element.30), channel_id=1, source_target_pairs={{0,224},{32,0},{64,32},{96,64},{128,96},{160,128},{192,160},{224,1... | collective-permute-start | bytes 233480 | tf_op jit(solution)/shard_map/ppermute | solution.py:506
  9.8 4.0 %collective-permute-start.2 = (f32[6,8,128]{2,1,0:T(8,128)S(1)}, f32[6,8,128]{2,1,0:T(8,128)S(1)}, u32[]{:S(2)}, u32[]{:S(2)}) collective-permute-start(f32[6,8,128]{2,1,0:T(8,128)S(1)} %get-tuple-element.34), channel_id=1, source_target_pairs={{0,1},{1,2},{2,3},{3,0},{4,5},{5,6},{6,7},{7,4},{8,9},{9,10},{10,1... | collective-permute-start | bytes 73736 | tf_op jit(solution)/shard_map/ppermute | solution.py:506
  11.2 2.7 %collective-permute-start.3 = (f32[6,8,128]{2,1,0:T(8,128)S(1)}, f32[6,8,128]{2,1,0:T(8,128)S(1)}, u32[]{:S(2)}, u32[]{:S(2)}) collective-permute-start(f32[6,8,128]{2,1,0:T(8,128)S(1)} %get-tuple-element.35), channel_id=1, source_target_pairs={{0,3},{1,0},{2,1},{3,2},{4,7},{5,4},{6,5},{7,6},{8,11},{9,8},{10,9... | collective-permute-start | bytes 73736 | tf_op jit(solution)/shard_map/ppermute | solution.py:506
  13.9 9.2 %copy-start.4 = (s32[32,8,128]{2,1,0:T(8,128)S(1)}, s32[32,8,128]{2,1,0:T(8,128)}, u32[]{:S(2)}) copy-start(s32[32,8,128]{2,1,0:T(8,128)} %sp.1) | copy-start | bytes 393220
  14.2 0.9 %copy-start.3 = (f32[5,296,128]{2,1,0:T(8,128)}, f32[5,296,128]{2,1,0:T(8,128)S(1)}, u32[]{:S(2)}) copy-start(f32[5,296,128]{2,1,0:T(8,128)S(1)} %get-tuple-element.41.partial) | copy-start | bytes 2273284
  15.1 8.0 %collective-permute-start.5 = (f32[6,72,128]{2,1,0:T(8,128)S(1)}, f32[6,72,128]{2,1,0:T(8,128)S(1)}, u32[]{:S(2)}, u32[]{:S(2)}) collective-permute-start(f32[6,72,128]{2,1,0:T(8,128)S(1)} %get-tuple-element.39.y_low), channel_id=1, source_target_pairs={{0,28},{4,0},{8,4},{12,8},{16,12},{20,16},{24,20},{28,24},{1,29},{... | collective-permute-start | bytes 663560 | tf_op jit(solution)/shard_map/ppermute | solution.py:506
  18.1 5.0 %collective-permute-start.4 = (f32[6,72,128]{2,1,0:T(8,128)S(1)}, f32[6,72,128]{2,1,0:T(8,128)S(1)}, u32[]{:S(2)}, u32[]{:S(2)}) collective-permute-start(f32[6,72,128]{2,1,0:T(8,128)S(1)} %get-tuple-element.40.y_high), channel_id=1, source_target_pairs={{0,4},{4,8},{8,12},{12,16},{16,20},{20,24},{24,28},{28,0},{1,5},{5... | collective-permute-start | bytes 663560 | tf_op jit(solution)/shard_map/ppermute | solution.py:506
  23.1 11.3 %copy-start.1 = (f32[5,32,8,128]{3,2,1,0:T(8,128)S(1)}, f32[5,32,8,128]{3,2,1,0:T(8,128)}, u32[]{:S(2)}) copy-start(f32[5,32,8,128]{3,2,1,0:T(8,128)} %u.1) | copy-start | bytes 1966084
  27.2 14.0 %all-to-all-start = ((f32[32,1,128]{2,1,0:T(1,128)}), f32[32,1,128]{2,1,0:T(1,128)S(1)}, u32[]{:S(2)}, u32[]{:S(2)}) async-start(f32[32,1,128]{2,1,0:T(1,128)} %bitcast.8), calls=%async_computation | async-start | bytes 32768 | tf_op jit(solution)/shard_map/all_to_all | solution.py:631
